TPU v7x, 32 devices: a whole 2x2x4 slice. The times are simulated.
32 devices in a mesh: ctx: 16 (over z, y, core), fsdp: 2 (over x).
Axes of the slice: x: 2, y: 2, z: 4, core: 2. Of those that a mesh axis runs over, the one named last changes fastest.
Arguments:
- tokens: bfloat16 [4096, 2560], P('ctx', 'fsdp'), may hold values from -6 to 6
- x_weight: bfloat16 [2560, 2560], P('fsdp'), may hold values from -0.125 to 0.125
- bc_weight: bfloat16 [2560, 256], P('fsdp'), may hold values from -0.125 to 0.125
- dt_weight: bfloat16 [2560, 40], P('fsdp'), may hold values from -0.125 to 0.125
- conv_inner: float32 [4, 2560], P(None, 'fsdp'), may hold values from -4 to 4
- conv_shared: float32 [4, 256], replicated, may hold values from -4 to 4
- dt_bias: float32 [40], P('fsdp'), may hold values from -3 to 3
- decay_rate: float32 [40], P('fsdp'), as said below
- norm_gain: float32 [2560], P('fsdp'), may hold values from 0.5 to 1.5
- doc_starts: int32 [4], replicated, may hold values from 0 to 3968, as said below
- grad_out: bfloat16 [4096, 2560], P('ctx', 'fsdp'), may hold values from -6 to 6
Outputs:
- mixed_out: bfloat16 [4096, 2560], P('ctx', 'fsdp')
- grad_tokens: bfloat16 [4096, 2560], P('ctx', 'fsdp')
Inputs may be any that keep to these rules, and one draw needn't show every extreme that they name: `decay_rate`: positive rates, one a head. `doc_starts`: strictly increasing token offsets; the first is 0 and the last is 3968.
All inputs are finite; a program needn't handle non-finite values.
Results may differ from a plain program's by a relative error of at most 0.015.
Values may be sent and summed in bfloat16 or wider, within the bound.
No kernel may reach another device: no remote copies, remote signals or barrier semaphores. Data moves between devices by JAX's collectives and lax.ppermute only.
A program may use at most 128 MiB of HBM per device.

v0:
```python
import functools

import jax
import jax.numpy as jnp
from jax import lax
from jax.experimental import pallas as pl
from jax.experimental.pallas import tpu as pltpu
from jax.sharding import PartitionSpec as P

HEAD_DIM = 64
STATE = 128


exact = lax.Precision.HIGHEST
epsilon = 1e-05


def from_behind(value, axis, steps):
    count = lax.axis_size(axis)
    leading, last = (max(0, -steps), min(count, count - steps))
    return lax.ppermute(value, axis, [(source, source + steps) for source in range(leading, last)])


def prefix(part, axis, combine, identity, reverse):
    count = lax.axis_size(axis)
    place = lax.axis_index(axis)
    ahead = count - 1 - place if reverse else place
    gathered = jax.tree.map(lambda a: lax.all_gather(a, axis), part)
    state = jax.tree.map(lambda a, e: jnp.zeros_like(a) + jnp.asarray(e, a.dtype), part, identity)

    def one(step, state):
        source = count - 1 - step if reverse else step
        return combine(
            state, jax.tree.map(lambda a: lax.dynamic_index_in_dim(a, source, 0, False), gathered)
        )

    return lax.fori_loop(0, ahead, one, state)


def doc_index(positions, doc_starts):
    hits = (doc_starts[None, :] <= positions[:, None]).astype(jnp.int32)
    return jnp.sum(hits, axis=1) - 1


def causal_conv(padded, docs_ext, taps):
    count = padded.shape[0] - 3
    docs_now = docs_ext[3:]
    total = jnp.zeros((count, padded.shape[1]), jnp.float32)
    for offset in range(4):
        rows = padded[3 - offset : 3 - offset + count]
        same = (docs_ext[3 - offset : 3 - offset + count] == docs_now).astype(jnp.float32)
        total = total + taps[offset][None, :] * rows * same[:, None]
    return total


def block_out(x_act, b_act, c_act, delta, docs, doc_before, state_in, decay_rate):
    count = delta.shape[0]
    places = jnp.arange(count, dtype=jnp.int32)
    lower = places[:, None] >= places[None, :]
    ramp = -jnp.dot(lower.astype(jnp.float32), delta, precision=exact) * decay_rate[None, :]
    same = jnp.logical_and(docs[:, None] == docs[None, :], lower)
    gap = ramp[:, None, :] - ramp[None, :, :]
    decay = jnp.exp(jnp.where(same[:, :, None], gap, 0.0)) * same.astype(jnp.float32)[:, :, None]
    scores = jnp.dot(c_act, b_act.T, precision=exact)
    mixing = decay * scores[:, :, None] * delta[None, :, :]
    inner = jnp.einsum("tsh,shp->thp", mixing, x_act, precision=exact)
    carried = (docs == doc_before).astype(jnp.float32)
    enter = jnp.exp(ramp) * carried[:, None]
    from_state = jnp.einsum("tn,hpn->thp", c_act, state_in, precision=exact) * enter[:, :, None]
    last_doc = docs[count - 1]
    tail = (
        jnp.exp(ramp[count - 1][None, :] - ramp)
        * (docs == last_doc).astype(jnp.float32)[:, None]
        * delta
    )
    weighted = tail[:, :, None] * x_act
    state_loc = jnp.einsum("shp,sn->hpn", weighted, b_act, precision=exact)
    keep = jnp.exp(ramp[count - 1]) * (last_doc == doc_before).astype(jnp.float32)
    return (inner + from_state, state_loc, keep)


def head_norm(values, norm_gain):
    scale = lax.rsqrt(jnp.mean(values * values, axis=-1, keepdims=True) + epsilon)
    normed = values * scale
    return normed.reshape(values.shape[0], values.shape[1] * values.shape[2]) * norm_gain[None, :]


def link(earlier, later):
    return (earlier[0] * later[0], later[0][:, None, None] * earlier[1] + later[1])


def on_device(
    tokens,
    x_weight,
    bc_weight,
    dt_weight,
    conv_inner,
    conv_shared,
    dt_bias,
    decay_rate,
    norm_gain,
    doc_starts,
    grad_out,
):
    count = tokens.shape[0]
    heads_here = decay_rate.shape[0]
    features = lax.all_gather(tokens, "fsdp", axis=1, tiled=True)
    x_cols, dt_cols = (
        lax.all_to_all(x_weight, "fsdp", split_axis=1, concat_axis=0, tiled=True),
        lax.all_to_all(dt_weight, "fsdp", split_axis=1, concat_axis=0, tiled=True),
    )
    bc_all = lax.all_gather(bc_weight, "fsdp", axis=0, tiled=True)
    x_proj = jnp.dot(features, x_cols, preferred_element_type=jnp.float32).astype(jnp.bfloat16)
    bc_proj = jnp.dot(features, bc_all, preferred_element_type=jnp.float32)
    dt_raw = jnp.dot(features, dt_cols, preferred_element_type=jnp.float32)
    x_wide = lax.optimization_barrier(x_proj).astype(jnp.float32)
    rim_x, rim_bc = from_behind((x_wide[count - 3 :], bc_proj[count - 3 :]), "ctx", 1)
    x_ext = jnp.concatenate([rim_x, x_wide], axis=0)
    bc_ext = jnp.concatenate([rim_bc, bc_proj], axis=0)
    first = lax.axis_index("ctx") * count
    positions = first - 3 + jnp.arange(count + 3, dtype=jnp.int32)
    docs_ext = doc_index(positions, doc_starts)
    docs = docs_ext[3:]
    doc_before = docs_ext[2]

    def layer(x_in, bc_in, dt_in, state_in):
        x_act = jax.nn.silu(causal_conv(x_in, docs_ext, conv_inner))
        bc_act = jax.nn.silu(causal_conv(bc_in, docs_ext, conv_shared))
        delta = jax.nn.softplus(dt_in + dt_bias[None, :])
        values, state_loc, keep = block_out(
            x_act.reshape(count, heads_here, HEAD_DIM),
            bc_act[:, :STATE],
            bc_act[:, STATE:],
            delta,
            docs,
            doc_before,
            state_in,
            decay_rate,
        )
        return (head_norm(values, norm_gain), state_loc, keep)

    blank = jnp.zeros((heads_here, HEAD_DIM, STATE), jnp.float32)
    unit = jnp.ones((heads_here,), jnp.float32)
    _, state_loc, keep = layer(x_ext, bc_ext, dt_raw, blank)
    state_in = prefix((keep, state_loc), "ctx", link, (unit, blank), False)[1]
    outputs, pull = jax.vjp(layer, x_ext, bc_ext, dt_raw, state_in)
    normed = outputs[0]
    grads_out = pull((grad_out.astype(jnp.float32), jnp.zeros_like(blank), jnp.zeros_like(unit)))
    adjoint = prefix((keep, grads_out[3]), "ctx", link, (unit, blank), True)[1]
    keep_grad = jnp.sum(adjoint * state_in, axis=(1, 2))
    grads_state = pull((jnp.zeros_like(normed), adjoint, keep_grad))
    grad_xe = grads_out[0] + grads_state[0]
    grad_bce = grads_out[1] + grads_state[1]
    grad_dt = grads_out[2] + grads_state[2]
    back_x, back_bc = from_behind((grad_xe[:3], grad_bce[:3]), "ctx", -1)
    grad_x = grad_xe[3:].at[count - 3 :].add(back_x)
    grad_bc = grad_bce[3:].at[count - 3 :].add(back_bc)
    grad_xb = grad_x.astype(jnp.bfloat16)
    grad_rows = lax.all_gather(grad_xb, "fsdp", axis=1, tiled=True)
    column = lax.axis_index("fsdp") * heads_here
    dt_wide = lax.dynamic_update_slice(
        jnp.zeros((count, dt_weight.shape[1]), jnp.float32), grad_dt, (jnp.int32(0), column)
    )
    bc_total, dt_total = lax.psum((grad_bc, dt_wide), "fsdp")
    grad_local = jnp.dot(grad_rows, x_weight.T, preferred_element_type=jnp.float32)
    grad_local = grad_local + jnp.dot(bc_total, bc_weight.T.astype(jnp.float32), precision=exact)
    grad_local = grad_local + jnp.dot(dt_total, dt_weight.T.astype(jnp.float32), precision=exact)
    grad_tokens = grad_local.astype(jnp.bfloat16)
    return (normed.astype(jnp.bfloat16), grad_tokens)


BF = jnp.bfloat16
F32 = jnp.float32
LOG2E = 1.4426950408889634
LANES = 128
NEG = -1e30


def params(mb=60, **kw):
    return pltpu.CompilerParams(vmem_limit_bytes=mb * 1024 * 1024, **kw)


def cost(flops, nbytes):
    return pl.CostEstimate(flops=int(flops), bytes_accessed=int(nbytes), transcendentals=0)


def mm(a, b):
    return jnp.dot(a, b, preferred_element_type=F32)


def mm_nt(a, b):
    return lax.dot_general(a, b, (((1,), (1,)), ((), ())), preferred_element_type=F32)


def mm_tn(a, b):
    return lax.dot_general(a, b, (((0,), (0,)), ((), ())), preferred_element_type=F32)


def split2(v):
    hi = v.astype(BF)
    return hi, (v - hi.astype(F32)).astype(BF)


def iota(shape, dim):
    return lax.broadcasted_iota(jnp.int32, shape, dim)


def doc_start_of(pos, docs_ref, count):
    start = jnp.zeros_like(pos)
    for i in range(count):
        start = jnp.where(docs_ref[i] <= pos, docs_ref[i], start)
    return start


def spread(heads, width):
    shape = (LANES, width)
    row, col = iota(shape, 0), iota(shape, 1)
    head = jnp.right_shift(col, 6)
    return jnp.where((row == head) | (row == head + 16), 1.0, 0.0).astype(BF)


def gather_heads(width):
    shape = (width, LANES)
    return jnp.where(jnp.right_shift(iota(shape, 0), 6) == iota(shape, 1), 1.0, 0.0).astype(BF)


def packed(v):
    hi = v.astype(BF).astype(F32)
    lo = v - hi
    lane = iota(v.shape, 1)
    return jnp.where(lane < 16, hi, pltpu.roll(lo, 16, 1)).astype(BF)


def over_heads(v, gather):
    hi, lo = split2(v)
    return mm(hi, gather) + mm(lo, gather)


def silu_parts(v):
    sig = 1.0 / (1.0 + jnp.exp(-v))
    return v * sig, sig * (1.0 + v * (1.0 - sig))


def small_proj_kernel(tok_ref, bcw_ref, dtw_ref, out_ref, low_ref):
    states = bcw_ref.shape[1]
    heads = dtw_ref.shape[1]
    tok = tok_ref[...]
    out_ref[:, :states], low_ref[...] = split2(mm(tok, bcw_ref[...]))
    hi, lo = split2(mm(tok, dtw_ref[...]))
    shape = (heads, LANES)
    row, col = iota(shape, 0), iota(shape, 1)
    first = jnp.where(row == col, 1.0, 0.0).astype(BF)
    second = jnp.where(row + heads == col, 1.0, 0.0).astype(BF)
    out_ref[:, states:] = (mm(hi, first) + mm(lo, second)).astype(BF)


def small_proj(tokens, bc_weight, dt_weight):
    rows = tokens.shape[0]
    return pl.pallas_call(
        small_proj_kernel,
        out_shape=[
            jax.ShapeDtypeStruct((rows, bc_weight.shape[1] + LANES), BF),
            jax.ShapeDtypeStruct((rows, bc_weight.shape[1]), BF),
        ],
        compiler_params=params(),
        cost_estimate=cost(3e8, 2e6),
        name="small_proj",
    )(tokens, bc_weight, dt_weight)


def piece_kernel(meta_ref, tok_ref, w_ref, out_ref):
    out_ref[...] = mm(tok_ref[...], w_ref[...]).astype(BF)


def proj_piece(tokens, x_weight, block, width):
    rows, depth = tokens.shape
    tiles = width // LANES
    return pl.pallas_call(
        piece_kernel,
        grid_spec=pltpu.PrefetchScalarGridSpec(
            num_scalar_prefetch=1,
            grid=(tiles,),
            in_specs=[
                pl.BlockSpec((rows, depth), lambda i, m: (0, 0)),
                pl.BlockSpec((depth, LANES), lambda i, m: (0, m[0] * tiles + i)),
            ],
            out_specs=pl.BlockSpec((rows, LANES), lambda i, m: (0, i)),
        ),
        out_shape=jax.ShapeDtypeStruct((rows, width), BF),
        compiler_params=params(),
        cost_estimate=cost(2 * rows * depth * width, 2 * depth * width),
        name="proj_piece",
    )(block, tokens, x_weight)


def rim_kernel(meta_ref, ra_ref, rb_ref, own_w_ref, peer_w_ref, bcw_ref, own_ref, send_ref):
    width = own_w_ref.shape[1]
    rows = ra_ref[...] + rb_ref[...]
    shared = mm(rows, bcw_ref[...]).astype(BF)
    own_ref[:, :width] = mm(rows, own_w_ref[...]).astype(BF)
    own_ref[:, width:] = shared
    send_ref[:, :width] = mm(rows, peer_w_ref[...]).astype(BF)
    send_ref[:, width:] = shared


def rim_proj(ra, rb, x_weight, bc_weight, blocks, width):
    rows, depth = ra.shape
    states = bc_weight.shape[1]
    out = jax.ShapeDtypeStruct((rows, width + states), BF)
    full = lambda shape: pl.BlockSpec(shape, lambda i, m: (0, 0))
    return pl.pallas_call(
        rim_kernel,
        grid_spec=pltpu.PrefetchScalarGridSpec(
            num_scalar_prefetch=1,
            grid=(1,),
            in_specs=[
                full((rows, depth)),
                full((rows, depth)),
                pl.BlockSpec((depth, width), lambda i, m: (0, m[0])),
                pl.BlockSpec((depth, width), lambda i, m: (0, m[1])),
                full((depth, states)),
            ],
            out_specs=[full((rows, width + states)), full((rows, width + states))],
        ),
        out_shape=[out, out],
        compiler_params=params(),
        cost_estimate=cost(4 * rows * depth * width, 4 * depth * width),
        name="rim_proj",
    )(blocks, ra, rb, x_weight, x_weight, bc_weight)


def conv_masks(docs_ref, count, base, rows, lanes):
    pos = base + iota((rows, lanes), 0)
    start = doc_start_of(pos, docs_ref, count)
    return [jnp.where(pos - k >= start, 1.0, 0.0) for k in range(1, 4)]


def shared_kernel(
    docs, heads, all_heads, meta_ref, docs_ref, own_ref, xr_ref, cr_ref, dr_ref, rim_own_ref,
    rim_recv_ref, taps_ref, prm_ref, bact_ref, bpre_ref, delta_ref, ramp_ref, sig_ref, rampt_ref,
    dpk_ref, wpk_ref, epk_ref, keep_ref, ext_ref,
):
    k, x, chip = meta_ref[0], meta_ref[1], meta_ref[2]
    rows = own_ref.shape[0]
    total = 2 * rows
    states2 = bact_ref.shape[1]
    base = chip * total
    mine = pl.multiple_of(8 + k * rows, 8)
    other = pl.multiple_of(8 + (1 - k) * rows, 8)
    width = rim_own_ref.shape[1] - states2
    rim = rim_own_ref[:, width:].astype(F32) + rim_recv_ref[:, width:].astype(F32)
    ext_ref[0:8, :] = rim[8:16, :]
    ext_ref[pl.ds(mine, rows), :] = own_ref[:, :states2].astype(F32) + xr_ref[:, :states2].astype(F32)
    ext_ref[pl.ds(other, rows), :] = cr_ref[:, :states2].astype(F32) + dr_ref[:, :states2].astype(F32)

    tile = 64

    def conv(step, _):
        at = pl.multiple_of(step * tile, tile)
        masks = conv_masks(docs_ref, docs, base + at, tile, LANES)
        for lane in range(0, states2, LANES):
            sl = slice(lane, lane + LANES)
            window = ext_ref[pl.ds(at, tile + 8), sl]
            value = window[8:] * taps_ref[0:1, sl]
            for j in range(1, 4):
                value = value + window[8 - j : 8 - j + tile] * taps_ref[j : j + 1, sl] * masks[j - 1]
            bpre_ref[pl.ds(at, tile), sl] = value
            bact_ref[pl.ds(at, tile), sl] = (value / (1.0 + jnp.exp(-value))).astype(BF)
        return 0

    lax.fori_loop(0, total // tile, conv, 0)

    shape = (LANES, LANES)
    row, col = iota(shape, 0), iota(shape, 1)
    first = x * (all_heads // 2) + k * heads
    wanted = (col < heads) & ((row == first + col) | (row == all_heads + first + col))
    select = jnp.where(wanted, 1.0, 0.0).astype(BF)
    square = (rows, rows)
    lower = jnp.where(iota(square, 0) >= iota(square, 1), 1.0, 0.0).astype(BF)
    bias, rate = prm_ref[0:1, :], prm_ref[1:2, :]

    def steps(part, ref_a, ref_b):
        at = pl.multiple_of(part * rows, rows)
        raw = mm(ref_a[:, states2:], select) + mm(ref_b[:, states2:], select) + bias
        delta = jnp.maximum(raw, 0.0) + jnp.log1p(jnp.exp(-jnp.abs(raw)))
        delta_ref[pl.ds(at, rows), :] = delta
        sig_ref[pl.ds(at, rows), :] = 1.0 / (1.0 + jnp.exp(-raw))
        dpk_ref[pl.ds(at, rows), :] = packed(delta)
        hi, rest = split2(delta)
        mid = rest
        low = (delta - hi.astype(F32) - mid.astype(F32)).astype(BF)
        ramp = -(mm(lower, hi) + mm(lower, mid) + mm(lower, low)) * (rate * LOG2E)
        ramp_ref[pl.ds(at, rows), :] = ramp
        rampt_ref[part] = jnp.transpose(ramp)[:16, :]
        begin = base + at
        end = begin + rows - 1
        pos = begin + iota((rows, LANES), 0)
        start = doc_start_of(pos, docs_ref, docs)
        last = doc_start_of(jnp.zeros((1, LANES), jnp.int32) + end, docs_ref, docs)
        final = ramp[rows - 1 : rows, :]
        epk_ref[pl.ds(at, rows), :] = packed(jnp.where(start < begin, jnp.exp2(ramp), 0.0))
        wpk_ref[pl.ds(at, rows), :] = packed(jnp.where(pos >= last, jnp.exp2(final - ramp), 0.0))
        keep_ref[part] = jnp.zeros((8, LANES), F32) + jnp.where(last < begin, jnp.exp2(final), 0.0)

    steps(k, own_ref, xr_ref)
    steps(1 - k, cr_ref, dr_ref)


def shared_maps(meta, doc_starts, own, xr, cr, dr, rim_own, rim_recv, taps, prm, heads, all_heads):
    rows = own.shape[0]
    total, states2 = 2 * rows, own.shape[1] - LANES
    compact = jax.ShapeDtypeStruct((total, LANES), F32)
    compact_b = jax.ShapeDtypeStruct((total, LANES), BF)
    vm = pl.BlockSpec(memory_space=pltpu.VMEM)
    return pl.pallas_call(
        functools.partial(shared_kernel, doc_starts.shape[0], heads, all_heads),
        grid_spec=pltpu.PrefetchScalarGridSpec(
            num_scalar_prefetch=2,
            grid=(),
            in_specs=[vm] * 8,
            out_specs=[vm] * 10,
            scratch_shapes=[pltpu.VMEM((total + 8, states2), F32)],
        ),
        out_shape=[
            jax.ShapeDtypeStruct((total, states2), BF),
            jax.ShapeDtypeStruct((total, states2), F32),
            compact,
            compact,
            compact,
            jax.ShapeDtypeStruct((2, 16, rows), F32),
            compact_b,
            compact_b,
            compact_b,
            jax.ShapeDtypeStruct((2, 8, LANES), F32),
        ],
        compiler_params=params(),
        cost_estimate=cost(4e9, 4e6),
        name="shared_maps",
    )(meta, doc_starts, own, xr, cr, dr, rim_own, rim_recv, taps, prm)


def keep_row(keep, heads, width):
    hi, rest = split2(keep)
    low = (keep - hi.astype(F32) - rest.astype(F32)).astype(BF)
    wide = spread(heads, width)
    lane = iota(keep.shape, 1)
    clean = lambda v: jnp.where(lane < 16, v.astype(F32), 0.0).astype(BF)
    return mm(clean(hi), wide) + mm(clean(rest), wide) + mm(clean(low), wide)


def inner_kernel(
    docs, heads, meta_ref, docs_ref, own_ref, xr_ref, cr_ref, dr_ref, rim_own_ref, rim_recv_ref,
    taps_ref, bact_ref, dpk_ref, wpk_ref, keep_ref, pre_ref, xd_ref, loc_ref, send_ref, ext_ref,
    wx_ref,
):
    k, chip = meta_ref[0], meta_ref[2]
    rows, width = own_ref.shape
    total = 2 * rows
    states = bact_ref.shape[1] // 2
    base = chip * total
    mine = pl.multiple_of(8 + k * rows, 8)
    other = pl.multiple_of(8 + (1 - k) * rows, 8)
    rim = (rim_own_ref[:, :width].astype(F32) + rim_recv_ref[:, :width].astype(F32))
    ext_ref[0:8, :] = rim.astype(BF).astype(F32)[8:16, :]

    def total_of(a, b):
        return (a[...].astype(F32) + b[...].astype(F32)).astype(BF).astype(F32)

    ext_ref[pl.ds(mine, rows), :] = total_of(own_ref, xr_ref)
    ext_ref[pl.ds(other, rows), :] = total_of(cr_ref, dr_ref)
    wide = spread(heads, width)
    tile = 64

    def conv(step, _):
        at = pl.multiple_of(step * tile, tile)
        masks = conv_masks(docs_ref, docs, base + at, tile, LANES)
        dpk = dpk_ref[pl.ds(at, tile), :]
        wpk = wpk_ref[pl.ds(at, tile), :]
        for lane in range(0, width, LANES):
            sl = slice(lane, lane + LANES)
            window = ext_ref[pl.ds(at, tile + 8), sl]
            value = window[8:] * taps_ref[0:1, sl]
            for j in range(1, 4):
                value = value + window[8 - j : 8 - j + tile] * taps_ref[j : j + 1, sl] * masks[j - 1]
            pre_ref[pl.ds(at, tile), sl] = value
            act = value / (1.0 + jnp.exp(-value))
            xd = act * mm(dpk, wide[:, sl])
            xd_ref[pl.ds(at, tile), sl] = xd.astype(BF)
            wx_ref[pl.ds(at, tile), sl] = (xd * mm(wpk, wide[:, sl])).astype(BF)
        return 0

    lax.fori_loop(0, total // tile, conv, 0)
    locs = []
    for part in range(2):
        sl = slice(part * rows, (part + 1) * rows)
        loc = mm_tn(bact_ref[sl, :states], wx_ref[sl, :])
        loc_ref[part] = loc
        locs.append(loc)
    second = keep_row(keep_ref[1], heads, width)[0:1, :]
    state = locs[0] * second + locs[1]
    chips, piece = send_ref.shape[0], send_ref.shape[1]
    for i in range(chips):
        send_ref[i, :, :width] = state[i * piece : (i + 1) * piece, :].astype(BF)
    keep = jnp.where(iota((8, LANES), 1) < 16, keep_ref[0] * keep_ref[1], 0.0)
    hi, mid = split2(keep)
    low = (keep - hi.astype(F32) - mid.astype(F32)).astype(BF)
    row = iota((8, LANES), 0)
    stack = jnp.where(row == 0, hi.astype(F32), jnp.where(row == 1, mid.astype(F32), low.astype(F32)))
    stack = jnp.concatenate([stack, jnp.zeros((piece - 8, LANES), F32)], axis=0).astype(BF)
    for i in range(chips):
        send_ref[i, :, width:] = stack


def inner_maps(
    meta, doc_starts, own, xr, cr, dr, rim_own, rim_recv, taps, bact, dpk, wpk, keep, heads, chips
):
    rows, width = own.shape
    total, states = 2 * rows, bact.shape[1] // 2
    vm = pl.BlockSpec(memory_space=pltpu.VMEM)
    whole = lambda shape: pl.BlockSpec(shape, lambda i, m, d: (0,) * len(shape))
    half = pl.BlockSpec((taps.shape[0], width), lambda i, m, d: (0, m[0]))
    outs = [
        jax.ShapeDtypeStruct((total, width), F32),
        jax.ShapeDtypeStruct((total, width), BF),
        jax.ShapeDtypeStruct((2, states, width), F32),
        jax.ShapeDtypeStruct((chips, states // chips, width + LANES), BF),
    ]
    return pl.pallas_call(
        functools.partial(inner_kernel, doc_starts.shape[0], heads),
        grid_spec=pltpu.PrefetchScalarGridSpec(
            num_scalar_prefetch=2,
            grid=(1,),
            in_specs=[
                whole(own.shape), whole(xr.shape), whole(cr.shape), whole(dr.shape),
                whole(rim_own.shape), whole(rim_recv.shape), half, whole(bact.shape),
                whole(dpk.shape), whole(wpk.shape), whole(keep.shape),
            ],
            out_specs=[whole(o.shape) for o in outs],
            scratch_shapes=[pltpu.VMEM((total + 8, width), F32), pltpu.VMEM((total, width), BF)],
        ),
        out_shape=outs,
        compiler_params=params(),
        cost_estimate=cost(4e9, 4e6),
        name="inner_maps",
    )(meta, doc_starts, own, xr, cr, dr, rim_own, rim_recv, taps, bact, dpk, wpk, keep)


def within_kernel(
    docs, heads, meta_ref, docs_ref, xd_ref, ramp_ref, rampt_ref, own_ref, xr_ref, cr_ref, dr_ref,
    own_low_ref, xr_low_ref, cr_low_ref, dr_low_ref, rim_own_ref, rim_recv_ref, taps_ref, y_ref,
    cbt_ref, cb_ref, gate_ref, ext_ref, high_ref, low_ref,
):
    k, chip = meta_ref[0], meta_ref[2]
    total, width = xd_ref.shape
    rows = total // 2
    states2 = own_low_ref.shape[1]
    states = states2 // 2
    mine = pl.multiple_of(8 + k * rows, 8)
    other = pl.multiple_of(8 + (1 - k) * rows, 8)
    rim = rim_own_ref[:, width:].astype(F32) + rim_recv_ref[:, width:].astype(F32)
    ext_ref[0:8, :] = rim[8:16, :]

    def exact_sum(a, a_low, b, b_low):
        high = a[:, :states2].astype(F32) + b[:, :states2].astype(F32)
        return high + (a_low[...].astype(F32) + b_low[...].astype(F32))

    ext_ref[pl.ds(mine, rows), :] = exact_sum(own_ref, own_low_ref, xr_ref, xr_low_ref)
    ext_ref[pl.ds(other, rows), :] = exact_sum(cr_ref, cr_low_ref, dr_ref, dr_low_ref)
    tile = 64

    def conv(step, _):
        at = pl.multiple_of(step * tile, tile)
        masks = conv_masks(docs_ref, docs, chip * total + at, tile, LANES)
        for lane in range(0, states2, LANES):
            sl = slice(lane, lane + LANES)
            window = ext_ref[pl.ds(at, tile + 8), sl]
            value = window[8:] * taps_ref[0:1, sl]
            for j in range(1, 4):
                value = value + window[8 - j : 8 - j + tile] * taps_ref[j : j + 1, sl] * masks[j - 1]
            high, low = split2(value / (1.0 + jnp.exp(-value)))
            high_ref[pl.ds(at, tile), sl] = high
            low_ref[pl.ds(at, tile), sl] = low
        return 0

    lax.fori_loop(0, total // tile, conv, 0)
    square = (rows, rows)
    lane = iota((rows, LANES), 1)
    for part in range(2):
        sl = slice(part * rows, (part + 1) * rows)
        begin = chip * total + part * rows
        b, c = high_ref[sl, :states], high_ref[sl, states:]
        b_low, c_low = low_ref[sl, :states], low_ref[sl, states:]
        cb_ref[...] = mm_nt(c, b) + (mm_nt(c, b_low) + mm_nt(c_low, b))
        cbt_ref[part] = jnp.transpose(cb_ref[...])
        pos, src = begin + iota(square, 0), begin + iota(square, 1)
        start = doc_start_of(pos, docs_ref, docs)
        gate_ref[...] = jnp.where((src <= pos) & (src >= start), 0.0, NEG)
        for pair in range(heads // 2):
            cols = slice(pair * LANES, (pair + 1) * LANES)
            xd = xd_ref[sl, cols]
            found = []
            for head in (2 * pair, 2 * pair + 1):
                gap = ramp_ref[sl, head : head + 1] - rampt_ref[part, head : head + 1, :]
                high, low = split2(jnp.exp2(gap + gate_ref[...]) * cb_ref[...])
                found.append(mm(high, xd) + mm(low, xd))
            y_ref[sl, cols] = jnp.where(lane < HEAD_DIM, found[0], found[1])


def within(meta, doc_starts, xd, ramp, rampt, smalls, lows, rim_own, rim_recv, taps, heads):
    total, width = xd.shape
    rows, states2 = total // 2, lows[0].shape[1]
    vm = pl.BlockSpec(memory_space=pltpu.VMEM)
    return pl.pallas_call(
        functools.partial(within_kernel, doc_starts.shape[0], heads),
        grid_spec=pltpu.PrefetchScalarGridSpec(
            num_scalar_prefetch=2,
            grid=(),
            in_specs=[vm] * 14,
            out_specs=[vm] * 2,
            scratch_shapes=[
                pltpu.VMEM((rows, rows), F32),
                pltpu.VMEM((rows, rows), F32),
                pltpu.VMEM((total + 8, states2), F32),
                pltpu.VMEM((total, states2), BF),
                pltpu.VMEM((total, states2), BF),
            ],
        ),
        out_shape=[
            jax.ShapeDtypeStruct((total, width), F32),
            jax.ShapeDtypeStruct((2, rows, rows), F32),
        ],
        compiler_params=params(),
        cost_estimate=cost(6e9, 4e6),
        name="within",
    )(meta, doc_starts, xd, ramp, rampt, *smalls, *lows, rim_own, rim_recv, taps)


def chain_kernel(heads, reverse, recv_ref, keep_ref, out_ref):
    chips = recv_ref.shape[0]
    width = out_ref.shape[2]
    state = jnp.zeros(out_ref.shape[1:], F32)
    wide = spread(heads, width)
    for step in range(chips):
        i = chips - 1 - step if reverse else step
        out_ref[i] = state.astype(BF)
        if step < chips - 1:
            factor = mm(keep_ref[i, :, width:], wide)
            factor = factor[0:1] + factor[1:2] + factor[2:3]
            state = state * factor + recv_ref[i, :, :width].astype(F32)


def chain(recv, keeps, heads, width, reverse):
    chips, piece = recv.shape[0], recv.shape[1]
    return pl.pallas_call(
        functools.partial(chain_kernel, heads, reverse),
        out_shape=jax.ShapeDtypeStruct((chips, piece, width), BF),
        compiler_params=params(),
        cost_estimate=cost(1e8, 1e6),
        name="chain",
    )(recv, keeps)


def out_kernel(
    heads, meta_ref, y_ref, state_ref, loc_ref, bact_ref, epk_ref, keep_ref, go_ref, go_recv_ref,
    gain_ref, mix_own_ref, mix_send_ref, dy_ref, edy_ref, dot_ref, both_ref, late_ref, send_ref,
    go_all_ref, mix_ref,
):
    k = meta_ref[0]
    total, width = y_ref.shape
    rows = total // 2
    states = bact_ref.shape[1] // 2
    mine = pl.multiple_of(k * rows, rows)
    other = pl.multiple_of((1 - k) * rows, rows)
    go_all_ref[pl.ds(mine, rows), :] = go_ref[...]
    go_all_ref[pl.ds(other, rows), :] = go_recv_ref[...]
    state = state_ref[...]
    keep0 = keep_row(keep_ref[0], heads, width)[0:1, :]
    both_ref[0] = state
    both_ref[1] = (state.astype(F32) * keep0 + loc_ref[0]).astype(BF)
    wide = spread(heads, width)
    gather = gather_heads(width)
    tile = 128
    per = rows // tile

    def one(step, _):
        at = pl.multiple_of(step * tile, tile)
        sl = pl.ds(at, tile)
        enter = mm(epk_ref[sl, :], wide)
        carried = mm(bact_ref[sl, states:], both_ref[step // per])
        y = y_ref[sl, :] + carried * enter
        u = go_all_ref[sl, :].astype(F32) * gain_ref[...]
        mean = over_heads(y * y, gather) * (1.0 / HEAD_DIM)
        along = over_heads(u * y, gather)
        scale = lax.rsqrt(mean + epsilon)
        cube = scale * scale * scale
        wide_scale = mm(packed(scale), wide)
        wide_back = mm(packed(cube * along * (1.0 / HEAD_DIM)), wide)
        mix_ref[sl, :] = (y * wide_scale * gain_ref[...]).astype(BF)
        dy = u * wide_scale - y * wide_back
        hi, lo = split2(dy)
        for pair in range(width // LANES):
            cols = slice(pair * LANES, (pair + 1) * LANES)
            dy_ref[sl, 2 * pair * LANES : (2 * pair + 1) * LANES] = hi[:, cols]
            dy_ref[sl, (2 * pair + 1) * LANES : (2 * pair + 2) * LANES] = lo[:, cols]
        edy_ref[sl, :] = (dy * enter).astype(BF)
        dot_ref[sl, :] = epsilon * cube * along
        return 0

    lax.fori_loop(0, total // tile, one, 0)
    mix_own_ref[...] = mix_ref[pl.ds(mine, rows), :]
    mix_send_ref[...] = mix_ref[pl.ds(other, rows), :]
    late = mm_tn(bact_ref[rows:, states:], edy_ref[rows:, :])
    late_ref[...] = late
    back = late * keep0 + mm_tn(bact_ref[:rows, states:], edy_ref[:rows, :])
    chips, piece = send_ref.shape[0], send_ref.shape[1]
    for i in range(chips):
        send_ref[i] = back[i * piece : (i + 1) * piece, :].astype(BF)


def outputs_of(meta, y, state, loc, bact, epk, keep, grad_out, go_recv, gain, heads, chips):
    total, width = y.shape
    rows, states = total // 2, bact.shape[1] // 2
    whole = lambda shape: pl.BlockSpec(shape, lambda i, m: (0,) * len(shape))
    half = lambda count: pl.BlockSpec((count, width), lambda i, m: (0, m[0]))
    outs = [
        jax.ShapeDtypeStruct((rows, width), BF),
        jax.ShapeDtypeStruct((rows, width), BF),
        jax.ShapeDtypeStruct((total, 2 * width), BF),
        jax.ShapeDtypeStruct((total, width), BF),
        jax.ShapeDtypeStruct((total, LANES), F32),
        jax.ShapeDtypeStruct((2, states, width), BF),
        jax.ShapeDtypeStruct((states, width), F32),
        jax.ShapeDtypeStruct((chips, states // chips, width), BF),
    ]
    return pl.pallas_call(
        functools.partial(out_kernel, heads),
        grid_spec=pltpu.PrefetchScalarGridSpec(
            num_scalar_prefetch=1,
            grid=(1,),
            in_specs=[
                whole(y.shape), whole(state.shape), whole(loc.shape), whole(bact.shape),
                whole(epk.shape), whole(keep.shape), half(rows), whole(go_recv.shape), half(1),
            ],
            out_specs=[whole(o.shape) for o in outs],
            scratch_shapes=[pltpu.VMEM((total, width), BF), pltpu.VMEM((total, width), BF)],
        ),
        out_shape=outs,
        compiler_params=params(),
        cost_estimate=cost(4e9, 4e6),
        name="outputs_of",
    )(meta, y, state, loc, bact, epk, keep, grad_out, go_recv, gain)


def within_back_kernel(
    docs, heads, meta_ref, docs_ref, dy_ref, edy_ref, both_ref, xd_ref, bact_ref, ramp_ref,
    rampt_ref, cbt_ref, dxd_ref, dbc_ref, gate_ref, sum_ref,
):
    chip = meta_ref[2]
    total, width = xd_ref.shape
    rows = total // 2
    states = bact_ref.shape[1] // 2
    square = (rows, rows)
    lane = iota((rows, LANES), 1)
    for part in range(2):
        sl = slice(part * rows, (part + 1) * rows)
        begin = chip * total + part * rows
        b, c = bact_ref[sl, :states], bact_ref[sl, states:]
        src, pos = begin + iota(square, 0), begin + iota(square, 1)
        start = doc_start_of(pos, docs_ref, docs)
        gate_ref[...] = jnp.where((src <= pos) & (src >= start), 0.0, NEG)
        sum_ref[...] = jnp.zeros(square, F32)
        for pair in range(heads // 2):
            cols = slice(pair * LANES, (pair + 1) * LANES)
            xd = xd_ref[sl, cols]
            dy_both = dy_ref[sl, 2 * pair * LANES : (2 * pair + 2) * LANES]
            dy = dy_both[:, :LANES]
            found = []
            for side, head in enumerate((2 * pair, 2 * pair + 1)):
                keep_side = (lane < HEAD_DIM) if side == 0 else (lane >= HEAD_DIM)
                only = jnp.where(keep_side, xd.astype(F32), 0.0).astype(BF)
                only = jnp.concatenate([only, only], axis=1)
                gap = rampt_ref[part, head : head + 1, :] - ramp_ref[sl, head : head + 1]
                decay = jnp.exp2(gap + gate_ref[...])
                found.append(mm((decay * cbt_ref[part]).astype(BF), dy))
                sum_ref[...] += mm_nt(only, dy_both) * decay
            dxd_ref[sl, cols] = jnp.where(lane < HEAD_DIM, found[0], found[1])
        grad, low = split2(sum_ref[...])
        dbc_ref[sl, :states] = mm(grad, c) + mm(low, c)
        dbc_ref[sl, states:] = mm_tn(grad, b) + mm_tn(low, b) + mm_nt(edy_ref[sl, :], both_ref[part])


def within_back(meta, doc_starts, dy, edy, both, xd, bact, ramp, rampt, cbt, heads):
    total, width = xd.shape
    rows = total // 2
    vm = pl.BlockSpec(memory_space=pltpu.VMEM)
    return pl.pallas_call(
        functools.partial(within_back_kernel, doc_starts.shape[0], heads),
        grid_spec=pltpu.PrefetchScalarGridSpec(
            num_scalar_prefetch=2,
            grid=(),
            in_specs=[vm] * 8,
            out_specs=[vm] * 2,
            scratch_shapes=[pltpu.VMEM((rows, rows), F32)] * 2,
        ),
        out_shape=[
            jax.ShapeDtypeStruct((total, width), F32),
            jax.ShapeDtypeStruct((total, bact.shape[1]), F32),
        ],
        compiler_params=params(),
        cost_estimate=cost(1e10, 6e6),
        name="within_back",
    )(meta, doc_starts, dy, edy, both, xd, bact, ramp, rampt, cbt)


def grads_kernel(
    docs, heads, meta_ref, docs_ref, adj_ref, late_ref, loc_ref, both_ref, dxd_ref, dbc_ref,
    pre_ref, bpre_ref, xd_ref, bact_ref, delta_ref, sig_ref, dpk_ref, wpk_ref, keep_ref, dot_ref,
    prm_ref, taps_ref, taps_bc_ref, own_ref, other_ref, bc_own_ref, bc_other_ref, rim_ref,
    adj2_ref, gx_ref, gb_ref, q_ref, wx_ref, all_ref, bc_all_ref,
):
    k, chip = meta_ref[0], meta_ref[2]
    total, width = dxd_ref.shape
    rows = total // 2
    states2 = bact_ref.shape[1]
    states = states2 // 2
    base = chip * total
    mine = pl.multiple_of(k * rows, rows)
    other = pl.multiple_of((1 - k) * rows, rows)
    keep1 = keep_row(keep_ref[1], heads, width)[0:1, :]
    adj = adj_ref[...].astype(F32)
    early = adj * keep1 + late_ref[...]
    adj2_ref[0] = early.astype(BF)
    adj2_ref[1] = adj_ref[...]
    middle = both_ref[1].astype(F32)
    final = middle * keep1 + loc_ref[1]
    gather = gather_heads(width)
    ends = [
        over_heads(jnp.sum(a * s, axis=0, keepdims=True) + jnp.zeros((8, width), F32), gather)
        for a, s in ((early, middle), (adj, final))
    ]
    wide = spread(heads, width)
    tile = 64
    per = rows // tile
    gx_ref[0:8, :] = jnp.zeros((8, width), F32)
    gx_ref[total + 8 :, :] = jnp.zeros((8, width), F32)
    gb_ref[0:8, :] = jnp.zeros((8, states2), F32)
    gb_ref[total + 8 :, :] = jnp.zeros((8, states2), F32)

    def one(step, _):
        at = pl.multiple_of(step * tile, tile)
        sl = pl.ds(at, tile)
        part = step // per
        b = bact_ref[sl, :states]
        q = jnp.zeros((tile, LANES), F32)
        for lane in range(0, width, LANES):
            ls = slice(lane, lane + LANES)
            far = mm(b, adj2_ref[part, :, ls])
            w = mm(wpk_ref[sl, :], wide[:, ls])
            dxd = dxd_ref[sl, ls] + far * w
            act, slope = silu_parts(pre_ref[sl, ls])
            q = q + over_heads(act * dxd, gather[ls, :])
            gx_ref[pl.ds(pl.multiple_of(at + 8, 8), tile), ls] = dxd * mm(dpk_ref[sl, :], wide[:, ls]) * slope
            wx_ref[sl, ls] = (xd_ref[sl, ls].astype(F32) * w).astype(BF)
        q_ref[sl, :] = q
        return 0

    lax.fori_loop(0, total // tile, one, 0)
    square = (rows, rows)
    upper = jnp.where(iota(square, 0) <= iota(square, 1), 1.0, 0.0).astype(BF)
    rate = prm_ref[1:2, :]
    row = iota((rows, LANES), 0)
    for part in range(2):
        sl = slice(part * rows, (part + 1) * rows)
        q = q_ref[sl, :]
        ramp_grad = dot_ref[sl, :] - delta_ref[sl, :] * q
        ramp_grad = ramp_grad + jnp.where(row == rows - 1, ends[part][0:1, :], 0.0)
        hi, mid = split2(ramp_grad)
        low = (ramp_grad - hi.astype(F32) - mid.astype(F32)).astype(BF)
        later = mm(upper, hi) + mm(upper, mid) + mm(upper, low)
        bc_all_ref[sl, states2:] = ((q - rate * later) * sig_ref[sl, :])
        back = mm_nt(wx_ref[sl, :], adj2_ref[part])
        for lane, grad in ((0, dbc_ref[sl, :states] + back), (states, dbc_ref[sl, states:])):
            ls = slice(lane, lane + states)
            _, slope = silu_parts(bpre_ref[sl, ls])
            gb_ref[8 + part * rows : 8 + (part + 1) * rows, ls] = grad * slope

    def spill(src_ref, taps, at, count, ls):
        window = src_ref[pl.ds(at, count + 8), ls]
        value = window[:count] * taps[0:1, ls]
        pos = base + at - 8 + iota((count, LANES), 0)
        for j in range(1, 4):
            start = doc_start_of(pos + j, docs_ref, docs)
            mask = jnp.where(pos >= start, 1.0, 0.0)
            value = value + window[j : j + count] * taps[j : j + 1, ls] * mask
        return value

    def back(step, _):
        at = pl.multiple_of(step * tile, tile)
        sl = pl.ds(at, tile)
        for lane in range(0, width, LANES):
            ls = slice(lane, lane + LANES)
            all_ref[sl, ls] = spill(gx_ref, taps_ref, pl.multiple_of(at + 8, 8), tile, ls).astype(BF)
        for lane in range(0, states2, LANES):
            ls = slice(lane, lane + LANES)
            bc_all_ref[sl, ls] = spill(gb_ref, taps_bc_ref, pl.multiple_of(at + 8, 8), tile, ls)
        return 0

    lax.fori_loop(0, total // tile, back, 0)
    rim_ref[...] = jnp.zeros(rim_ref.shape, BF)
    pad = jnp.zeros((8, LANES), F32)
    for lane in range(0, width, LANES):
        ls = slice(lane, lane + LANES)
        value = jnp.concatenate([pad, spill(gx_ref, taps_ref, 0, 8, ls)], axis=0)
        rim_ref[:, ls] = value.astype(BF)
    for lane in range(0, states2, LANES):
        ls = slice(lane, lane + LANES)
        value = jnp.concatenate([pad, spill(gb_ref, taps_bc_ref, 0, 8, ls)], axis=0)
        rim_ref[:, width + lane : width + lane + LANES] = value.astype(BF)
    own_ref[...] = all_ref[pl.ds(mine, rows), :]
    other_ref[...] = all_ref[pl.ds(other, rows), :]
    bc_own_ref[...] = bc_all_ref[pl.ds(mine, rows), :]
    bc_other_ref[...] = bc_all_ref[pl.ds(other, rows), :]


def grads_of(
    meta, doc_starts, adj, late, loc, both, dxd, dbc, pre, bpre, xd, bact, delta, sig, dpk, wpk,
    keep, dots, prm, taps, taps_bc, heads,
):
    total, width = dxd.shape
    rows, states2 = total // 2, bact.shape[1]
    states = states2 // 2
    whole = lambda shape: pl.BlockSpec(shape, lambda i, m, d: (0,) * len(shape))
    half = pl.BlockSpec((taps.shape[0], width), lambda i, m, d: (0, m[0]))
    outs = [
        jax.ShapeDtypeStruct((rows, width), BF),
        jax.ShapeDtypeStruct((rows, width), BF),
        jax.ShapeDtypeStruct((rows, states2 + LANES), F32),
        jax.ShapeDtypeStruct((rows, states2 + LANES), F32),
        jax.ShapeDtypeStruct((16, width + states2), BF),
    ]
    ins = [adj, late, loc, both, dxd, dbc, pre, bpre, xd, bact, delta, sig, dpk, wpk, keep, dots, prm]
    return pl.pallas_call(
        functools.partial(grads_kernel, doc_starts.shape[0], heads),
        grid_spec=pltpu.PrefetchScalarGridSpec(
            num_scalar_prefetch=2,
            grid=(1,),
            in_specs=[whole(a.shape) for a in ins] + [half, whole(taps_bc.shape)],
            out_specs=[whole(o.shape) for o in outs],
            scratch_shapes=[
                pltpu.VMEM((2, states, width), BF),
                pltpu.VMEM((total + 16, width), F32),
                pltpu.VMEM((total + 16, states2), F32),
                pltpu.VMEM((total, LANES), F32),
                pltpu.VMEM((total, width), BF),
                pltpu.VMEM((total, width), BF),
                pltpu.VMEM((total, states2 + LANES), F32),
            ],
        ),
        out_shape=outs,
        compiler_params=params(),
        cost_estimate=cost(4e9, 8e6),
        name="grads_of",
    )(meta, doc_starts, *ins, taps, taps_bc)


def join_kernel(heads, meta_ref, own_ref, recv_ref, out_ref, send_ref):
    k = meta_ref[0]
    states2 = own_ref.shape[1] - LANES
    total = own_ref[:, :states2] + recv_ref[:, :states2]
    out_ref[:, :states2] = total
    send_ref[:, :states2] = total.astype(BF)
    shape = (LANES, LANES)
    row, col = iota(shape, 0), iota(shape, 1)
    mine = jnp.where((row < heads) & (col == row + k * heads), 1.0, 0.0).astype(BF)
    other = jnp.where((row < heads) & (col == row + (1 - k) * heads), 1.0, 0.0).astype(BF)
    steps = mm(own_ref[:, states2:].astype(BF), mine) + mm(recv_ref[:, states2:].astype(BF), other)
    out_ref[:, states2:] = steps
    send_ref[:, states2:] = steps.astype(BF)


def join(meta, own, recv, heads):
    vm = pl.BlockSpec(memory_space=pltpu.VMEM)
    return pl.pallas_call(
        functools.partial(join_kernel, heads),
        grid_spec=pltpu.PrefetchScalarGridSpec(
            num_scalar_prefetch=1, grid=(), in_specs=[vm] * 2, out_specs=[vm] * 2
        ),
        out_shape=[jax.ShapeDtypeStruct(own.shape, F32), jax.ShapeDtypeStruct(own.shape, BF)],
        compiler_params=params(),
        cost_estimate=cost(1e8, 1e6),
        name="join",
    )(meta, own, recv)


def first_kernel(meta_ref, mine_ref, other_ref, rim_ref, w_mine_ref, w_other_ref, out_ref):
    rows, width = mine_ref.shape

    def whole(ref, rim):
        tail = ref[rows - 16 :, :].astype(F32) + rim.astype(F32)
        return jnp.concatenate([ref[: rows - 16, :], tail.astype(BF)], axis=0)

    mine = whole(mine_ref, rim_ref[:16, :width])
    other = whole(other_ref, rim_ref[16:, :width])
    out_ref[...] = mm_nt(mine, w_mine_ref[...]) + mm_nt(other, w_other_ref[...])


def first_half(blocks, mine, other, rim, x_weight, tile):
    rows, width = mine.shape
    depth = x_weight.shape[0]
    whole = lambda shape: pl.BlockSpec(shape, lambda i, m: (0, 0))
    return pl.pallas_call(
        first_kernel,
        grid_spec=pltpu.PrefetchScalarGridSpec(
            num_scalar_prefetch=1,
            grid=(depth // tile,),
            in_specs=[
                whole(mine.shape), whole(other.shape), whole(rim.shape),
                pl.BlockSpec((tile, width), lambda i, m: (i, m[0])),
                pl.BlockSpec((tile, width), lambda i, m: (i, m[1])),
            ],
            out_specs=pl.BlockSpec((rows, tile), lambda i, m: (0, i)),
        ),
        out_shape=jax.ShapeDtypeStruct((rows, depth), F32),
        compiler_params=params(),
        cost_estimate=cost(2e9, 4e6),
        name="first_half",
    )(blocks, mine, other, rim, x_weight, x_weight)


def last_kernel(
    heads, side_ref, part_ref, mine_ref, other_ref, rim_ref, rim0_ref, bc_own_ref, bc_recv_ref,
    w_mine_ref, w_other_ref, bcw_ref, dtw_ref, out_ref, bc_ref, dt_ref, left_ref, right_ref,
):
    rows, width = mine_ref.shape
    states2 = bcw_ref.shape[1]
    all_heads = dtw_ref.shape[1]

    @pl.when(pl.program_id(0) == 0)
    def _():
        for ref, rim, to_ref in (
            (mine_ref, rim_ref[:16, :width], left_ref),
            (other_ref, rim_ref[16:, :width], right_ref),
        ):
            to_ref[: rows - 16, :] = ref[: rows - 16, :]
            to_ref[rows - 16 :, :] = (ref[rows - 16 :, :].astype(F32) + rim.astype(F32)).astype(BF)
        bc = bc_own_ref[:, :states2] + bc_recv_ref[:, :states2].astype(F32)
        rim = rim_ref[...].astype(F32) + rim0_ref[...].astype(F32)
        extra = rim[:16, width:] + rim[16:, width:]
        for at, value in ((0, bc[: rows - 16, :]), (rows - 16, bc[rows - 16 :, :] + extra)):
            high, low = split2(value)
            bc_ref[at : at + value.shape[0], :states2] = high
            bc_ref[at : at + value.shape[0], states2:] = low
        shape = (LANES, all_heads)
        row, col = iota(shape, 0), iota(shape, 1)
        x = side_ref[2]
        here = jnp.where((row < heads) & (col == row + x * heads), 1.0, 0.0).astype(BF)
        there = jnp.where((row < heads) & (col == row + (1 - x) * heads), 1.0, 0.0).astype(BF)
        dt_ref[...] = (mm(bc_own_ref[:, states2:].astype(BF), here) + mm(bc_recv_ref[:, states2:], there)).astype(BF)

    total = part_ref[...] + mm_nt(left_ref[...], w_mine_ref[...])
    total = total + mm_nt(right_ref[...], w_other_ref[...])
    bcw = bcw_ref[...]
    total = total + mm_nt(bc_ref[...], jnp.concatenate([bcw, bcw], axis=1)) + mm_nt(dt_ref[...], dtw_ref[...])
    out_ref[...] = total.astype(BF)


def last_half(blocks, part, mine, other, rim, rim0, bc_own, bc_recv, x_weight, bc_weight, dt_weight, tile):
    rows, width = mine.shape
    depth = x_weight.shape[0]
    states2, all_heads = bc_weight.shape[1], dt_weight.shape[1]
    whole = lambda a: pl.BlockSpec(a.shape, lambda i, m: (0, 0))
    return pl.pallas_call(
        functools.partial(last_kernel, all_heads // 2),
        grid_spec=pltpu.PrefetchScalarGridSpec(
            num_scalar_prefetch=1,
            grid=(depth // tile,),
            in_specs=[
                pl.BlockSpec((rows, tile), lambda i, m: (0, i)),
                whole(mine), whole(other), whole(rim), whole(rim0), whole(bc_own), whole(bc_recv),
                pl.BlockSpec((tile, width), lambda i, m: (i, m[0])),
                pl.BlockSpec((tile, width), lambda i, m: (i, m[1])),
                pl.BlockSpec((tile, states2), lambda i, m: (i, 0)),
                pl.BlockSpec((tile, all_heads), lambda i, m: (i, 0)),
            ],
            out_specs=pl.BlockSpec((rows, tile), lambda i, m: (0, i)),
            scratch_shapes=[
                pltpu.VMEM((rows, 2 * states2), BF),
                pltpu.VMEM((rows, all_heads), BF),
                pltpu.VMEM((rows, width), BF),
                pltpu.VMEM((rows, width), BF),
            ],
        ),
        out_shape=jax.ShapeDtypeStruct((rows, depth), BF),
        compiler_params=params(),
        cost_estimate=cost(2e9, 4e6),
        name="last_half",
    )(blocks, part, mine, other, rim, rim0, bc_own, bc_recv, x_weight, x_weight, bc_weight, dt_weight)


def by_chips(
    tokens, x_weight, bc_weight, dt_weight, conv_inner, conv_shared, dt_bias, decay_rate, norm_gain,
    doc_starts, grad_out,
):
    blocks = lax.axis_size("ctx")
    chips = blocks // 2
    rows = tokens.shape[0]
    all_heads = dt_weight.shape[1]
    heads = decay_rate.shape[0] // 2
    width = heads * HEAD_DIM
    place = lax.axis_index("ctx").astype(jnp.int32)
    x = lax.axis_index("fsdp").astype(jnp.int32)
    k = place % 2
    meta = jnp.stack([k, x, place // 2])

    core = [(i, i ^ 1) for i in range(blocks)]
    pair = [(0, 1), (1, 0)]
    cross = [(2 * i + j, 2 * (i ^ 1) + (1 - j)) for i in range(blocks) for j in range(2)]
    by_core = lambda a: lax.ppermute(a, "ctx", core)
    by_x = lambda a: lax.ppermute(a, "fsdp", pair)
    by_both = lambda a: lax.ppermute(a, ("ctx", "fsdp"), cross)
    groups = [[2 * i for i in range(chips)], [2 * i + 1 for i in range(chips)]]
    exchange = lambda a: lax.all_to_all(a, "ctx", 0, 0, axis_index_groups=groups)

    def column_block(side, half):
        return (side * 2 + half)[None]

    tail = tokens[rows - 16 :]
    ra = lax.ppermute(tail, "ctx", [(2 * i - 1, 2 * i) for i in range(1, chips)])
    rb = lax.ppermute(tail, "ctx", [(2 * i - 1, 2 * i + 1) for i in range(1, chips)])

    small, low = small_proj(tokens, bc_weight, dt_weight)
    small_x = by_x(small)
    to_cross = proj_piece(tokens, x_weight, column_block(1 - x, 1 - k), width)
    from_cross = by_both(to_cross)
    to_x = proj_piece(tokens, x_weight, column_block(1 - x, k), width)
    from_x = by_x(to_x)
    to_core = proj_piece(tokens, x_weight, column_block(x, 1 - k), width)
    from_core = by_core(to_core)
    mine = proj_piece(tokens, x_weight, column_block(x, k), width)
    rim_own, rim_send = rim_proj(
        ra, rb, x_weight, bc_weight, jnp.stack([x * 2 + k, (1 - x) * 2 + k]), width
    )
    rim_recv = by_x(rim_send)
    small_core = by_core(small)
    small_cross = by_core(small_x)
    low_x = by_x(low)
    lows = (low, low_x, by_core(low), by_core(low_x))
    go_recv = by_core(lax.dynamic_slice(grad_out, (jnp.int32(0), (1 - k) * width), (rows, width)))

    prm = jnp.stack([lax.dynamic_slice(v, (k * heads,), (heads,)) for v in (dt_bias, decay_rate)])
    prm = jnp.pad(prm, ((0, 6), (0, LANES - heads)))
    bact, bpre, delta, ramp, sig, rampt, dpk, wpk, epk, keep = shared_maps(
        meta, doc_starts, small, small_x, small_core, small_cross, rim_own, rim_recv, conv_shared,
        prm, heads, all_heads,
    )
    pre, xd, loc, send = inner_maps(
        meta, doc_starts, mine, from_x, from_core, from_cross, rim_own, rim_recv, conv_inner, bact,
        dpk, wpk, keep, heads, chips,
    )
    keeps = exchange(send)
    y, cbt = within(
        meta, doc_starts, xd, ramp, rampt, (small, small_x, small_core, small_cross), lows, rim_own, rim_recv,
        conv_shared, heads,
    )
    states = exchange(chain(keeps, keeps, heads, width, False))
    state = states.reshape(STATE, width)
    mix_own, mix_send, dy, edy, dots, both, late, back = outputs_of(
        meta, y, state, loc, bact, epk, keep, grad_out, go_recv, norm_gain[None, :], heads, chips
    )
    backs = exchange(back)
    dxd, dbc = within_back(meta, doc_starts, dy, edy, both, xd, bact, ramp, rampt, cbt, heads)
    mix_recv = by_core(mix_send)
    mixed = jnp.where(
        k == 0,
        jnp.concatenate([mix_own, mix_recv], axis=1),
        jnp.concatenate([mix_recv, mix_own], axis=1),
    )
    adj = exchange(chain(backs, keeps, heads, width, True)).reshape(STATE, width)
    g_mine, g_other, bc_mine, bc_other, rim = grads_of(
        meta, doc_starts, adj, late, loc, both, dxd, dbc, pre, bpre, xd, bact, delta, sig, dpk, wpk,
        keep, dots, prm, conv_inner, conv_shared, heads,
    )
    g_x = by_x(g_mine)
    g_cross = by_both(g_other)
    g_core = by_core(g_other)
    rims = jnp.concatenate([rim, by_core(rim)], axis=0)
    back_perm = [(2 * i + 1, 2 * i - 1) for i in range(1, chips)]
    rim0 = lax.ppermute(rims, "ctx", back_perm)
    rim1 = lax.ppermute(
        rims, ("ctx", "fsdp"), [(2 * a + j, 2 * b + (1 - j)) for a, b in back_perm for j in range(2)]
    )
    bc_chip, bc_send = join(meta, bc_mine, by_core(bc_other), heads)
    bc_recv = by_x(bc_send)
    part = first_half(
        jnp.stack([x * 2 + k, x * 2 + 1 - k]), g_mine, g_core, rim0, x_weight, 256
    )
    grad_tokens = last_half(
        jnp.stack([(1 - x) * 2 + k, (1 - x) * 2 + 1 - k, x]), part, g_x, g_cross, rim1, rim0, bc_chip,
        bc_recv, x_weight, bc_weight, dt_weight, 256,
    )
    return (mixed, grad_tokens)


def splits_by_chip(mesh):
    return mesh.shape["fsdp"] == 2 and mesh.shape["ctx"] == 16


def solution(mesh):
    in_specs = (
        P("ctx", "fsdp"),
        P("fsdp", None),
        P("fsdp", None),
        P("fsdp", None),
        P(None, "fsdp"),
        P(),
        P("fsdp"),
        P("fsdp"),
        P("fsdp"),
        P(),
        P("ctx", "fsdp"),
    )
    body = by_chips if splits_by_chip(mesh) else on_device
    out_specs = (P("ctx", "fsdp"), P("ctx", "fsdp"))
    return jax.shard_map(
        body, mesh=mesh, in_specs=in_specs, out_specs=out_specs, check_vma=False
    )
```

profile of v0, /device:TPU:0, one launch (start us, length us, event | category | flops | bytes accessed | tf_op | source)
XLA Modules:
  0.0 169.5 jit_solution(13563688852682642169)
XLA Ops:
  2.7 1.8 %copy.13.dtw_ref = bf16[1280,40]{1,0:T(8,128)(2,1)} copy(bf16[1280,40]{0,1:T(8,128)(2,1)} %param.14) | data formatting | bytes 204800 | tf_op args[3]
  4.5 2.8 %small_proj.1 = (bf16[256,384]{1,0:T(8,128)(2,1)}, bf16[256,256]{1,0:T(8,128)(2,1)}) custom-call(bf16[256,1280]{1,0:T(8,128)(2,1)} %tok_ref.9, bf16[1280,256]{1,0:T(8,128)(2,1)} %bcw_ref.5, bf16[1280,40]{1,0:T(8,128)(2,1)} %copy.13.dtw_ref), custom_call_target="tpu_custom_call" | custom-call | flops 300000000 | bytes 2000000 | tf_op jit(solution)/shard_map/small_proj/pallas_call | solution.py:259
  7.3 4.4 %collective-permute-start.7 = (bf16[256,384]{1,0:T(8,128)(2,1)}, bf16[256,384]{1,0:T(8,128)(2,1)S(1)}, u32[]{:S(2)}, u32[]{:S(2)}) collective-permute-start(bf16[256,384]{1,0:T(8,128)(2,1)} %get-tuple-element.41.own_ref), channel_id=1, source_target_pairs={{0,2},{2,0},{4,6},{6,4},{8,10},{10,8},{12,14},{14,12},{16,18},{18,... | collective-permute-start | bytes 589832 | tf_op jit(solution)/shard_map/ppermute | solution.py:1118
  11.7 1.5 collective-permute-start.6
  13.2 4.9 %proj_piece.6 = bf16[256,640]{1,0:T(8,128)(2,1)} custom-call(s32[1]{0:T(128)} %bitcast.5.meta_ref, bf16[256,1280]{1,0:T(8,128)(2,1)} %tok_ref.9, bf16[1280,2560]{1,0:T(8,128)(2,1)} %w_other_ref.3), custom_call_target="tpu_custom_call" | custom-call | flops 419430400 | bytes 1638400 | tf_op jit(solution)/shard_map/proj_piece/pallas_call | solution.py:278
  20.4 4.8 %proj_piece.4.own_ref = bf16[256,640]{1,0:T(8,128)(2,1)} custom-call(s32[1]{0:T(128)} %bitcast.3.meta_ref, bf16[256,1280]{1,0:T(8,128)(2,1)} %tok_ref.9, bf16[1280,2560]{1,0:T(8,128)(2,1)} %w_other_ref.3), custom_call_target="tpu_custom_call" | custom-call | flops 419430400 | bytes 1638400 | tf_op jit(solution)/shard_map/proj_piece/pallas_call | solution.py:278
  25.3 4.9 %proj_piece.7 = bf16[256,640]{1,0:T(8,128)(2,1)} custom-call(s32[1]{0:T(128)} %bitcast.6.meta_ref, bf16[256,1280]{1,0:T(8,128)(2,1)} %tok_ref.9, bf16[1280,2560]{1,0:T(8,128)(2,1)} %w_other_ref.3), custom_call_target="tpu_custom_call" | custom-call | flops 419430400 | bytes 1638400 | tf_op jit(solution)/shard_map/proj_piece/pallas_call | solution.py:278
  31.4 4.0 %rim_proj.1 = (bf16[16,896]{1,0:T(8,128)(2,1)}, bf16[16,896]{1,0:T(8,128)(2,1)}) custom-call(s32[2]{0:T(128)} %pad_add_fusion.1.meta_ref, bf16[16,1280]{1,0:T(8,128)(2,1)} %copy-done.14, bf16[16,1280]{1,0:T(8,128)(2,1)} %copy-done.13, bf16[1280,2560]{1,0:T(8,128)(2,1)} %w_other_ref.3, bf16[1280,2560]{1,0:T(8,128)(2,1)} %w_other_ref.3, bf16[1280,256]{1,0:T(8,128)(2,1)} %bcw_ref.5), custom_call_target="tpu_custom_call" | custom-call | flops 52428800 | bytes 3276800 | tf_op jit(solution)/shard_map/rim_proj/pallas_call | solution.py:311
  36.5 4.8 %proj_piece.5 = bf16[256,640]{1,0:T(8,128)(2,1)} custom-call(s32[1]{0:T(128)} %bitcast.4.meta_ref, bf16[256,1280]{1,0:T(8,128)(2,1)} %tok_ref.9, bf16[1280,2560]{1,0:T(8,128)(2,1)} %w_other_ref.3), custom_call_target="tpu_custom_call" | custom-call | flops 419430400 | bytes 1638400 | tf_op jit(solution)/shard_map/proj_piece/pallas_call | solution.py:278
  43.1 5.0 %shared_maps.1 = (bf16[512,256]{1,0:T(8,128)(2,1)}, f32[512,256]{1,0:T(8,128)}, f32[512,128]{1,0:T(8,128)}, f32[512,128]{1,0:T(8,128)}, f32[512,128]{1,0:T(8,128...) custom-call(s32[3]{0:T(128)} %pad_add_fusion.meta_ref, ...), custom_call_target="tpu_custom_call" | custom-call | flops 4000000000 | bytes 4000000 | tf_op jit(solution)/shard_map/shared_maps/pallas_call | solution.py:415
  48.1 3.3 %collective-permute-done.xr_ref = bf16[256,640]{1,0:T(8,128)(2,1)S(1)} collective-permute-done((bf16[256,640]{1,0:T(8,128)(2,1)}, bf16[256,640]{1,0:T(8,128)(2,1)S(1)}, u32[]{:S(2)}, u32[]{:S(2)}) %collective-permute-start) | collective-permute-done | bytes 327712 | tf_op jit(solution)/shard_map/ppermute | solution.py:1119
  52.1 6.3 %inner_maps.1 = (f32[512,640]{1,0:T(8,128)}, bf16[512,640]{1,0:T(8,128)(2,1)}, f32[2,128,640]{2,1,0:T(8,128)}, bf16[8,16,768]{2,1,0:T(8,128)(2,1)}) custom-call(s32[3]{0:T(128)} %pad_add_fusion.meta_ref, s32[4]{0:T(128)} %docs_ref.9, bf16[256,640]{1,0:T(8,128)(2,1)} %proj_piece.4.own_ref, bf16[256,640]{1,0:T(8,128)(2,1)} %copy-done.22, ...), custom_call_target="tpu_custom_call" | custom-call | flops 4000000000 | bytes 4000000 | tf_op jit(solution)/shard_map/inner_maps/pallas_call | solution.py:528
  58.4 4.9 %all-to-all-start = ((bf16[8,16,768]{2,1,0:T(8,128)(2,1)}), bf16[8,16,768]{2,1,0:T(8,128)(2,1)S(1)}, u32[]{:S(2)}, u32[]{:S(2)}) async-start(bf16[8,16,768]{2,1,0:T(8,128)(2,1)} %get-tuple-element.51), calls=%async_computation | async-start | bytes 393216 | tf_op jit(solution)/shard_map/all_to_all | solution.py:1122
  63.9 4.4 %collective-permute-done.9.xr_low_ref = bf16[256,256]{1,0:T(8,128)(2,1)S(1)} collective-permute-done((bf16[256,256]{1,0:T(8,128)(2,1)S(1)}, bf16[256,256]{1,0:T(8,128)(2,1)S(1)}, u32[]{:S(2)}, u32[]{:S(2)}) %collective-permute-start.9) | collective-permute-done | bytes 131104 | tf_op jit(solution)/shard_map/ppermute | solution.py:1119
  69.5 1.5 all-to-all-done.recv_ref.keep_ref
  71.7 2.1 %chain.2 = bf16[8,16,640]{2,1,0:T(8,128)(2,1)} custom-call(bf16[8,16,768]{2,1,0:T(8,128)(2,1)} %copy-done, bf16[8,16,768]{2,1,0:T(8,128)(2,1)} %copy-done), custom_call_target="tpu_custom_call" | custom-call | flops 100000000 | bytes 1000000 | tf_op jit(solution)/shard_map/chain/pallas_call | solution.py:654
  73.8 4.4 %all-to-all-start.1 = ((bf16[8,16,640]{2,1,0:T(8,128)(2,1)}), bf16[8,16,640]{2,1,0:T(8,128)(2,1)S(1)}, u32[]{:S(2)}, u32[]{:S(2)}) async-start(bf16[8,16,640]{2,1,0:T(8,128)(2,1)} %chain.2), calls=%async_computation.1 | async-start | bytes 327680 | tf_op jit(solution)/shard_map/all_to_all | solution.py:1122
  78.9 6.8 %within.1 = (f32[512,640]{1,0:T(8,128)}, f32[2,256,256]{2,1,0:T(8,128)}) custom-call(s32[3]{0:T(128)} %pad_add_fusion.meta_ref, s32[4]{0:T(128)} %docs_ref.9, bf16[512,640]{1,0:T(8,128)(2,1)} %get-tuple-element.46.xd_ref, f32[512,128]{1,0:T(8,128)} %get-tuple-element.47.ramp_ref, f32[2,16,256]{2,1,0:T(8,128)} %get-tuple-element.48.rampt_ref, ...), custom_call_target="tpu_custom_call" | custom-call | flops 6000000000 | bytes 4000000 | tf_op jit(solution)/shard_map/within/pallas_call | solution.py:613
  86.5 8.0 %outputs_of.1 = (bf16[256,640]{1,0:T(8,128)(2,1)}, bf16[256,640]{1,0:T(8,128)(2,1)}, bf16[512,1280]{1,0:T(8,128)(2,1)}, bf16[512,640]{1,0:T(8,128)(2,1)}, f32[51...) custom-call(s32[3]{0:T(128)} %pad_add_fusion.meta_ref, ...), custom_call_target="tpu_custom_call" | custom-call | flops 4000000000 | bytes 4000000 | tf_op jit(solution)/shard_map/outputs_of/pallas_call | solution.py:735
  94.5 6.0 %all-to-all-start.2 = ((bf16[8,16,640]{2,1,0:T(8,128)(2,1)}), bf16[8,16,640]{2,1,0:T(8,128)(2,1)S(1)}, u32[]{:S(2)}, u32[]{:S(2)}) async-start(bf16[8,16,640]{2,1,0:T(8,128)(2,1)} %get-tuple-element.56), calls=%async_computation.2 | async-start | bytes 327680 | tf_op jit(solution)/shard_map/all_to_all | solution.py:1122
  100.5 7.6 %all-to-all-done.2.recv_ref = bf16[8,16,640]{2,1,0:T(8,128)(2,1)S(1)} async-done(((bf16[8,16,640]{2,1,0:T(8,128)(2,1)}), bf16[8,16,640]{2,1,0:T(8,128)(2,1)S(1)}, u32[]{:S(2)}, u32[]{:S(2)}) %all-to-all-start.2) | async-done | bytes 163872 | tf_op jit(solution)/shard_map/all_to_all | solution.py:1122
  108.8 2.0 %chain.3 = bf16[8,16,640]{2,1,0:T(8,128)(2,1)} custom-call(bf16[8,16,640]{2,1,0:T(8,128)(2,1)} %copy-done.1, bf16[8,16,768]{2,1,0:T(8,128)(2,1)} %copy-done), custom_call_target="tpu_custom_call" | custom-call | flops 100000000 | bytes 1000000 | tf_op jit(solution)/shard_map/chain/pallas_call | solution.py:654
  110.8 3.6 %all-to-all-start.3 = ((bf16[8,16,640]{2,1,0:T(8,128)(2,1)}), bf16[8,16,640]{2,1,0:T(8,128)(2,1)S(1)}, u32[]{:S(2)}, u32[]{:S(2)}) async-start(bf16[8,16,640]{2,1,0:T(8,128)(2,1)} %chain.3), calls=%async_computation.3 | async-start | bytes 327680 | tf_op jit(solution)/shard_map/all_to_all | solution.py:1122
  114.4 6.1 %within_back.1 = (f32[512,640]{1,0:T(8,128)}, f32[512,256]{1,0:T(8,128)}) custom-call(s32[3]{0:T(128)} %pad_add_fusion.meta_ref, s32[4]{0:T(128)} %docs_ref.9, bf16[512,1280]{1,0:T(8,128)(2,1)} %get-tuple-element.59.dy_ref, bf16[512,640]{1,0:T(8,128)(2,1)} %get-tuple-element.60.edy_ref, bf16[2,128,640]{2,1,0:T(8,128)(2,1)} %get-tuple-element.58.both_ref, ...), custom_call_target="tpu_custom_call" | custom-call | flops 10000000000 | bytes 6000000 | tf_op jit(solution)/shard_map/within_back/pallas_call | solution.py:796
  120.5 1.2 all-to-all-done.3
  122.3 14.4 %grads_of.1 = (bf16[256,640]{1,0:T(8,128)(2,1)}, bf16[256,640]{1,0:T(8,128)(2,1)}, f32[256,384]{1,0:T(8,128)}, f32[256,384]{1,0:T(8,128)}, bf16[16,896]{1,0:T(8,128)(2,1)}) custom-call(s32[3]{0:T(128)} %pad_add_fusion.meta_ref, s32[4]{0:T(128)} %docs_ref.9, bf16[128,640]{1,0:T(8,128)(2,1)} %bitcast.16, f32[128,640]{1,0:T(8,128)} %get-tuple-element.57.late_ref, ...), custom_call_target="tpu_custom_call" | custom-call | flops 4000000000 | bytes 8000000 | tf_op jit(solution)/shard_map/grads_of/pallas_call | solution.py:942
  140.0 1.5 collective-permute-start.17
  142.2 2.8 %join.1 = (f32[256,384]{1,0:T(8,128)}, bf16[256,384]{1,0:T(8,128)(2,1)}) custom-call(s32[3]{0:T(128)} %pad_add_fusion.meta_ref, f32[256,384]{1,0:T(8,128)} %get-tuple-element.72.own_ref, f32[256,384]{1,0:T(8,128)} %copy-done.2), custom_call_target="tpu_custom_call" | custom-call | flops 100000000 | bytes 1000000 | tf_op jit(solution)/shard_map/join/pallas_call | solution.py:983
  147.9 6.2 %first_half.1.part_ref = f32[256,1280]{1,0:T(8,128)} custom-call(s32[2]{0:T(128)} %pad_add_fusion.3.meta_ref, bf16[256,640]{1,0:T(8,128)(2,1)} %get-tuple-element.69.mine_ref, bf16[256,640]{1,0:T(8,128)(2,1)} %copy-done.6, bf16[32,896]{1,0:T(8,128)(2,1)} %copy-done.7, bf16[1280,2560]{1,0:T(8,128)(2,1)} %w_other_ref.3, bf16[1280,2560]{1,0:T(8,128)(2,1)} %w_other_ref.3), custom_call_target="tpu_custom_call" | custom-call | flops 2000000000 | bytes 4000000 | tf_op jit(solution)/shard_map/first_half/pallas_call | solution.py:1011
  154.2 3.6 %collective-permute-done.17.mine_ref = bf16[256,640]{1,0:T(8,128)(2,1)S(1)} collective-permute-done((bf16[256,640]{1,0:T(8,128)(2,1)}, bf16[256,640]{1,0:T(8,128)(2,1)S(1)}, u32[]{:S(2)}, u32[]{:S(2)}) %collective-permute-start.17) | collective-permute-done | bytes 327712 | tf_op jit(solution)/shard_map/ppermute | solution.py:1119
  157.7 3.6 %collective-permute-done.21.bc_recv_ref = bf16[256,384]{1,0:T(8,128)(2,1)S(1)} collective-permute-done((bf16[256,384]{1,0:T(8,128)(2,1)}, bf16[256,384]{1,0:T(8,128)(2,1)S(1)}, u32[]{:S(2)}, u32[]{:S(2)}) %collective-permute-start.21) | collective-permute-done | bytes 196640 | tf_op jit(solution)/shard_map/ppermute | solution.py:1119
  162.0 7.5 %last_half.1 = bf16[256,1280]{1,0:T(8,128)(2,1)} custom-call(s32[3]{0:T(128)} %pad_add_fusion.2.side_ref, f32[256,1280]{1,0:T(8,128)} %first_half.1.part_ref, bf16[256,640]{1,0:T(8,128)(2,1)} %copy-done.5, bf16[256,640]{1,0:T(8,128)(2,1)} %copy-done.4, bf16[32,896]{1,0:T(8,128)(2,1)} %copy-done.12, bf16[32,896]{1,0:T(8,128)(2,1)} %copy-done.7, ...), custom_call_target="tpu_custom_call" | custom-call | flops 2000000000 | bytes 4000000 | tf_op jit(solution)/shard_map/last_half/pallas_call | solution.py:1072
  (112 shorter events, 22.2 us)
Async XLA Ops:
  1.4 28.7 %collective-permute-start.4 = (bf16[16,1280]{1,0:T(8,128)(2,1)S(1)}, bf16[16,1280]{1,0:T(8,128)(2,1)S(1)}, u32[]{:S(2)}, u32[]{:S(2)}) collective-permute-start(bf16[16,1280]{1,0:T(8,128)(2,1)S(1)} %slice.3), channel_id=1, source_target_pairs={{2,6},{6,10},{10,14},{14,18},{18,22},{22,26},{26,30},{3,7},{7,11},... | collective-permute-start | bytes 122888 | tf_op jit(solution)/shard_map/ppermute | solution.py:1129
  2.1 28.6 %collective-permute-start.3 = (bf16[16,1280]{1,0:T(8,128)(2,1)S(1)}, bf16[16,1280]{1,0:T(8,128)(2,1)S(1)}, u32[]{:S(2)}, u32[]{:S(2)}) collective-permute-start(bf16[16,1280]{1,0:T(8,128)(2,1)S(1)} %slice.3), channel_id=1, source_target_pairs={{2,4},{6,8},{10,12},{14,16},{18,20},{22,24},{26,28},{3,5},{7,9},{1... | collective-permute-start | bytes 122888 | tf_op jit(solution)/shard_map/ppermute | solution.py:1128
  7.3 35.0 %collective-permute-start.7 = (bf16[256,384]{1,0:T(8,128)(2,1)}, bf16[256,384]{1,0:T(8,128)(2,1)S(1)}, u32[]{:S(2)}, u32[]{:S(2)}) collective-permute-start(bf16[256,384]{1,0:T(8,128)(2,1)} %get-tuple-element.41.own_ref), channel_id=1, source_target_pairs={{0,2},{2,0},{4,6},{6,4},{8,10},{10,8},{12,14},{14,12},{16,18},{18,... | collective-permute-start | bytes 589832 | tf_op jit(solution)/shard_map/ppermute | solution.py:1118
  11.7 7.6 %collective-permute-start.6 = (bf16[256,384]{1,0:T(8,128)(2,1)}, bf16[256,384]{1,0:T(8,128)(2,1)S(1)}, u32[]{:S(2)}, u32[]{:S(2)}) collective-permute-start(bf16[256,384]{1,0:T(8,128)(2,1)} %get-tuple-element.41.own_ref), channel_id=1, source_target_pairs={{0,1},{1,0},{2,3},{3,2},{4,5},{5,4},{6,7},{7,6},{8,9},{9,8},{10,11... | collective-permute-start | bytes 589832 | tf_op jit(solution)/shard_map/ppermute | solution.py:1119
  18.0 30.0 %collective-permute-start.1 = (bf16[256,640]{1,0:T(8,128)(2,1)}, bf16[256,640]{1,0:T(8,128)(2,1)S(1)}, u32[]{:S(2)}, u32[]{:S(2)}) collective-permute-start(bf16[256,640]{1,0:T(8,128)(2,1)} %proj_piece.6), channel_id=1, source_target_pairs={{0,2},{2,0},{4,6},{6,4},{8,10},{10,8},{12,14},{14,12},{16,18},{18,... | collective-permute-start | bytes 983048 | tf_op jit(solution)/shard_map/ppermute | solution.py:1118
  19.3 23.0 %collective-permute-start.8 = (bf16[256,384]{1,0:T(8,128)(2,1)S(1)}, bf16[256,384]{1,0:T(8,128)(2,1)S(1)}, u32[]{:S(2)}, u32[]{:S(2)}) collective-permute-start(bf16[256,384]{1,0:T(8,128)(2,1)S(1)} %collective-permute-done.6.xr_ref), channel_id=1, source_target_pairs={{0,2},{2,0},{4,6},{6,4},{8,10},{10,8},{12,14},{14,12},{16,18},{18,... | collective-permute-start | bytes 589832 | tf_op jit(solution)/shard_map/ppermute | solution.py:1118
  30.1 17.9 %collective-permute-start.2 = (bf16[256,640]{1,0:T(8,128)(2,1)}, bf16[256,640]{1,0:T(8,128)(2,1)S(1)}, u32[]{:S(2)}, u32[]{:S(2)}) collective-permute-start(bf16[256,640]{1,0:T(8,128)(2,1)} %proj_piece.7), channel_id=1, source_target_pairs={{0,3},{1,2},{2,1},{3,0},{4,7},{5,6},{6,5},{7,4},{8,11},{9,10},{10,... | collective-permute-start | bytes 983048 | tf_op jit(solution)/shard_map/ppermute | solution.py:1120
  35.4 5.9 %collective-permute-start.5 = (bf16[16,896]{1,0:T(8,128)(2,1)}, bf16[16,896]{1,0:T(8,128)(2,1)S(1)}, u32[]{:S(2)}, u32[]{:S(2)}) collective-permute-start(bf16[16,896]{1,0:T(8,128)(2,1)} %get-tuple-element.40), channel_id=1, source_target_pairs={{0,1},{1,0},{2,3},{3,2},{4,5},{5,4},{6,7},{7,6},{8,9},{9,8},{10,11... | collective-permute-start | bytes 86024 | tf_op jit(solution)/shard_map/ppermute | solution.py:1119
  41.3 10.0 %collective-permute-start = (bf16[256,640]{1,0:T(8,128)(2,1)}, bf16[256,640]{1,0:T(8,128)(2,1)S(1)}, u32[]{:S(2)}, u32[]{:S(2)}) collective-permute-start(bf16[256,640]{1,0:T(8,128)(2,1)} %proj_piece.5), channel_id=1, source_target_pairs={{0,1},{1,0},{2,3},{3,2},{4,5},{5,4},{6,7},{7,6},{8,9},{9,8},{10,11... | collective-permute-start | bytes 983048 | tf_op jit(solution)/shard_map/ppermute | solution.py:1119
  52.1 11.1 %copy-start.26 = (bf16[256,256]{1,0:T(8,128)(2,1)S(1)}, bf16[256,256]{1,0:T(8,128)(2,1)}, u32[]{:S(2)}) copy-start(bf16[256,256]{1,0:T(8,128)(2,1)} %get-tuple-element.49.own_low_ref) | copy-start | bytes 393220
  52.1 16.2 %copy-start.11 = (bf16[256,1280]{1,0:T(8,128)(2,1)S(1)}, bf16[256,1280]{1,0:T(8,128)(2,1)}, u32[]{:S(2)}) copy-start(bf16[256,1280]{1,0:T(8,128)(2,1)} %go_ref.1) | copy-start | bytes 1966084
  52.1 16.8 %copy-start.15 = (f32[1280]{0:T(1024)S(1)}, f32[1280]{0:T(1024)}, u32[]{:S(2)}) copy-start(f32[1280]{0:T(1024)} %param.19) | copy-start | bytes 15364
  58.4 12.7 %all-to-all-start = ((bf16[8,16,768]{2,1,0:T(8,128)(2,1)}), bf16[8,16,768]{2,1,0:T(8,128)(2,1)S(1)}, u32[]{:S(2)}, u32[]{:S(2)}) async-start(bf16[8,16,768]{2,1,0:T(8,128)(2,1)} %get-tuple-element.51), calls=%async_computation | async-start | bytes 393216 | tf_op jit(solution)/shard_map/all_to_all | solution.py:1122
  63.2 5.0 %collective-permute-start.9 = (bf16[256,256]{1,0:T(8,128)(2,1)S(1)}, bf16[256,256]{1,0:T(8,128)(2,1)S(1)}, u32[]{:S(2)}, u32[]{:S(2)}) collective-permute-start(bf16[256,256]{1,0:T(8,128)(2,1)S(1)} %copy-done.26), channel_id=1, source_target_pairs={{0,1},{1,0},{2,3},{3,2},{4,5},{5,4},{6,7},{7,6},{8,9},{9,8},{10,11... | collective-permute-start | bytes 393224 | tf_op jit(solution)/shard_map/ppermute | solution.py:1119
  63.9 14.3 %collective-permute-start.10 = (bf16[256,256]{1,0:T(8,128)(2,1)S(1)}, bf16[256,256]{1,0:T(8,128)(2,1)S(1)}, u32[]{:S(2)}, u32[]{:S(2)}) collective-permute-start(bf16[256,256]{1,0:T(8,128)(2,1)S(1)} %copy-done.26), channel_id=1, source_target_pairs={{0,2},{2,0},{4,6},{6,4},{8,10},{10,8},{12,14},{14,12},{16,18},{18,... | collective-permute-start | bytes 393224 | tf_op jit(solution)/shard_map/ppermute | solution.py:1118
  68.3 9.9 %copy-start.27 = (bf16[256,256]{1,0:T(8,128)(2,1)}, bf16[256,256]{1,0:T(8,128)(2,1)S(1)}, u32[]{:S(2)}) copy-start(bf16[256,256]{1,0:T(8,128)(2,1)S(1)} %collective-permute-done.9.xr_low_ref) | copy-start | bytes 393220
  68.3 9.9 %collective-permute-start.11 = (bf16[256,256]{1,0:T(8,128)(2,1)S(1)}, bf16[256,256]{1,0:T(8,128)(2,1)S(1)}, u32[]{:S(2)}, u32[]{:S(2)}) collective-permute-start(bf16[256,256]{1,0:T(8,128)(2,1)S(1)} %collective-permute-done.9.xr_low_ref), channel_id=1, source_target_pairs={{0,2},{2,0},{4,6},{6,4},{8,10},{10,8},{12,14},{14,12},{16,18},{18,... | collective-permute-start | bytes 393224 | tf_op jit(solution)/shard_map/ppermute | solution.py:1118
  68.3 17.4 %collective-permute-start.12 = (bf16[256,640]{1,0:T(8,128)(2,1)S(1)}, bf16[256,640]{1,0:T(8,128)(2,1)S(1)}, u32[]{:S(2)}, u32[]{:S(2)}) collective-permute-start(bf16[256,640]{1,0:T(8,128)(2,1)S(1)} %constant_dynamic-slice_fusion), channel_id=1, source_target_pairs={{0,2},{2,0},{4,6},{6,4},{8,10},{10,8},{12,14},{14,12},{16,18},{18,... | collective-permute-start | bytes 983048 | tf_op jit(solution)/shard_map/ppermute | solution.py:1118
  73.8 12.1 %all-to-all-start.1 = ((bf16[8,16,640]{2,1,0:T(8,128)(2,1)}), bf16[8,16,640]{2,1,0:T(8,128)(2,1)S(1)}, u32[]{:S(2)}, u32[]{:S(2)}) async-start(bf16[8,16,640]{2,1,0:T(8,128)(2,1)} %chain.2), calls=%async_computation.1 | async-start | bytes 327680 | tf_op jit(solution)/shard_map/all_to_all | solution.py:1122
  94.5 13.5 %all-to-all-start.2 = ((bf16[8,16,640]{2,1,0:T(8,128)(2,1)}), bf16[8,16,640]{2,1,0:T(8,128)(2,1)S(1)}, u32[]{:S(2)}, u32[]{:S(2)}) async-start(bf16[8,16,640]{2,1,0:T(8,128)(2,1)} %get-tuple-element.56), calls=%async_computation.2 | async-start | bytes 327680 | tf_op jit(solution)/shard_map/all_to_all | solution.py:1122
  110.8 10.9 %all-to-all-start.3 = ((bf16[8,16,640]{2,1,0:T(8,128)(2,1)}), bf16[8,16,640]{2,1,0:T(8,128)(2,1)S(1)}, u32[]{:S(2)}, u32[]{:S(2)}) async-start(bf16[8,16,640]{2,1,0:T(8,128)(2,1)} %chain.3), calls=%async_computation.3 | async-start | bytes 327680 | tf_op jit(solution)/shard_map/all_to_all | solution.py:1122
  122.3 15.1 %copy-start.18 = (bf16[256,640]{1,0:T(8,128)(2,1)S(1)}, bf16[256,640]{1,0:T(8,128)(2,1)}, u32[]{:S(2)}) copy-start(bf16[256,640]{1,0:T(8,128)(2,1)} %get-tuple-element.55) | copy-start | bytes 983044
  122.3 23.2 %copy-start.3 = (bf16[256,640]{1,0:T(8,128)(2,1)S(1)}, bf16[256,640]{1,0:T(8,128)(2,1)}, u32[]{:S(2)}) copy-start(bf16[256,640]{1,0:T(8,128)(2,1)} %get-tuple-element.54) | copy-start | bytes 983044
  136.7 4.7 %collective-permute-start.20 = (f32[256,384]{1,0:T(8,128)}, f32[256,384]{1,0:T(8,128)S(1)}, u32[]{:S(2)}, u32[]{:S(2)}) collective-permute-start(f32[256,384]{1,0:T(8,128)} %get-tuple-element.73), channel_id=1, source_target_pairs={{0,2},{2,0},{4,6},{6,4},{8,10},{10,8},{12,14},{14,12},{16,18},{18,... | collective-permute-start | bytes 1179656 | tf_op jit(solution)/shard_map/ppermute | solution.py:1118
  137.4 7.5 %collective-permute-start.13 = (bf16[256,640]{1,0:T(8,128)(2,1)S(1)}, bf16[256,640]{1,0:T(8,128)(2,1)S(1)}, u32[]{:S(2)}, u32[]{:S(2)}) collective-permute-start(bf16[256,640]{1,0:T(8,128)(2,1)S(1)} %copy-done.18), channel_id=1, source_target_pairs={{0,2},{2,0},{4,6},{6,4},{8,10},{10,8},{12,14},{14,12},{16,18},{18,... | collective-permute-start | bytes 983048 | tf_op jit(solution)/shard_map/ppermute | solution.py:1118
  138.5 1.5 collective-permute-start.15
  139.3 18.5 %collective-permute-start.18 = (bf16[256,640]{1,0:T(8,128)(2,1)}, bf16[256,640]{1,0:T(8,128)(2,1)S(1)}, u32[]{:S(2)}, u32[]{:S(2)}) collective-permute-start(bf16[256,640]{1,0:T(8,128)(2,1)} %get-tuple-element.70), channel_id=1, source_target_pairs={{0,3},{1,2},{2,1},{3,0},{4,7},{5,6},{6,5},{7,4},{8,11},{9,10},{10,... | collective-permute-start | bytes 983048 | tf_op jit(solution)/shard_map/ppermute | solution.py:1120
  139.9 7.2 %collective-permute-start.14 = (bf16[256,640]{1,0:T(8,128)(2,1)}, bf16[256,640]{1,0:T(8,128)(2,1)S(1)}, u32[]{:S(2)}, u32[]{:S(2)}) collective-permute-start(bf16[256,640]{1,0:T(8,128)(2,1)} %get-tuple-element.70), channel_id=1, source_target_pairs={{0,2},{2,0},{4,6},{6,4},{8,10},{10,8},{12,14},{14,12},{16,18},{18,... | collective-permute-start | bytes 983048 | tf_op jit(solution)/shard_map/ppermute | solution.py:1118
  140.0 17.8 %collective-permute-start.17 = (bf16[256,640]{1,0:T(8,128)(2,1)}, bf16[256,640]{1,0:T(8,128)(2,1)S(1)}, u32[]{:S(2)}, u32[]{:S(2)}) collective-permute-start(bf16[256,640]{1,0:T(8,128)(2,1)} %get-tuple-element.69.mine_ref), channel_id=1, source_target_pairs={{0,1},{1,0},{2,3},{3,2},{4,5},{5,4},{6,7},{7,6},{8,9},{9,8},{10,11... | collective-permute-start | bytes 983048 | tf_op jit(solution)/shard_map/ppermute | solution.py:1119
  141.4 5.1 %collective-permute-start.16 = (bf16[32,896]{1,0:T(8,128)(2,1)S(1)}, bf16[32,896]{1,0:T(8,128)(2,1)S(1)}, u32[]{:S(2)}, u32[]{:S(2)}) collective-permute-start(bf16[32,896]{1,0:T(8,128)(2,1)S(1)} %constant_dynamic-update-slice_fusion), channel_id=1, source_target_pairs={{6,2},{10,6},{14,10},{18,14},{22,18},{26,22},{30,26},{7,3},{11,7},... | collective-permute-start | bytes 172040 | tf_op jit(solution)/shard_map/ppermute | solution.py:1188
  144.9 16.4 %collective-permute-start.21 = (bf16[256,384]{1,0:T(8,128)(2,1)}, bf16[256,384]{1,0:T(8,128)(2,1)S(1)}, u32[]{:S(2)}, u32[]{:S(2)}) collective-permute-start(bf16[256,384]{1,0:T(8,128)(2,1)} %get-tuple-element.75), channel_id=1, source_target_pairs={{0,1},{1,0},{2,3},{3,2},{4,5},{5,4},{6,7},{7,6},{8,9},{9,8},{10,11... | collective-permute-start | bytes 589832 | tf_op jit(solution)/shard_map/ppermute | solution.py:1119
  146.5 7.7 %collective-permute-start.19 = (bf16[32,896]{1,0:T(8,128)(2,1)S(1)}, bf16[32,896]{1,0:T(8,128)(2,1)S(1)}, u32[]{:S(2)}, u32[]{:S(2)}) collective-permute-start(bf16[32,896]{1,0:T(8,128)(2,1)S(1)} %constant_dynamic-update-slice_fusion), channel_id=1, source_target_pairs={{6,3},{7,2},{10,7},{11,6},{14,11},{15,10},{18,15},{19,14},{22,19},... | collective-permute-start | bytes 172040 | tf_op jit(solution)/shard_map/ppermute | solution.py:1189
  (25 other events, 48.7 us)
where the time goes:
time: 171 us; the launch traced here: 169 us
  Pallas kernels  93.3 us (55%)
  starting transfers between devices  34.8 us (20%)
  waiting for transfers between devices  25.3 us (15%)
  local copies, waits for them, and re-layouts  11.2 us (7%)
  other arithmetic  3.98 us (2%)
    pallas_call x4, Pallas kernels, proj_piece(): pl.pallas_call(piece_kernel, grid_spec=pltpu.PrefetchScalarGridSpec(num_s...  19.4 us
    all_to_all x4, starting transfers between devices, by_chips(): lax.all_to_all(a, 'ctx', 0, 0, axis_index_groups=groups)  18.8 us
    ppermute x6, waiting for transfers between devices, by_chips(): by_x = lambda a: lax.ppermute(a, 'fsdp', pair)  14.8 us
    pallas_call x1, Pallas kernels, grads_of(): pl.pallas_call(functools.partial(grads_kernel, doc_starts.shape[0], heads...  14.4 us
    all_to_all x4, waiting for transfers between devices, by_chips(): lax.all_to_all(a, 'ctx', 0, 0, axis_index_groups=groups)  10.4 us
    unnamed x64, local copies, waits for them, and re-layouts  9.65 us
    pallas_call x1, Pallas kernels, outputs_of(): pl.pallas_call(functools.partial(out_kernel, heads), grid_spec=pltpu.Pref...  8.01 us
    pallas_call x1, Pallas kernels, last_half(): pl.pallas_call(functools.partial(last_kernel, all_heads // 2), grid_spec=...  7.46 us
  transfers between devices with their start and end apart: 26, of which 8 were waited for; matrix products, arithmetic and copies ran while one was open for 4% of the time, Pallas kernels for 33%

commit v1 on v0

--- a/solution.py
+++ b/solution.py
@@ -241,12 +241,34 @@
     return v * sig, sig * (1.0 + v * (1.0 - sig))
 
 
-def small_proj_kernel(tok_ref, bcw_ref, dtw_ref, out_ref, low_ref):
+def fetch(src, dst, sem):
+    copy = pltpu.make_async_copy(src, dst, sem)
+    copy.start()
+    return copy
+
+
+def columns(w_ref, block, width):
+    return w_ref.at[:, pl.ds(pl.multiple_of(block * width, LANES), width)]
+
+
+def lead_kernel(
+    meta_ref, tok_hbm, w_hbm, bcw_hbm, dtw_hbm, piece_ref, out_ref, low_ref, tok_ref, w_ref, bcw_ref,
+    dtw_ref, sems,
+):
+    width = w_ref.shape[1]
+    get_tok = fetch(tok_hbm, tok_ref, sems.at[0])
+    get_w = fetch(columns(w_hbm, meta_ref[0], width), w_ref, sems.at[1])
+    get_bcw = fetch(bcw_hbm, bcw_ref, sems.at[2])
+    get_dtw = fetch(dtw_hbm, dtw_ref, sems.at[3])
+    get_tok.wait()
+    get_w.wait()
+    piece_ref[...] = mm(tok_ref[...], w_ref[...]).astype(BF)
+    get_bcw.wait()
+    get_dtw.wait()
     states = bcw_ref.shape[1]
-    heads = dtw_ref.shape[1]
-    tok = tok_ref[...]
-    out_ref[:, :states], low_ref[...] = split2(mm(tok, bcw_ref[...]))
-    hi, lo = split2(mm(tok, dtw_ref[...]))
+    heads = dtw_ref.shape[0]
+    out_ref[:, :states], low_ref[...] = split2(mm(tok_ref[...], bcw_ref[...]))
+    hi, lo = split2(mm_nt(tok_ref[...], dtw_ref[...]))
     shape = (heads, LANES)
     row, col = iota(shape, 0), iota(shape, 1)
     first = jnp.where(row == col, 1.0, 0.0).astype(BF)
@@ -254,79 +276,90 @@
     out_ref[:, states:] = (mm(hi, first) + mm(lo, second)).astype(BF)
 
 
-def small_proj(tokens, bc_weight, dt_weight):
-    rows = tokens.shape[0]
+def lead_proj(block, tokens, x_weight, bc_weight, dt_rows, width):
+    rows, depth = tokens.shape
+    states = bc_weight.shape[1]
+    hbm = pl.BlockSpec(memory_space=pl.ANY)
+    vm = pl.BlockSpec(memory_space=pltpu.VMEM)
     return pl.pallas_call(
-        small_proj_kernel,
+        lead_kernel,
+        grid_spec=pltpu.PrefetchScalarGridSpec(
+            num_scalar_prefetch=1,
+            grid=(),
+            in_specs=[hbm] * 4,
+            out_specs=[vm] * 3,
+            scratch_shapes=[
+                pltpu.VMEM((rows, depth), BF),
+                pltpu.VMEM((depth, width), BF),
+                pltpu.VMEM((depth, states), BF),
+                pltpu.VMEM(dt_rows.shape, BF),
+                pltpu.SemaphoreType.DMA((4,)),
+            ],
+        ),
         out_shape=[
-            jax.ShapeDtypeStruct((rows, bc_weight.shape[1] + LANES), BF),
-            jax.ShapeDtypeStruct((rows, bc_weight.shape[1]), BF),
+            jax.ShapeDtypeStruct((rows, width), BF),
+            jax.ShapeDtypeStruct((rows, states + LANES), BF),
+            jax.ShapeDtypeStruct((rows, states), BF),
         ],
         compiler_params=params(),
-        cost_estimate=cost(3e8, 2e6),
-        name="small_proj",
-    )(tokens, bc_weight, dt_weight)
-
-
-def piece_kernel(meta_ref, tok_ref, w_ref, out_ref):
-    out_ref[...] = mm(tok_ref[...], w_ref[...]).astype(BF)
-
-
-def proj_piece(tokens, x_weight, block, width):
+        cost_estimate=cost(2 * rows * depth * width, 3e6),
+        name="lead_proj",
+    )(block, tokens, x_weight, bc_weight, dt_rows)
+
+
+def rest_kernel(
+    meta_ref, tok_hbm, w_hbm, bcw_hbm, ra_hbm, rb_hbm, peer_ref, core_ref, mine_ref, own_ref, send_ref,
+    tok_ref, w_ref, bcw_ref, ra_ref, rb_ref, sems,
+):
+    width = w_ref.shape[2]
+    get_tok = fetch(tok_hbm, tok_ref, sems.at[0])
+    get_w = [fetch(columns(w_hbm, meta_ref[i], width), w_ref.at[i], sems.at[1 + i]) for i in range(3)]
+    get_bcw = fetch(bcw_hbm, bcw_ref, sems.at[4])
+    get_ra = fetch(ra_hbm, ra_ref, sems.at[5])
+    get_rb = fetch(rb_hbm, rb_ref, sems.at[6])
+    get_tok.wait()
+    for i, ref in enumerate((peer_ref, core_ref, mine_ref)):
+        get_w[i].wait()
+        ref[...] = mm(tok_ref[...], w_ref[i]).astype(BF)
+    get_bcw.wait()
+    get_ra.wait()
+    get_rb.wait()
+    rim = ra_ref[...] + rb_ref[...]
+    shared = mm(rim, bcw_ref[...]).astype(BF)
+    own_ref[:, :width] = mm(rim, w_ref[2]).astype(BF)
+    own_ref[:, width:] = shared
+    send_ref[:, :width] = mm(rim, w_ref[0]).astype(BF)
+    send_ref[:, width:] = shared
+
+
+def rest_proj(blocks, tokens, x_weight, bc_weight, ra, rb, width):
     rows, depth = tokens.shape
-    tiles = width // LANES
+    states = bc_weight.shape[1]
+    hbm = pl.BlockSpec(memory_space=pl.ANY)
+    vm = pl.BlockSpec(memory_space=pltpu.VMEM)
+    piece = jax.ShapeDtypeStruct((rows, width), BF)
+    rim = jax.ShapeDtypeStruct((ra.shape[0], width + states), BF)
     return pl.pallas_call(
-        piece_kernel,
+        rest_kernel,
         grid_spec=pltpu.PrefetchScalarGridSpec(
             num_scalar_prefetch=1,
-            grid=(tiles,),
-            in_specs=[
-                pl.BlockSpec((rows, depth), lambda i, m: (0, 0)),
-                pl.BlockSpec((depth, LANES), lambda i, m: (0, m[0] * tiles + i)),
+            grid=(),
+            in_specs=[hbm] * 5,
+            out_specs=[vm] * 5,
+            scratch_shapes=[
+                pltpu.VMEM((rows, depth), BF),
+                pltpu.VMEM((3, depth, width), BF),
+                pltpu.VMEM((depth, states), BF),
+                pltpu.VMEM(ra.shape, BF),
+                pltpu.VMEM(rb.shape, BF),
+                pltpu.SemaphoreType.DMA((7,)),
             ],
-            out_specs=pl.BlockSpec((rows, LANES), lambda i, m: (0, i)),
         ),
-        out_shape=jax.ShapeDtypeStruct((rows, width), BF),
+        out_shape=[piece, piece, piece, rim, rim],
         compiler_params=params(),
-        cost_estimate=cost(2 * rows * depth * width, 2 * depth * width),
-        name="proj_piece",
-    )(block, tokens, x_weight)
-
-
-def rim_kernel(meta_ref, ra_ref, rb_ref, own_w_ref, peer_w_ref, bcw_ref, own_ref, send_ref):
-    width = own_w_ref.shape[1]
-    rows = ra_ref[...] + rb_ref[...]
-    shared = mm(rows, bcw_ref[...]).astype(BF)
-    own_ref[:, :width] = mm(rows, own_w_ref[...]).astype(BF)
-    own_ref[:, width:] = shared
-    send_ref[:, :width] = mm(rows, peer_w_ref[...]).astype(BF)
-    send_ref[:, width:] = shared
-
-
-def rim_proj(ra, rb, x_weight, bc_weight, blocks, width):
-    rows, depth = ra.shape
-    states = bc_weight.shape[1]
-    out = jax.ShapeDtypeStruct((rows, width + states), BF)
-    full = lambda shape: pl.BlockSpec(shape, lambda i, m: (0, 0))
-    return pl.pallas_call(
-        rim_kernel,
-        grid_spec=pltpu.PrefetchScalarGridSpec(
-            num_scalar_prefetch=1,
-            grid=(1,),
-            in_specs=[
-                full((rows, depth)),
-                full((rows, depth)),
-                pl.BlockSpec((depth, width), lambda i, m: (0, m[0])),
-                pl.BlockSpec((depth, width), lambda i, m: (0, m[1])),
-                full((depth, states)),
-            ],
-            out_specs=[full((rows, width + states)), full((rows, width + states))],
-        ),
-        out_shape=[out, out],
-        compiler_params=params(),
-        cost_estimate=cost(4 * rows * depth * width, 4 * depth * width),
-        name="rim_proj",
-    )(blocks, ra, rb, x_weight, x_weight, bc_weight)
+        cost_estimate=cost(6 * rows * depth * width, 6e6),
+        name="rest_proj",
+    )(blocks, tokens, x_weight, bc_weight, ra, rb)
 
 
 def conv_masks(docs_ref, count, base, rows, lanes):
@@ -654,7 +687,7 @@
     return pl.pallas_call(
         functools.partial(chain_kernel, heads, reverse),
         out_shape=jax.ShapeDtypeStruct((chips, piece, width), BF),
-        compiler_params=params(),
+        compiler_params=params(16),
         cost_estimate=cost(1e8, 1e6),
         name="chain",
     )(recv, keeps)
@@ -676,10 +709,12 @@
     state = state_ref[...]
     keep0 = keep_row(keep_ref[0], heads, width)[0:1, :]
     both_ref[0] = state
-    both_ref[1] = (state.astype(F32) * keep0 + loc_ref[0]).astype(BF)
+    middle = state.astype(F32) * keep0 + loc_ref[0]
+    both_ref[1] = middle.astype(BF)
+    both_ref[2] = (middle * keep_row(keep_ref[1], heads, width)[0:1, :] + loc_ref[1]).astype(BF)
     wide = spread(heads, width)
     gather = gather_heads(width)
-    tile = 128
+    tile = 256
     per = rows // tile
 
     def one(step, _):
@@ -728,7 +763,7 @@
         jax.ShapeDtypeStruct((total, 2 * width), BF),
         jax.ShapeDtypeStruct((total, width), BF),
         jax.ShapeDtypeStruct((total, LANES), F32),
-        jax.ShapeDtypeStruct((2, states, width), BF),
+        jax.ShapeDtypeStruct((3, states, width), BF),
         jax.ShapeDtypeStruct((states, width), F32),
         jax.ShapeDtypeStruct((chips, states // chips, width), BF),
     ]
@@ -753,8 +788,9 @@
 
 def within_back_kernel(
     docs, heads, meta_ref, docs_ref, dy_ref, edy_ref, both_ref, xd_ref, bact_ref, ramp_ref,
-    rampt_ref, cbt_ref, dxd_ref, dbc_ref, gate_ref, sum_ref,
+    rampt_ref, cbt_ref, act_ref, slope_ref, near_ref, q_ref, dbc_ref, gate_ref, sum_ref,
 ):
+    gather = gather_heads(xd_ref.shape[1])
     chip = meta_ref[2]
     total, width = xd_ref.shape
     rows = total // 2
@@ -769,6 +805,7 @@
         start = doc_start_of(pos, docs_ref, docs)
         gate_ref[...] = jnp.where((src <= pos) & (src >= start), 0.0, NEG)
         sum_ref[...] = jnp.zeros(square, F32)
+        q = jnp.zeros((rows, LANES), F32)
         for pair in range(heads // 2):
             cols = slice(pair * LANES, (pair + 1) * LANES)
             xd = xd_ref[sl, cols]
@@ -783,13 +820,16 @@
                 decay = jnp.exp2(gap + gate_ref[...])
                 found.append(mm((decay * cbt_ref[part]).astype(BF), dy))
                 sum_ref[...] += mm_nt(only, dy_both) * decay
-            dxd_ref[sl, cols] = jnp.where(lane < HEAD_DIM, found[0], found[1])
+            dxd = jnp.where(lane < HEAD_DIM, found[0], found[1])
+            near_ref[sl, cols] = (dxd * slope_ref[sl, cols].astype(F32)).astype(BF)
+            q = q + mm((dxd * act_ref[sl, cols].astype(F32)).astype(BF), gather[cols, :])
+        q_ref[sl, :] = q
         grad, low = split2(sum_ref[...])
         dbc_ref[sl, :states] = mm(grad, c) + mm(low, c)
         dbc_ref[sl, states:] = mm_tn(grad, b) + mm_tn(low, b) + mm_nt(edy_ref[sl, :], both_ref[part])
 
 
-def within_back(meta, doc_starts, dy, edy, both, xd, bact, ramp, rampt, cbt, heads):
+def within_back(meta, doc_starts, dy, edy, both, xd, bact, ramp, rampt, cbt, act, slope, heads):
     total, width = xd.shape
     rows = total // 2
     vm = pl.BlockSpec(memory_space=pltpu.VMEM)
@@ -798,139 +838,153 @@
         grid_spec=pltpu.PrefetchScalarGridSpec(
             num_scalar_prefetch=2,
             grid=(),
-            in_specs=[vm] * 8,
-            out_specs=[vm] * 2,
+            in_specs=[vm] * 10,
+            out_specs=[vm] * 3,
             scratch_shapes=[pltpu.VMEM((rows, rows), F32)] * 2,
         ),
         out_shape=[
-            jax.ShapeDtypeStruct((total, width), F32),
+            jax.ShapeDtypeStruct((total, width), BF),
+            jax.ShapeDtypeStruct((total, LANES), F32),
             jax.ShapeDtypeStruct((total, bact.shape[1]), F32),
         ],
         compiler_params=params(),
         cost_estimate=cost(1e10, 6e6),
         name="within_back",
-    )(meta, doc_starts, dy, edy, both, xd, bact, ramp, rampt, cbt)
+    )(meta, doc_starts, dy, edy, both, xd, bact, ramp, rampt, cbt, act, slope)
+
+
+def slopes_kernel(pre_ref, dpk_ref, wpk_ref, act_ref, far_ref, wx_ref, slope_ref, reach_ref):
+    total, width = pre_ref.shape
+    wide = spread(width // HEAD_DIM, width)
+    tile = total // 2
+    for at in range(0, total, tile):
+        sl = slice(at, at + tile)
+        for lane in range(0, width, LANES):
+            ls = slice(lane, lane + LANES)
+            w = mm(wpk_ref[sl, :], wide[:, ls])
+            step = mm(dpk_ref[sl, :], wide[:, ls])
+            act, slope = silu_parts(pre_ref[sl, ls])
+            slope = slope * step
+            act_ref[sl, ls] = act.astype(BF)
+            far_ref[sl, ls] = (act * w).astype(BF)
+            wx_ref[sl, ls] = (act * step * w).astype(BF)
+            slope_ref[sl, ls] = slope.astype(BF)
+            reach_ref[sl, ls] = (slope * w).astype(BF)
+
+
+def slopes_of(pre, dpk, wpk):
+    return pl.pallas_call(
+        slopes_kernel,
+        out_shape=[jax.ShapeDtypeStruct(pre.shape, BF)] * 5,
+        compiler_params=params(),
+        cost_estimate=cost(2e9, 4e6),
+        name="slopes_of",
+    )(pre, dpk, wpk)
+
+
+def back_masks(docs_ref, docs, pos):
+    return [jnp.where(pos >= doc_start_of(pos + j, docs_ref, docs), 1.0, 0.0) for j in range(1, 4)]
+
+
+def conv_back(src_ref, taps, at, count, ls, masks):
+    window = src_ref[pl.ds(at, count + 8), ls]
+    value = window[:count] * taps[0:1, ls]
+    for j in range(1, 4):
+        value = value + window[j : j + count] * taps[j : j + 1, ls] * masks[j - 1]
+    return value
 
 
 def grads_kernel(
-    docs, heads, meta_ref, docs_ref, adj_ref, late_ref, loc_ref, both_ref, dxd_ref, dbc_ref,
-    pre_ref, bpre_ref, xd_ref, bact_ref, delta_ref, sig_ref, dpk_ref, wpk_ref, keep_ref, dot_ref,
-    prm_ref, taps_ref, taps_bc_ref, own_ref, other_ref, bc_own_ref, bc_other_ref, rim_ref,
-    adj2_ref, gx_ref, gb_ref, q_ref, wx_ref, all_ref, bc_all_ref,
+    docs, heads, meta_ref, docs_ref, adj_ref, late_ref, keep_ref, both_ref, b_ref, near_ref, far_ref,
+    wx_ref, reach_ref, q_ref, dbc_ref, bpre_ref, delta_ref, sig_ref, dot_ref, prm_ref, taps_bc_ref,
+    taps_ref, own_ref, other_ref, bc_own_ref, bc_other_ref, rim_ref, adj2_ref, gx_ref, gb_ref, all_ref,
+    bc_all_ref,
 ):
     k, chip = meta_ref[0], meta_ref[2]
-    total, width = dxd_ref.shape
+    total, width = near_ref.shape
     rows = total // 2
-    states2 = bact_ref.shape[1]
-    states = states2 // 2
+    states = b_ref.shape[1]
+    states2 = 2 * states
     base = chip * total
-    mine = pl.multiple_of(k * rows, rows)
-    other = pl.multiple_of((1 - k) * rows, rows)
-    keep1 = keep_row(keep_ref[1], heads, width)[0:1, :]
     adj = adj_ref[...].astype(F32)
-    early = adj * keep1 + late_ref[...]
+    early = adj * keep_row(keep_ref[1], heads, width)[0:1, :] + late_ref[...]
     adj2_ref[0] = early.astype(BF)
     adj2_ref[1] = adj_ref[...]
-    middle = both_ref[1].astype(F32)
-    final = middle * keep1 + loc_ref[1]
     gather = gather_heads(width)
     ends = [
-        over_heads(jnp.sum(a * s, axis=0, keepdims=True) + jnp.zeros((8, width), F32), gather)
-        for a, s in ((early, middle), (adj, final))
+        over_heads(
+            jnp.sum(a * both_ref[i].astype(F32), axis=0, keepdims=True) + jnp.zeros((8, width), F32),
+            gather,
+        )
+        for i, a in ((1, early), (2, adj))
     ]
-    wide = spread(heads, width)
-    tile = 64
-    per = rows // tile
-    gx_ref[0:8, :] = jnp.zeros((8, width), F32)
-    gx_ref[total + 8 :, :] = jnp.zeros((8, width), F32)
-    gb_ref[0:8, :] = jnp.zeros((8, states2), F32)
-    gb_ref[total + 8 :, :] = jnp.zeros((8, states2), F32)
-
-    def one(step, _):
-        at = pl.multiple_of(step * tile, tile)
-        sl = pl.ds(at, tile)
-        part = step // per
-        b = bact_ref[sl, :states]
-        q = jnp.zeros((tile, LANES), F32)
-        for lane in range(0, width, LANES):
-            ls = slice(lane, lane + LANES)
-            far = mm(b, adj2_ref[part, :, ls])
-            w = mm(wpk_ref[sl, :], wide[:, ls])
-            dxd = dxd_ref[sl, ls] + far * w
-            act, slope = silu_parts(pre_ref[sl, ls])
-            q = q + over_heads(act * dxd, gather[ls, :])
-            gx_ref[pl.ds(pl.multiple_of(at + 8, 8), tile), ls] = dxd * mm(dpk_ref[sl, :], wide[:, ls]) * slope
-            wx_ref[sl, ls] = (xd_ref[sl, ls].astype(F32) * w).astype(BF)
-        q_ref[sl, :] = q
-        return 0
-
-    lax.fori_loop(0, total // tile, one, 0)
+    for ref, lanes in ((gx_ref, width), (gb_ref, states2)):
+        ref[0:8, :] = jnp.zeros((8, lanes), F32)
+        ref[total + 8 :, :] = jnp.zeros((8, lanes), F32)
     square = (rows, rows)
     upper = jnp.where(iota(square, 0) <= iota(square, 1), 1.0, 0.0).astype(BF)
     rate = prm_ref[1:2, :]
     row = iota((rows, LANES), 0)
     for part in range(2):
         sl = slice(part * rows, (part + 1) * rows)
+        inside = slice(8 + part * rows, 8 + (part + 1) * rows)
         q = q_ref[sl, :]
+        for lane in range(0, width, LANES):
+            ls = slice(lane, lane + LANES)
+            back = mm(b_ref[sl, :], adj2_ref[part, :, ls])
+            gx_ref[inside, ls] = near_ref[sl, ls].astype(F32) + back * reach_ref[sl, ls].astype(F32)
+            q = q + mm((back * far_ref[sl, ls].astype(F32)).astype(BF), gather[ls, :])
         ramp_grad = dot_ref[sl, :] - delta_ref[sl, :] * q
         ramp_grad = ramp_grad + jnp.where(row == rows - 1, ends[part][0:1, :], 0.0)
-        hi, mid = split2(ramp_grad)
-        low = (ramp_grad - hi.astype(F32) - mid.astype(F32)).astype(BF)
-        later = mm(upper, hi) + mm(upper, mid) + mm(upper, low)
-        bc_all_ref[sl, states2:] = ((q - rate * later) * sig_ref[sl, :])
+        hi, lo = split2(ramp_grad)
+        later = mm(upper, hi) + mm(upper, lo)
+        bc_all_ref[sl, states2:] = (q - rate * later) * sig_ref[sl, :]
         back = mm_nt(wx_ref[sl, :], adj2_ref[part])
         for lane, grad in ((0, dbc_ref[sl, :states] + back), (states, dbc_ref[sl, states:])):
             ls = slice(lane, lane + states)
             _, slope = silu_parts(bpre_ref[sl, ls])
-            gb_ref[8 + part * rows : 8 + (part + 1) * rows, ls] = grad * slope
-
-    def spill(src_ref, taps, at, count, ls):
-        window = src_ref[pl.ds(at, count + 8), ls]
-        value = window[:count] * taps[0:1, ls]
-        pos = base + at - 8 + iota((count, LANES), 0)
-        for j in range(1, 4):
-            start = doc_start_of(pos + j, docs_ref, docs)
-            mask = jnp.where(pos >= start, 1.0, 0.0)
-            value = value + window[j : j + count] * taps[j : j + 1, ls] * mask
-        return value
+            gb_ref[inside, ls] = grad * slope
+    tile = 64
 
     def back(step, _):
         at = pl.multiple_of(step * tile, tile)
-        sl = pl.ds(at, tile)
+        begin = pl.multiple_of(at + 8, 8)
+        masks = back_masks(docs_ref, docs, base + at + iota((tile, LANES), 0))
         for lane in range(0, width, LANES):
             ls = slice(lane, lane + LANES)
-            all_ref[sl, ls] = spill(gx_ref, taps_ref, pl.multiple_of(at + 8, 8), tile, ls).astype(BF)
+            all_ref[pl.ds(at, tile), ls] = conv_back(gx_ref, taps_ref, begin, tile, ls, masks).astype(BF)
         for lane in range(0, states2, LANES):
             ls = slice(lane, lane + LANES)
-            bc_all_ref[sl, ls] = spill(gb_ref, taps_bc_ref, pl.multiple_of(at + 8, 8), tile, ls)
+            bc_all_ref[pl.ds(at, tile), ls] = conv_back(gb_ref, taps_bc_ref, begin, tile, ls, masks)
         return 0
 
     lax.fori_loop(0, total // tile, back, 0)
-    rim_ref[...] = jnp.zeros(rim_ref.shape, BF)
     pad = jnp.zeros((8, LANES), F32)
-    for lane in range(0, width, LANES):
-        ls = slice(lane, lane + LANES)
-        value = jnp.concatenate([pad, spill(gx_ref, taps_ref, 0, 8, ls)], axis=0)
-        rim_ref[:, ls] = value.astype(BF)
-    for lane in range(0, states2, LANES):
-        ls = slice(lane, lane + LANES)
-        value = jnp.concatenate([pad, spill(gb_ref, taps_bc_ref, 0, 8, ls)], axis=0)
-        rim_ref[:, width + lane : width + lane + LANES] = value.astype(BF)
-    own_ref[...] = all_ref[pl.ds(mine, rows), :]
-    other_ref[...] = all_ref[pl.ds(other, rows), :]
-    bc_own_ref[...] = bc_all_ref[pl.ds(mine, rows), :]
-    bc_other_ref[...] = bc_all_ref[pl.ds(other, rows), :]
+    masks = back_masks(docs_ref, docs, base - 8 + iota((8, LANES), 0))
+    for src, taps, first, lanes in ((gx_ref, taps_ref, 0, width), (gb_ref, taps_bc_ref, width, states2)):
+        for lane in range(0, lanes, LANES):
+            value = conv_back(src, taps, 0, 8, slice(lane, lane + LANES), masks)
+            value = jnp.concatenate([pad, value], axis=0)
+            rim_ref[:, first + lane : first + lane + LANES] = value.astype(BF)
+    mine = pl.ds(pl.multiple_of(k * rows, rows), rows)
+    other = pl.ds(pl.multiple_of((1 - k) * rows, rows), rows)
+    own_ref[...] = all_ref[mine, :]
+    other_ref[...] = all_ref[other, :]
+    bc_own_ref[...] = bc_all_ref[mine, :]
+    bc_other_ref[...] = bc_all_ref[other, :]
 
 
 def grads_of(
-    meta, doc_starts, adj, late, loc, both, dxd, dbc, pre, bpre, xd, bact, delta, sig, dpk, wpk,
-    keep, dots, prm, taps, taps_bc, heads,
+    meta, doc_starts, adj, late, keep, both, bact, near, far, wx, reach, q, dbc, bpre, delta, sig, dots,
+    prm, taps_bc, taps, heads,
 ):
-    total, width = dxd.shape
+    total, width = near.shape
     rows, states2 = total // 2, bact.shape[1]
     states = states2 // 2
     whole = lambda shape: pl.BlockSpec(shape, lambda i, m, d: (0,) * len(shape))
     half = pl.BlockSpec((taps.shape[0], width), lambda i, m, d: (0, m[0]))
+    first = pl.BlockSpec((total, states), lambda i, m, d: (0, 0))
+    ins = [near, far, wx, reach, q, dbc, bpre, delta, sig, dots, prm, taps_bc]
     outs = [
         jax.ShapeDtypeStruct((rows, width), BF),
         jax.ShapeDtypeStruct((rows, width), BF),
@@ -938,20 +992,20 @@
         jax.ShapeDtypeStruct((rows, states2 + LANES), F32),
         jax.ShapeDtypeStruct((16, width + states2), BF),
     ]
-    ins = [adj, late, loc, both, dxd, dbc, pre, bpre, xd, bact, delta, sig, dpk, wpk, keep, dots, prm]
     return pl.pallas_call(
         functools.partial(grads_kernel, doc_starts.shape[0], heads),
         grid_spec=pltpu.PrefetchScalarGridSpec(
             num_scalar_prefetch=2,
             grid=(1,),
-            in_specs=[whole(a.shape) for a in ins] + [half, whole(taps_bc.shape)],
+            in_specs=[whole(a.shape) for a in (adj, late, keep, both)]
+            + [first]
+            + [whole(a.shape) for a in ins]
+            + [half],
             out_specs=[whole(o.shape) for o in outs],
             scratch_shapes=[
                 pltpu.VMEM((2, states, width), BF),
                 pltpu.VMEM((total + 16, width), F32),
                 pltpu.VMEM((total + 16, states2), F32),
-                pltpu.VMEM((total, LANES), F32),
-                pltpu.VMEM((total, width), BF),
                 pltpu.VMEM((total, width), BF),
                 pltpu.VMEM((total, states2 + LANES), F32),
             ],
@@ -960,7 +1014,7 @@
         compiler_params=params(),
         cost_estimate=cost(4e9, 8e6),
         name="grads_of",
-    )(meta, doc_starts, *ins, taps, taps_bc)
+    )(meta, doc_starts, adj, late, keep, both, bact, *ins, taps)
 
 
 def join_kernel(heads, meta_ref, own_ref, recv_ref, out_ref, send_ref):
@@ -986,7 +1040,7 @@
             num_scalar_prefetch=1, grid=(), in_specs=[vm] * 2, out_specs=[vm] * 2
         ),
         out_shape=[jax.ShapeDtypeStruct(own.shape, F32), jax.ShapeDtypeStruct(own.shape, BF)],
-        compiler_params=params(),
+        compiler_params=params(16),
         cost_estimate=cost(1e8, 1e6),
         name="join",
     )(meta, own, recv)
@@ -1021,7 +1075,7 @@
             out_specs=pl.BlockSpec((rows, tile), lambda i, m: (0, i)),
         ),
         out_shape=jax.ShapeDtypeStruct((rows, depth), F32),
-        compiler_params=params(),
+        compiler_params=params(16),
         cost_estimate=cost(2e9, 4e6),
         name="first_half",
     )(blocks, mine, other, rim, x_weight, x_weight)
@@ -1033,7 +1087,7 @@
 ):
     rows, width = mine_ref.shape
     states2 = bcw_ref.shape[1]
-    all_heads = dtw_ref.shape[1]
+    all_heads = dtw_ref.shape[0]
 
     @pl.when(pl.program_id(0) == 0)
     def _():
@@ -1060,14 +1114,14 @@
     total = part_ref[...] + mm_nt(left_ref[...], w_mine_ref[...])
     total = total + mm_nt(right_ref[...], w_other_ref[...])
     bcw = bcw_ref[...]
-    total = total + mm_nt(bc_ref[...], jnp.concatenate([bcw, bcw], axis=1)) + mm_nt(dt_ref[...], dtw_ref[...])
+    total = total + mm_nt(bc_ref[...], jnp.concatenate([bcw, bcw], axis=1)) + mm(dt_ref[...], dtw_ref[...])
     out_ref[...] = total.astype(BF)
 
 
-def last_half(blocks, part, mine, other, rim, rim0, bc_own, bc_recv, x_weight, bc_weight, dt_weight, tile):
+def last_half(blocks, part, mine, other, rim, rim0, bc_own, bc_recv, x_weight, bc_weight, dt_rows, tile):
     rows, width = mine.shape
     depth = x_weight.shape[0]
-    states2, all_heads = bc_weight.shape[1], dt_weight.shape[1]
+    states2, all_heads = bc_weight.shape[1], dt_rows.shape[0]
     whole = lambda a: pl.BlockSpec(a.shape, lambda i, m: (0, 0))
     return pl.pallas_call(
         functools.partial(last_kernel, all_heads // 2),
@@ -1080,7 +1134,7 @@
                 pl.BlockSpec((tile, width), lambda i, m: (i, m[0])),
                 pl.BlockSpec((tile, width), lambda i, m: (i, m[1])),
                 pl.BlockSpec((tile, states2), lambda i, m: (i, 0)),
-                pl.BlockSpec((tile, all_heads), lambda i, m: (i, 0)),
+                pl.BlockSpec((all_heads, tile), lambda i, m: (0, i)),
             ],
             out_specs=pl.BlockSpec((rows, tile), lambda i, m: (0, i)),
             scratch_shapes=[
@@ -1091,10 +1145,10 @@
             ],
         ),
         out_shape=jax.ShapeDtypeStruct((rows, depth), BF),
-        compiler_params=params(),
+        compiler_params=params(16),
         cost_estimate=cost(2e9, 4e6),
         name="last_half",
-    )(blocks, part, mine, other, rim, rim0, bc_own, bc_recv, x_weight, x_weight, bc_weight, dt_weight)
+    )(blocks, part, mine, other, rim, rim0, bc_own, bc_recv, x_weight, x_weight, bc_weight, dt_rows)
 
 
 def by_chips(
@@ -1128,18 +1182,17 @@
     ra = lax.ppermute(tail, "ctx", [(2 * i - 1, 2 * i) for i in range(1, chips)])
     rb = lax.ppermute(tail, "ctx", [(2 * i - 1, 2 * i + 1) for i in range(1, chips)])
 
-    small, low = small_proj(tokens, bc_weight, dt_weight)
+    dt_rows = dt_weight.T
+    to_cross, small, low = lead_proj(
+        column_block(1 - x, 1 - k), tokens, x_weight, bc_weight, dt_rows, width
+    )
+    from_cross = by_both(to_cross)
     small_x = by_x(small)
-    to_cross = proj_piece(tokens, x_weight, column_block(1 - x, 1 - k), width)
-    from_cross = by_both(to_cross)
-    to_x = proj_piece(tokens, x_weight, column_block(1 - x, k), width)
+    to_x, to_core, mine, rim_own, rim_send = rest_proj(
+        jnp.stack([(1 - x) * 2 + k, x * 2 + 1 - k, x * 2 + k]), tokens, x_weight, bc_weight, ra, rb, width
+    )
     from_x = by_x(to_x)
-    to_core = proj_piece(tokens, x_weight, column_block(x, 1 - k), width)
     from_core = by_core(to_core)
-    mine = proj_piece(tokens, x_weight, column_block(x, k), width)
-    rim_own, rim_send = rim_proj(
-        ra, rb, x_weight, bc_weight, jnp.stack([x * 2 + k, (1 - x) * 2 + k]), width
-    )
     rim_recv = by_x(rim_send)
     small_core = by_core(small)
     small_cross = by_core(small_x)
@@ -1167,8 +1220,11 @@
     mix_own, mix_send, dy, edy, dots, both, late, back = outputs_of(
         meta, y, state, loc, bact, epk, keep, grad_out, go_recv, norm_gain[None, :], heads, chips
     )
+    act, far, wx, slope, reach = slopes_of(pre, dpk, wpk)
     backs = exchange(back)
-    dxd, dbc = within_back(meta, doc_starts, dy, edy, both, xd, bact, ramp, rampt, cbt, heads)
+    near, q, dbc = within_back(
+        meta, doc_starts, dy, edy, both, xd, bact, ramp, rampt, cbt, act, slope, heads
+    )
     mix_recv = by_core(mix_send)
     mixed = jnp.where(
         k == 0,
@@ -1177,8 +1233,8 @@
     )
     adj = exchange(chain(backs, keeps, heads, width, True)).reshape(STATE, width)
     g_mine, g_other, bc_mine, bc_other, rim = grads_of(
-        meta, doc_starts, adj, late, loc, both, dxd, dbc, pre, bpre, xd, bact, delta, sig, dpk, wpk,
-        keep, dots, prm, conv_inner, conv_shared, heads,
+        meta, doc_starts, adj, late, keep, both, bact, near, far, wx, reach, q, dbc, bpre, delta, sig,
+        dots, prm, conv_shared, conv_inner, heads,
     )
     g_x = by_x(g_mine)
     g_cross = by_both(g_other)
@@ -1192,11 +1248,11 @@
     bc_chip, bc_send = join(meta, bc_mine, by_core(bc_other), heads)
     bc_recv = by_x(bc_send)
     part = first_half(
-        jnp.stack([x * 2 + k, x * 2 + 1 - k]), g_mine, g_core, rim0, x_weight, 256
+        jnp.stack([x * 2 + k, x * 2 + 1 - k]), g_mine, g_core, rim0, x_weight, 640
     )
     grad_tokens = last_half(
         jnp.stack([(1 - x) * 2 + k, (1 - x) * 2 + 1 - k, x]), part, g_x, g_cross, rim1, rim0, bc_chip,
-        bc_recv, x_weight, bc_weight, dt_weight, 256,
+        bc_recv, x_weight, bc_weight, dt_rows, 640,
     )
     return (mixed, grad_tokens)
 

time: 171 us -> 142 us (0.83)
  Pallas kernels: 93.3 us -> 63.1 us
  waiting for transfers between devices: 25.3 us -> 28.8 us
    pallas_call x6 -> x3, Pallas kernels: 26.2 us -> 13.7 us  [the longest x1 5.78 us: rest_proj(): pl.pallas_call(rest_kernel, grid_spec=pltpu.PrefetchScalarGridSpec(num_sc...]
    ppermute x6, waiting for transfers between devices: 14.8 us -> 22.7 us  [by_chips(): by_x = lambda a: lax.ppermute(a, 'fsdp', pair)]
    pallas_call x1, Pallas kernels: 14.4 us -> 7.96 us  [grads_of(): pl.pallas_call(functools.partial(grads_kernel, doc_starts.shape[0], heads...]
    all_to_all x4, waiting for transfers between devices: 10.4 us -> 5.75 us  [by_chips(): lax.all_to_all(a, 'ctx', 0, 0, axis_index_groups=groups)]
    pallas_call x1, Pallas kernels: 6.25 us -> 2.57 us  [first_half(): pl.pallas_call(first_kernel, grid_spec=pltpu.PrefetchScalarGridSpec(num_s...]
    pallas_call x1, Pallas kernels: 7.46 us -> 4.19 us  [last_half(): pl.pallas_call(functools.partial(last_kernel, all_heads // 2), grid_spec=...]
    pallas_call x1, Pallas kernels: 2.76 us -> 0.73 us  [join(): pl.pallas_call(functools.partial(join_kernel, heads), grid_spec=pltpu.Pre...]
    pallas_call x2, Pallas kernels: 4.09 us -> 2.11 us  [chain(): pl.pallas_call(functools.partial(chain_kernel, heads, reverse), out_shape...]
  transfers between devices with their start and end apart: 26 -> 26, of which waited for: 8 -> 11; matrix products, arithmetic and copies ran while one was open for 4% -> 3% of each run, Pallas kernels for 33% -> 26%
where the time goes in v1:
time: 142 us; the launch traced here: 141 us
  Pallas kernels  63.1 us (44%)
  starting transfers between devices  33.8 us (24%)
  waiting for transfers between devices  28.8 us (20%)
  local copies, waits for them, and re-layouts  11.1 us (8%)
  other arithmetic  3.04 us (2%)
    ppermute x6, waiting for transfers between devices, by_chips(): by_x = lambda a: lax.ppermute(a, 'fsdp', pair)  22.7 us
    all_to_all x4, starting transfers between devices, by_chips(): lax.all_to_all(a, 'ctx', 0, 0, axis_index_groups=groups)  18.6 us
    unnamed x57, local copies, waits for them, and re-layouts  9.58 us
    pallas_call x1, Pallas kernels, grads_of(): pl.pallas_call(functools.partial(grads_kernel, doc_starts.shape[0], heads...  7.96 us
    pallas_call x1, Pallas kernels, outputs_of(): pl.pallas_call(functools.partial(out_kernel, heads), grid_spec=pltpu.Pref...  7.12 us
    pallas_call x1, Pallas kernels, within(): pl.pallas_call(functools.partial(within_kernel, doc_starts.shape[0], head...  6.83 us
    pallas_call x1, Pallas kernels, within_back(): pl.pallas_call(functools.partial(within_back_kernel, doc_starts.shape[0],...  6.8 us
    ppermute x6, starting transfers between devices, by_chips(): by_x = lambda a: lax.ppermute(a, 'fsdp', pair)  6.27 us
  transfers between devices with their start and end apart: 26, of which 11 were waited for; matrix products, arithmetic and copies ran while one was open for 3% of the time, Pallas kernels for 26%

profile of v1, /device:TPU:0, one launch (start us, length us, event | category | flops | bytes accessed | tf_op | source)
XLA Modules:
  0.0 140.9 jit_solution(15841872122671927020)
XLA Ops:
  2.8 3.7 %lead_proj.1 = (bf16[256,640]{1,0:T(8,128)(2,1)}, bf16[256,384]{1,0:T(8,128)(2,1)}, bf16[256,256]{1,0:T(8,128)(2,1)}) custom-call(s32[1]{0:T(128)} %bitcast.6.meta_ref, bf16[256,1280]{1,0:T(8,128)(2,1)} %tok_hbm.3, bf16[1280,2560]{1,0:T(8,128)(2,1)} %w_other_ref.3, bf16[1280,256]{1,0:T(8,128)(2,1)} %bcw_ref.1, bf16[40,1280]{1,0:T(8,128)(2,1)} %bitcast.15), custom_call_target="tpu_custom_call" | custom-call | flops 419430400 | bytes 3000000 | tf_op jit(solution)/shard_map/lead_proj/pallas_call | solution.py:284
  6.5 4.5 %collective-permute-start.7 = (bf16[256,384]{1,0:T(8,128)(2,1)}, bf16[256,384]{1,0:T(8,128)(2,1)S(1)}, u32[]{:S(2)}, u32[]{:S(2)}) collective-permute-start(bf16[256,384]{1,0:T(8,128)(2,1)} %get-tuple-element.55.own_ref), channel_id=1, source_target_pairs={{0,2},{2,0},{4,6},{6,4},{8,10},{10,8},{12,14},{14,12},{16,18},{18,... | collective-permute-start | bytes 589832 | tf_op jit(solution)/shard_map/ppermute | solution.py:1172
  11.0 1.5 %collective-permute-start.6 = (bf16[256,384]{1,0:T(8,128)(2,1)}, bf16[256,384]{1,0:T(8,128)(2,1)S(1)}, u32[]{:S(2)}, u32[]{:S(2)}) collective-permute-start(bf16[256,384]{1,0:T(8,128)(2,1)} %get-tuple-element.55.own_ref), channel_id=1, source_target_pairs={{0,1},{1,0},{2,3},{3,2},{4,5},{5,4},{6,7},{7,6},{8,9},{9,8},{10,11... | collective-permute-start | bytes 589832 | tf_op jit(solution)/shard_map/ppermute | solution.py:1173
  13.8 5.2 %collective-permute-done.6.xr_ref = bf16[256,384]{1,0:T(8,128)(2,1)S(1)} collective-permute-done((bf16[256,384]{1,0:T(8,128)(2,1)}, bf16[256,384]{1,0:T(8,128)(2,1)S(1)}, u32[]{:S(2)}, u32[]{:S(2)}) %collective-permute-start.6) | collective-permute-done | bytes 196640 | tf_op jit(solution)/shard_map/ppermute | solution.py:1173
  20.2 5.8 %rest_proj.1 = (bf16[256,640]{1,0:T(8,128)(2,1)}, bf16[256,640]{1,0:T(8,128)(2,1)}, bf16[256,640]{1,0:T(8,128)(2,1)}, bf16[16,896]{1,0:T(8,128)(2,1)}, bf16[16,896]{1,0:T(8,128)(2,1)}) custom-call(s32[3]{0:T(128)} %pad_add_fusion.1.meta_ref, bf16[256,1280]{1,0:T(8,128)(2,1)} %tok_hbm.3, bf16[1280,2560]{1,0:T(8,128)(2,1)} %w_other_ref.3, ...), custom_call_target="tpu_custom_call" | custom-call | flops 1258291200 | bytes 6000000 | tf_op jit(solution)/shard_map/rest_proj/pallas_call | solution.py:342
  26.0 1.6 %collective-permute-start.5 = (bf16[16,896]{1,0:T(8,128)(2,1)}, bf16[16,896]{1,0:T(8,128)(2,1)S(1)}, u32[]{:S(2)}, u32[]{:S(2)}) collective-permute-start(bf16[16,896]{1,0:T(8,128)(2,1)} %get-tuple-element.54), channel_id=1, source_target_pairs={{0,1},{1,0},{2,3},{3,2},{4,5},{5,4},{6,7},{7,6},{8,9},{9,8},{10,11... | collective-permute-start | bytes 86024 | tf_op jit(solution)/shard_map/ppermute | solution.py:1173
  28.8 1.4 collective-permute-done.5.rim_recv_ref
  31.0 4.9 %shared_maps.1 = (bf16[512,256]{1,0:T(8,128)(2,1)}, f32[512,256]{1,0:T(8,128)}, f32[512,128]{1,0:T(8,128)}, f32[512,128]{1,0:T(8,128)}, f32[512,128]{1,0:T(8,128...) custom-call(s32[3]{0:T(128)} %pad_add_fusion.meta_ref, ...), custom_call_target="tpu_custom_call" | custom-call | flops 4000000000 | bytes 4000000 | tf_op jit(solution)/shard_map/shared_maps/pallas_call | solution.py:448
  35.9 2.3 %collective-permute-done.2.xr_ref = bf16[256,640]{1,0:T(8,128)(2,1)S(1)} collective-permute-done((bf16[256,640]{1,0:T(8,128)(2,1)}, bf16[256,640]{1,0:T(8,128)(2,1)S(1)}, u32[]{:S(2)}, u32[]{:S(2)}) %collective-permute-start.2) | collective-permute-done | bytes 327712 | tf_op jit(solution)/shard_map/ppermute | solution.py:1173
  39.1 6.2 %inner_maps.1 = (f32[512,640]{1,0:T(8,128)}, bf16[512,640]{1,0:T(8,128)(2,1)}, f32[2,128,640]{2,1,0:T(8,128)}, bf16[8,16,768]{2,1,0:T(8,128)(2,1)}) custom-call(s32[3]{0:T(128)} %pad_add_fusion.meta_ref, s32[4]{0:T(128)} %docs_ref.9, bf16[256,640]{1,0:T(8,128)(2,1)} %get-tuple-element.49.own_ref, bf16[256,640]{1,0:T(8,128)(2,1)} %copy-done.18, ...), custom_call_target="tpu_custom_call" | custom-call | flops 4000000000 | bytes 4000000 | tf_op jit(solution)/shard_map/inner_maps/pallas_call | solution.py:561
  45.4 4.9 %all-to-all-start = ((bf16[8,16,768]{2,1,0:T(8,128)(2,1)}), bf16[8,16,768]{2,1,0:T(8,128)(2,1)S(1)}, u32[]{:S(2)}, u32[]{:S(2)}) async-start(bf16[8,16,768]{2,1,0:T(8,128)(2,1)} %get-tuple-element.65), calls=%async_computation | async-start | bytes 393216 | tf_op jit(solution)/shard_map/all_to_all | solution.py:1176
  50.9 4.4 %collective-permute-done.9.xr_low_ref = bf16[256,256]{1,0:T(8,128)(2,1)S(1)} collective-permute-done((bf16[256,256]{1,0:T(8,128)(2,1)S(1)}, bf16[256,256]{1,0:T(8,128)(2,1)S(1)}, u32[]{:S(2)}, u32[]{:S(2)}) %collective-permute-start.9) | collective-permute-done | bytes 131104 | tf_op jit(solution)/shard_map/ppermute | solution.py:1173
  56.5 1.5 %all-to-all-done.recv_ref.keep_ref = bf16[8,16,768]{2,1,0:T(8,128)(2,1)S(1)} async-done(((bf16[8,16,768]{2,1,0:T(8,128)(2,1)}), bf16[8,16,768]{2,1,0:T(8,128)(2,1)S(1)}, u32[]{:S(2)}, u32[]{:S(2)}) %all-to-all-start) | async-done | bytes 196640 | tf_op jit(solution)/shard_map/all_to_all | solution.py:1176
  58.0 1.1 chain.2
  59.1 4.4 %all-to-all-start.1 = ((bf16[8,16,640]{2,1,0:T(8,128)(2,1)}), bf16[8,16,640]{2,1,0:T(8,128)(2,1)S(1)}, u32[]{:S(2)}, u32[]{:S(2)}) async-start(bf16[8,16,640]{2,1,0:T(8,128)(2,1)} %chain.2), calls=%async_computation.1 | async-start | bytes 327680 | tf_op jit(solution)/shard_map/all_to_all | solution.py:1176
  64.2 6.8 %within.1 = (f32[512,640]{1,0:T(8,128)}, f32[2,256,256]{2,1,0:T(8,128)}) custom-call(s32[3]{0:T(128)} %pad_add_fusion.meta_ref, s32[4]{0:T(128)} %docs_ref.9, bf16[512,640]{1,0:T(8,128)(2,1)} %get-tuple-element.60.xd_ref, f32[512,128]{1,0:T(8,128)} %get-tuple-element.61.ramp_ref, f32[2,16,256]{2,1,0:T(8,128)} %get-tuple-element.62.rampt_ref, ...), custom_call_target="tpu_custom_call" | custom-call | flops 6000000000 | bytes 4000000 | tf_op jit(solution)/shard_map/within/pallas_call | solution.py:646
  71.9 7.1 %outputs_of.1 = (bf16[256,640]{1,0:T(8,128)(2,1)}, bf16[256,640]{1,0:T(8,128)(2,1)}, bf16[512,1280]{1,0:T(8,128)(2,1)}, bf16[512,640]{1,0:T(8,128)(2,1)}, f32[51...) custom-call(s32[3]{0:T(128)} %pad_add_fusion.meta_ref, ...), custom_call_target="tpu_custom_call" | custom-call | flops 4000000000 | bytes 4000000 | tf_op jit(solution)/shard_map/outputs_of/pallas_call | solution.py:770
  79.0 6.0 %all-to-all-start.2 = ((bf16[8,16,640]{2,1,0:T(8,128)(2,1)}), bf16[8,16,640]{2,1,0:T(8,128)(2,1)S(1)}, u32[]{:S(2)}, u32[]{:S(2)}) async-start(bf16[8,16,640]{2,1,0:T(8,128)(2,1)} %get-tuple-element.70), calls=%async_computation.2 | async-start | bytes 327680 | tf_op jit(solution)/shard_map/all_to_all | solution.py:1176
  85.0 4.1 %slopes_of.1 = (bf16[512,640]{1,0:T(8,128)(2,1)}, bf16[512,640]{1,0:T(8,128)(2,1)}, bf16[512,640]{1,0:T(8,128)(2,1)}, bf16[512,640]{1,0:T(8,128)(2,1)}, bf16[512,640]{1,0:T(8,128)(2,1)}) custom-call(f32[512,640]{1,0:T(8,128)} %get-tuple-element.76.pre_ref, bf16[512,128]{1,0:T(8,128)(2,1)} %get-tuple-element.57.dpk_ref, ...), custom_call_target="tpu_custom_call" | custom-call | flops 2000000000 | bytes 4000000 | tf_op jit(solution)/shard_map/slopes_of/pallas_call | solution.py:876
  89.1 3.4 %all-to-all-done.2.recv_ref = bf16[8,16,640]{2,1,0:T(8,128)(2,1)S(1)} async-done(((bf16[8,16,640]{2,1,0:T(8,128)(2,1)}), bf16[8,16,640]{2,1,0:T(8,128)(2,1)S(1)}, u32[]{:S(2)}, u32[]{:S(2)}) %all-to-all-start.2) | async-done | bytes 163872 | tf_op jit(solution)/shard_map/all_to_all | solution.py:1176
  92.5 1.1 chain.3
  93.6 3.4 %all-to-all-start.3 = ((bf16[8,16,640]{2,1,0:T(8,128)(2,1)}), bf16[8,16,640]{2,1,0:T(8,128)(2,1)S(1)}, u32[]{:S(2)}, u32[]{:S(2)}) async-start(bf16[8,16,640]{2,1,0:T(8,128)(2,1)} %chain.3), calls=%async_computation.3 | async-start | bytes 327680 | tf_op jit(solution)/shard_map/all_to_all | solution.py:1176
  97.0 6.8 %within_back.1 = (bf16[512,640]{1,0:T(8,128)(2,1)}, f32[512,128]{1,0:T(8,128)}, f32[512,256]{1,0:T(8,128)}) custom-call(s32[3]{0:T(128)} %pad_add_fusion.meta_ref, s32[4]{0:T(128)} %docs_ref.9, bf16[512,1280]{1,0:T(8,128)(2,1)} %get-tuple-element.73.dy_ref, bf16[512,640]{1,0:T(8,128)(2,1)} %get-tuple-element.74.edy_ref, ...), custom_call_target="tpu_custom_call" | custom-call | flops 10000000000 | bytes 6000000 | tf_op jit(solution)/shard_map/within_back/pallas_call | solution.py:836
  105.2 8.0 %grads_of.1 = (bf16[256,640]{1,0:T(8,128)(2,1)}, bf16[256,640]{1,0:T(8,128)(2,1)}, f32[256,384]{1,0:T(8,128)}, f32[256,384]{1,0:T(8,128)}, bf16[16,896]{1,0:T(8,128)(2,1)}) custom-call(s32[3]{0:T(128)} %pad_add_fusion.meta_ref, s32[4]{0:T(128)} %docs_ref.9, bf16[128,640]{1,0:T(8,128)(2,1)} %bitcast.18, f32[128,640]{1,0:T(8,128)} %get-tuple-element.71.late_ref, ...), custom_call_target="tpu_custom_call" | custom-call | flops 4000000000 | bytes 8000000 | tf_op jit(solution)/shard_map/grads_of/pallas_call | solution.py:995
  115.6 1.2 collective-permute-start.17
  117.4 1.0 copy-done.3
  120.1 1.0 maximum_select_fusion
  121.8 2.9 %copy-done = bf16[1280,2560]{1,0:T(8,128)(2,1)S(1)} copy-done((bf16[1280,2560]{1,0:T(8,128)(2,1)S(1)}, bf16[1280,2560]{1,0:T(8,128)(2,1)}, u32[]{:S(2)}) %copy-start) | copy-done | bytes 6553624
  124.7 2.6 %first_half.1.part_ref = f32[256,1280]{1,0:T(8,128)S(1)} custom-call(s32[2]{0:T(128)S(1)} %pad_add_fusion.3.meta_ref, bf16[256,640]{1,0:T(8,128)(2,1)S(1)} %copy-done.4, bf16[256,640]{1,0:T(8,128)(2,1)S(1)} %collective-permute-done.14.other_ref, bf16[32,896]{1,0:T(8,128)(2,1)S(1)} %collective-permute-done.16.rim_ref.rim0_ref, ...), custom_call_target="tpu_custom_call" | custom-call | flops 2000000000 | bytes 4000000 | tf_op jit(solution)/shard_map/first_half/pallas_call | solution.py:1065
  127.3 5.8 %collective-permute-done.17.mine_ref = bf16[256,640]{1,0:T(8,128)(2,1)S(1)} collective-permute-done((bf16[256,640]{1,0:T(8,128)(2,1)}, bf16[256,640]{1,0:T(8,128)(2,1)S(1)}, u32[]{:S(2)}, u32[]{:S(2)}) %collective-permute-start.17) | collective-permute-done | bytes 327712 | tf_op jit(solution)/shard_map/ppermute | solution.py:1173
  133.1 3.6 %collective-permute-done.21.bc_recv_ref = bf16[256,384]{1,0:T(8,128)(2,1)S(1)} collective-permute-done((bf16[256,384]{1,0:T(8,128)(2,1)S(1)}, bf16[256,384]{1,0:T(8,128)(2,1)S(1)}, u32[]{:S(2)}, u32[]{:S(2)}) %collective-permute-start.21) | collective-permute-done | bytes 196640 | tf_op jit(solution)/shard_map/ppermute | solution.py:1173
  136.7 4.2 %last_half.1 = bf16[256,1280]{1,0:T(8,128)(2,1)} custom-call(s32[3]{0:T(128)S(1)} %pad_add_fusion.2.side_ref, f32[256,1280]{1,0:T(8,128)S(1)} %first_half.1.part_ref, bf16[256,640]{1,0:T(8,128)(2,1)S(1)} %collective-permute-done.17.mine_ref, bf16[256,640]{1,0:T(8,128)(2,1)S(1)} %collective-permute-done.18.other_ref, ...), custom_call_target="tpu_custom_call" | custom-call | flops 2000000000 | bytes 4000000 | tf_op jit(solution)/shard_map/last_half/pallas_call | solution.py:1126
  (102 shorter events, 17.6 us)
Async XLA Ops:
  1.4 17.6 %collective-permute-start.1 = (bf16[16,1280]{1,0:T(8,128)(2,1)S(1)}, bf16[16,1280]{1,0:T(8,128)(2,1)S(1)}, u32[]{:S(2)}, u32[]{:S(2)}) collective-permute-start(bf16[16,1280]{1,0:T(8,128)(2,1)S(1)} %slice.3), channel_id=1, source_target_pairs={{2,6},{6,10},{10,14},{14,18},{18,22},{22,26},{26,30},{3,7},{7,11},... | collective-permute-start | bytes 122888 | tf_op jit(solution)/shard_map/ppermute | solution.py:1183
  2.1 16.9 %collective-permute-start = (bf16[16,1280]{1,0:T(8,128)(2,1)S(1)}, bf16[16,1280]{1,0:T(8,128)(2,1)S(1)}, u32[]{:S(2)}, u32[]{:S(2)}) collective-permute-start(bf16[16,1280]{1,0:T(8,128)(2,1)S(1)} %slice.3), channel_id=1, source_target_pairs={{2,4},{6,8},{10,12},{14,16},{18,20},{22,24},{26,28},{3,5},{7,9},{1... | collective-permute-start | bytes 122888 | tf_op jit(solution)/shard_map/ppermute | solution.py:1182
  6.5 23.7 %collective-permute-start.7 = (bf16[256,384]{1,0:T(8,128)(2,1)}, bf16[256,384]{1,0:T(8,128)(2,1)S(1)}, u32[]{:S(2)}, u32[]{:S(2)}) collective-permute-start(bf16[256,384]{1,0:T(8,128)(2,1)} %get-tuple-element.55.own_ref), channel_id=1, source_target_pairs={{0,2},{2,0},{4,6},{6,4},{8,10},{10,8},{12,14},{14,12},{16,18},{18,... | collective-permute-start | bytes 589832 | tf_op jit(solution)/shard_map/ppermute | solution.py:1172
  11.0 8.0 %collective-permute-start.6 = (bf16[256,384]{1,0:T(8,128)(2,1)}, bf16[256,384]{1,0:T(8,128)(2,1)S(1)}, u32[]{:S(2)}, u32[]{:S(2)}) collective-permute-start(bf16[256,384]{1,0:T(8,128)(2,1)} %get-tuple-element.55.own_ref), channel_id=1, source_target_pairs={{0,1},{1,0},{2,3},{3,2},{4,5},{5,4},{6,7},{7,6},{8,9},{9,8},{10,11... | collective-permute-start | bytes 589832 | tf_op jit(solution)/shard_map/ppermute | solution.py:1173
  12.5 23.4 %collective-permute-start.4 = (bf16[256,640]{1,0:T(8,128)(2,1)}, bf16[256,640]{1,0:T(8,128)(2,1)S(1)}, u32[]{:S(2)}, u32[]{:S(2)}) collective-permute-start(bf16[256,640]{1,0:T(8,128)(2,1)} %get-tuple-element.52), channel_id=1, source_target_pairs={{0,3},{1,2},{2,1},{3,0},{4,7},{5,6},{6,5},{7,4},{8,11},{9,10},{10,... | collective-permute-start | bytes 983048 | tf_op jit(solution)/shard_map/ppermute | solution.py:1174
  19.0 11.2 %collective-permute-start.8 = (bf16[256,384]{1,0:T(8,128)(2,1)S(1)}, bf16[256,384]{1,0:T(8,128)(2,1)S(1)}, u32[]{:S(2)}, u32[]{:S(2)}) collective-permute-start(bf16[256,384]{1,0:T(8,128)(2,1)S(1)} %collective-permute-done.6.xr_ref), channel_id=1, source_target_pairs={{0,2},{2,0},{4,6},{6,4},{8,10},{10,8},{12,14},{14,12},{16,18},{18,... | collective-permute-start | bytes 589832 | tf_op jit(solution)/shard_map/ppermute | solution.py:1172
  26.0 4.1 %collective-permute-start.5 = (bf16[16,896]{1,0:T(8,128)(2,1)}, bf16[16,896]{1,0:T(8,128)(2,1)S(1)}, u32[]{:S(2)}, u32[]{:S(2)}) collective-permute-start(bf16[16,896]{1,0:T(8,128)(2,1)} %get-tuple-element.54), channel_id=1, source_target_pairs={{0,1},{1,0},{2,3},{3,2},{4,5},{5,4},{6,7},{7,6},{8,9},{9,8},{10,11... | collective-permute-start | bytes 86024 | tf_op jit(solution)/shard_map/ppermute | solution.py:1173
  28.3 10.0 %collective-permute-start.2 = (bf16[256,640]{1,0:T(8,128)(2,1)}, bf16[256,640]{1,0:T(8,128)(2,1)S(1)}, u32[]{:S(2)}, u32[]{:S(2)}) collective-permute-start(bf16[256,640]{1,0:T(8,128)(2,1)} %get-tuple-element.50), channel_id=1, source_target_pairs={{0,1},{1,0},{2,3},{3,2},{4,5},{5,4},{6,7},{7,6},{8,9},{9,8},{10,11... | collective-permute-start | bytes 983048 | tf_op jit(solution)/shard_map/ppermute | solution.py:1173
  30.2 8.1 %collective-permute-start.3 = (bf16[256,640]{1,0:T(8,128)(2,1)}, bf16[256,640]{1,0:T(8,128)(2,1)S(1)}, u32[]{:S(2)}, u32[]{:S(2)}) collective-permute-start(bf16[256,640]{1,0:T(8,128)(2,1)} %get-tuple-element.51), channel_id=1, source_target_pairs={{0,2},{2,0},{4,6},{6,4},{8,10},{10,8},{12,14},{14,12},{16,18},{18,... | collective-permute-start | bytes 983048 | tf_op jit(solution)/shard_map/ppermute | solution.py:1172
  39.1 16.2 %copy-start.9 = (bf16[256,1280]{1,0:T(8,128)(2,1)S(1)}, bf16[256,1280]{1,0:T(8,128)(2,1)}, u32[]{:S(2)}) copy-start(bf16[256,1280]{1,0:T(8,128)(2,1)} %go_ref.1) | copy-start | bytes 1966084
  39.1 16.8 %copy-start.12 = (f32[1280]{0:T(1024)S(1)}, f32[1280]{0:T(1024)}, u32[]{:S(2)}) copy-start(f32[1280]{0:T(1024)} %param.19) | copy-start | bytes 15364
  45.4 12.7 %all-to-all-start = ((bf16[8,16,768]{2,1,0:T(8,128)(2,1)}), bf16[8,16,768]{2,1,0:T(8,128)(2,1)S(1)}, u32[]{:S(2)}, u32[]{:S(2)}) async-start(bf16[8,16,768]{2,1,0:T(8,128)(2,1)} %get-tuple-element.65), calls=%async_computation | async-start | bytes 393216 | tf_op jit(solution)/shard_map/all_to_all | solution.py:1176
  50.3 5.0 %collective-permute-start.9 = (bf16[256,256]{1,0:T(8,128)(2,1)S(1)}, bf16[256,256]{1,0:T(8,128)(2,1)S(1)}, u32[]{:S(2)}, u32[]{:S(2)}) collective-permute-start(bf16[256,256]{1,0:T(8,128)(2,1)S(1)} %copy-done.23), channel_id=1, source_target_pairs={{0,1},{1,0},{2,3},{3,2},{4,5},{5,4},{6,7},{7,6},{8,9},{9,8},{10,11... | collective-permute-start | bytes 393224 | tf_op jit(solution)/shard_map/ppermute | solution.py:1173
  50.9 12.6 %collective-permute-start.10 = (bf16[256,256]{1,0:T(8,128)(2,1)S(1)}, bf16[256,256]{1,0:T(8,128)(2,1)S(1)}, u32[]{:S(2)}, u32[]{:S(2)}) collective-permute-start(bf16[256,256]{1,0:T(8,128)(2,1)S(1)} %copy-done.23), channel_id=1, source_target_pairs={{0,2},{2,0},{4,6},{6,4},{8,10},{10,8},{12,14},{14,12},{16,18},{18,... | collective-permute-start | bytes 393224 | tf_op jit(solution)/shard_map/ppermute | solution.py:1172
  55.3 8.2 %collective-permute-start.11 = (bf16[256,256]{1,0:T(8,128)(2,1)S(1)}, bf16[256,256]{1,0:T(8,128)(2,1)S(1)}, u32[]{:S(2)}, u32[]{:S(2)}) collective-permute-start(bf16[256,256]{1,0:T(8,128)(2,1)S(1)} %collective-permute-done.9.xr_low_ref), channel_id=1, source_target_pairs={{0,2},{2,0},{4,6},{6,4},{8,10},{10,8},{12,14},{14,12},{16,18},{18,... | collective-permute-start | bytes 393224 | tf_op jit(solution)/shard_map/ppermute | solution.py:1172
  55.4 15.7 %collective-permute-start.12 = (bf16[256,640]{1,0:T(8,128)(2,1)S(1)}, bf16[256,640]{1,0:T(8,128)(2,1)S(1)}, u32[]{:S(2)}, u32[]{:S(2)}) collective-permute-start(bf16[256,640]{1,0:T(8,128)(2,1)S(1)} %constant_dynamic-slice_fusion), channel_id=1, source_target_pairs={{0,2},{2,0},{4,6},{6,4},{8,10},{10,8},{12,14},{14,12},{16,18},{18,... | collective-permute-start | bytes 983048 | tf_op jit(solution)/shard_map/ppermute | solution.py:1172
  59.1 12.0 %all-to-all-start.1 = ((bf16[8,16,640]{2,1,0:T(8,128)(2,1)}), bf16[8,16,640]{2,1,0:T(8,128)(2,1)S(1)}, u32[]{:S(2)}, u32[]{:S(2)}) async-start(bf16[8,16,640]{2,1,0:T(8,128)(2,1)} %chain.2), calls=%async_computation.1 | async-start | bytes 327680 | tf_op jit(solution)/shard_map/all_to_all | solution.py:1176
  79.0 13.6 %all-to-all-start.2 = ((bf16[8,16,640]{2,1,0:T(8,128)(2,1)}), bf16[8,16,640]{2,1,0:T(8,128)(2,1)S(1)}, u32[]{:S(2)}, u32[]{:S(2)}) async-start(bf16[8,16,640]{2,1,0:T(8,128)(2,1)} %get-tuple-element.70), calls=%async_computation.2 | async-start | bytes 327680 | tf_op jit(solution)/shard_map/all_to_all | solution.py:1176
  93.6 10.9 %all-to-all-start.3 = ((bf16[8,16,640]{2,1,0:T(8,128)(2,1)}), bf16[8,16,640]{2,1,0:T(8,128)(2,1)S(1)}, u32[]{:S(2)}, u32[]{:S(2)}) async-start(bf16[8,16,640]{2,1,0:T(8,128)(2,1)} %chain.3), calls=%async_computation.3 | async-start | bytes 327680 | tf_op jit(solution)/shard_map/all_to_all | solution.py:1176
  105.2 12.3 %copy-start.5 = (s32[3]{0:T(128)S(1)}, s32[3]{0:T(128)}, u32[]{:S(2)}) copy-start(s32[3]{0:T(128)} %pad_add_fusion.meta_ref) | copy-start | bytes 40
  105.2 15.0 %copy-start.6 = (bf16[256,640]{1,0:T(8,128)(2,1)S(1)}, bf16[256,640]{1,0:T(8,128)(2,1)}, u32[]{:S(2)}) copy-start(bf16[256,640]{1,0:T(8,128)(2,1)} %get-tuple-element.68) | copy-start | bytes 983044
  113.1 3.6 %collective-permute-start.20 = (f32[256,384]{1,0:T(8,128)}, f32[256,384]{1,0:T(8,128)S(1)}, u32[]{:S(2)}, u32[]{:S(2)}) collective-permute-start(f32[256,384]{1,0:T(8,128)} %get-tuple-element.93), channel_id=1, source_target_pairs={{0,2},{2,0},{4,6},{6,4},{8,10},{10,8},{12,14},{14,12},{16,18},{18,... | collective-permute-start | bytes 1179656 | tf_op jit(solution)/shard_map/ppermute | solution.py:1172
  113.2 5.9 %collective-permute-start.13 = (bf16[256,640]{1,0:T(8,128)(2,1)S(1)}, bf16[256,640]{1,0:T(8,128)(2,1)S(1)}, u32[]{:S(2)}, u32[]{:S(2)}) collective-permute-start(bf16[256,640]{1,0:T(8,128)(2,1)S(1)} %copy-done.15), channel_id=1, source_target_pairs={{0,2},{2,0},{4,6},{6,4},{8,10},{10,8},{12,14},{14,12},{16,18},{18,... | collective-permute-start | bytes 983048 | tf_op jit(solution)/shard_map/ppermute | solution.py:1172
  113.8 1.8 %collective-permute-start.15 = (bf16[16,896]{1,0:T(8,128)(2,1)}, bf16[16,896]{1,0:T(8,128)(2,1)S(1)}, u32[]{:S(2)}, u32[]{:S(2)}) collective-permute-start(bf16[16,896]{1,0:T(8,128)(2,1)} %get-tuple-element.91), channel_id=1, source_target_pairs={{0,2},{2,0},{4,6},{6,4},{8,10},{10,8},{12,14},{14,12},{16,18},{18,... | collective-permute-start | bytes 86024 | tf_op jit(solution)/shard_map/ppermute | solution.py:1172
  114.6 18.5 %collective-permute-start.18 = (bf16[256,640]{1,0:T(8,128)(2,1)}, bf16[256,640]{1,0:T(8,128)(2,1)S(1)}, u32[]{:S(2)}, u32[]{:S(2)}) collective-permute-start(bf16[256,640]{1,0:T(8,128)(2,1)} %get-tuple-element.90), channel_id=1, source_target_pairs={{0,3},{1,2},{2,1},{3,0},{4,7},{5,6},{6,5},{7,4},{8,11},{9,10},{10,... | collective-permute-start | bytes 983048 | tf_op jit(solution)/shard_map/ppermute | solution.py:1174
  115.2 6.6 %collective-permute-start.14 = (bf16[256,640]{1,0:T(8,128)(2,1)}, bf16[256,640]{1,0:T(8,128)(2,1)S(1)}, u32[]{:S(2)}, u32[]{:S(2)}) collective-permute-start(bf16[256,640]{1,0:T(8,128)(2,1)} %get-tuple-element.90), channel_id=1, source_target_pairs={{0,2},{2,0},{4,6},{6,4},{8,10},{10,8},{12,14},{14,12},{16,18},{18,... | collective-permute-start | bytes 983048 | tf_op jit(solution)/shard_map/ppermute | solution.py:1172
  115.6 17.5 %collective-permute-start.17 = (bf16[256,640]{1,0:T(8,128)(2,1)}, bf16[256,640]{1,0:T(8,128)(2,1)S(1)}, u32[]{:S(2)}, u32[]{:S(2)}) collective-permute-start(bf16[256,640]{1,0:T(8,128)(2,1)} %get-tuple-element.89.mine_ref), channel_id=1, source_target_pairs={{0,1},{1,0},{2,3},{3,2},{4,5},{5,4},{6,7},{7,6},{8,9},{9,8},{10,11... | collective-permute-start | bytes 983048 | tf_op jit(solution)/shard_map/ppermute | solution.py:1173
  116.8 4.4 %collective-permute-start.16 = (bf16[32,896]{1,0:T(8,128)(2,1)S(1)}, bf16[32,896]{1,0:T(8,128)(2,1)S(1)}, u32[]{:S(2)}, u32[]{:S(2)}) collective-permute-start(bf16[32,896]{1,0:T(8,128)(2,1)S(1)} %constant_dynamic-update-slice_fusion), channel_id=1, source_target_pairs={{6,2},{10,6},{14,10},{18,14},{22,18},{26,22},{30,26},{7,3},{11,7},... | collective-permute-start | bytes 172040 | tf_op jit(solution)/shard_map/ppermute | solution.py:1244
  119.2 17.5 %collective-permute-start.21 = (bf16[256,384]{1,0:T(8,128)(2,1)S(1)}, bf16[256,384]{1,0:T(8,128)(2,1)S(1)}, u32[]{:S(2)}, u32[]{:S(2)}) collective-permute-start(bf16[256,384]{1,0:T(8,128)(2,1)S(1)} %get-tuple-element.95), channel_id=1, source_target_pairs={{0,1},{1,0},{2,3},{3,2},{4,5},{5,4},{6,7},{7,6},{8,9},{9,8},{10,11... | collective-permute-start | bytes 589832 | tf_op jit(solution)/shard_map/ppermute | solution.py:1173
  120.1 16.6 %copy-start.1 = (bf16[1280,256]{1,0:T(8,128)(2,1)S(1)}, bf16[1280,256]{1,0:T(8,128)(2,1)}, u32[]{:S(2)}) copy-start(bf16[1280,256]{1,0:T(8,128)(2,1)} %bcw_ref.1) | copy-start | bytes 1966084
  120.1 16.6 %copy-start.2 = (bf16[1280,40]{0,1:T(8,128)(2,1)S(1)}, bf16[1280,40]{0,1:T(8,128)(2,1)}, u32[]{:S(2)}) copy-start(bf16[1280,40]{0,1:T(8,128)(2,1)} %param.14) | copy-start | bytes 307204
  121.1 6.1 %collective-permute-start.19 = (bf16[32,896]{1,0:T(8,128)(2,1)S(1)}, bf16[32,896]{1,0:T(8,128)(2,1)S(1)}, u32[]{:S(2)}, u32[]{:S(2)}) collective-permute-start(bf16[32,896]{1,0:T(8,128)(2,1)S(1)} %constant_dynamic-update-slice_fusion), channel_id=1, source_target_pairs={{6,3},{7,2},{10,7},{11,6},{14,11},{15,10},{18,15},{19,14},{22,19},... | collective-permute-start | bytes 172040 | tf_op jit(solution)/shard_map/ppermute | solution.py:1245
  (22 other events, 72.0 us)

commit v2 on v1

--- a/solution.py
+++ b/solution.py
@@ -1046,7 +1046,8 @@
     )(meta, own, recv)
 
 
-def first_kernel(meta_ref, mine_ref, other_ref, rim_ref, w_mine_ref, w_other_ref, out_ref):
+def half_kernel(meta_ref, *refs):
+    *before, mine_ref, other_ref, rim_ref, w_mine_ref, w_other_ref, out_ref = refs
     rows, width = mine_ref.shape
 
     def whole(ref, rim):
@@ -1055,100 +1056,91 @@
 
     mine = whole(mine_ref, rim_ref[:16, :width])
     other = whole(other_ref, rim_ref[16:, :width])
-    out_ref[...] = mm_nt(mine, w_mine_ref[...]) + mm_nt(other, w_other_ref[...])
-
-
-def first_half(blocks, mine, other, rim, x_weight, tile):
+    total = mm_nt(mine, w_mine_ref[...]) + mm_nt(other, w_other_ref[...])
+    for ref in before:
+        total = total + ref[...]
+    out_ref[...] = total
+
+
+def first_half(blocks, before, mine, other, rim, x_weight, tile):
     rows, width = mine.shape
     depth = x_weight.shape[0]
     whole = lambda shape: pl.BlockSpec(shape, lambda i, m: (0, 0))
+    part = pl.BlockSpec((rows, tile), lambda i, m: (0, i))
+    parts = [] if before is None else [before]
     return pl.pallas_call(
-        first_kernel,
+        half_kernel,
         grid_spec=pltpu.PrefetchScalarGridSpec(
             num_scalar_prefetch=1,
             grid=(depth // tile,),
-            in_specs=[
+            in_specs=[part] * len(parts)
+            + [
                 whole(mine.shape), whole(other.shape), whole(rim.shape),
                 pl.BlockSpec((tile, width), lambda i, m: (i, m[0])),
                 pl.BlockSpec((tile, width), lambda i, m: (i, m[1])),
             ],
-            out_specs=pl.BlockSpec((rows, tile), lambda i, m: (0, i)),
+            out_specs=part,
         ),
         out_shape=jax.ShapeDtypeStruct((rows, depth), F32),
         compiler_params=params(16),
         cost_estimate=cost(2e9, 4e6),
-        name="first_half",
-    )(blocks, mine, other, rim, x_weight, x_weight)
+        name="half_sum",
+    )(blocks, *parts, mine, other, rim, x_weight, x_weight)
 
 
 def last_kernel(
-    heads, side_ref, part_ref, mine_ref, other_ref, rim_ref, rim0_ref, bc_own_ref, bc_recv_ref,
-    w_mine_ref, w_other_ref, bcw_ref, dtw_ref, out_ref, bc_ref, dt_ref, left_ref, right_ref,
+    heads, rim_width, side_ref, part_ref, rim_ref, rim0_ref, bc_own_ref, bc_recv_ref, bcw_ref, dtw_ref,
+    out_ref, bc_ref, dt_ref,
 ):
-    rows, width = mine_ref.shape
+    rows = part_ref.shape[0]
     states2 = bcw_ref.shape[1]
     all_heads = dtw_ref.shape[0]
 
     @pl.when(pl.program_id(0) == 0)
     def _():
-        for ref, rim, to_ref in (
-            (mine_ref, rim_ref[:16, :width], left_ref),
-            (other_ref, rim_ref[16:, :width], right_ref),
-        ):
-            to_ref[: rows - 16, :] = ref[: rows - 16, :]
-            to_ref[rows - 16 :, :] = (ref[rows - 16 :, :].astype(F32) + rim.astype(F32)).astype(BF)
         bc = bc_own_ref[:, :states2] + bc_recv_ref[:, :states2].astype(F32)
-        rim = rim_ref[...].astype(F32) + rim0_ref[...].astype(F32)
-        extra = rim[:16, width:] + rim[16:, width:]
+        rim = rim_ref[:, rim_width:].astype(F32) + rim0_ref[:, rim_width:].astype(F32)
+        extra = rim[:16] + rim[16:]
         for at, value in ((0, bc[: rows - 16, :]), (rows - 16, bc[rows - 16 :, :] + extra)):
             high, low = split2(value)
             bc_ref[at : at + value.shape[0], :states2] = high
             bc_ref[at : at + value.shape[0], states2:] = low
         shape = (LANES, all_heads)
         row, col = iota(shape, 0), iota(shape, 1)
-        x = side_ref[2]
+        x = side_ref[0]
         here = jnp.where((row < heads) & (col == row + x * heads), 1.0, 0.0).astype(BF)
         there = jnp.where((row < heads) & (col == row + (1 - x) * heads), 1.0, 0.0).astype(BF)
-        dt_ref[...] = (mm(bc_own_ref[:, states2:].astype(BF), here) + mm(bc_recv_ref[:, states2:], there)).astype(BF)
-
-    total = part_ref[...] + mm_nt(left_ref[...], w_mine_ref[...])
-    total = total + mm_nt(right_ref[...], w_other_ref[...])
+        dt = mm(bc_own_ref[:, states2:].astype(BF), here) + mm(bc_recv_ref[:, states2:], there)
+        dt_ref[...] = dt.astype(BF)
+
     bcw = bcw_ref[...]
-    total = total + mm_nt(bc_ref[...], jnp.concatenate([bcw, bcw], axis=1)) + mm(dt_ref[...], dtw_ref[...])
-    out_ref[...] = total.astype(BF)
-
-
-def last_half(blocks, part, mine, other, rim, rim0, bc_own, bc_recv, x_weight, bc_weight, dt_rows, tile):
-    rows, width = mine.shape
-    depth = x_weight.shape[0]
+    total = part_ref[...] + mm_nt(bc_ref[...], jnp.concatenate([bcw, bcw], axis=1))
+    out_ref[...] = (total + mm(dt_ref[...], dtw_ref[...])).astype(BF)
+
+
+def last_half(side, part, rim, rim0, bc_own, bc_recv, bc_weight, dt_rows, tile):
+    rows, depth = part.shape
     states2, all_heads = bc_weight.shape[1], dt_rows.shape[0]
     whole = lambda a: pl.BlockSpec(a.shape, lambda i, m: (0, 0))
     return pl.pallas_call(
-        functools.partial(last_kernel, all_heads // 2),
+        functools.partial(last_kernel, all_heads // 2, rim.shape[1] - states2),
         grid_spec=pltpu.PrefetchScalarGridSpec(
             num_scalar_prefetch=1,
             grid=(depth // tile,),
             in_specs=[
                 pl.BlockSpec((rows, tile), lambda i, m: (0, i)),
-                whole(mine), whole(other), whole(rim), whole(rim0), whole(bc_own), whole(bc_recv),
-                pl.BlockSpec((tile, width), lambda i, m: (i, m[0])),
-                pl.BlockSpec((tile, width), lambda i, m: (i, m[1])),
+                whole(rim), whole(rim0), whole(bc_own), whole(bc_recv),
                 pl.BlockSpec((tile, states2), lambda i, m: (i, 0)),
                 pl.BlockSpec((all_heads, tile), lambda i, m: (0, i)),
             ],
             out_specs=pl.BlockSpec((rows, tile), lambda i, m: (0, i)),
-            scratch_shapes=[
-                pltpu.VMEM((rows, 2 * states2), BF),
-                pltpu.VMEM((rows, all_heads), BF),
-                pltpu.VMEM((rows, width), BF),
-                pltpu.VMEM((rows, width), BF),
-            ],
+            scratch_shapes=[pltpu.VMEM((rows, 2 * states2), BF), pltpu.VMEM((rows, all_heads), BF)],
         ),
         out_shape=jax.ShapeDtypeStruct((rows, depth), BF),
         compiler_params=params(16),
-        cost_estimate=cost(2e9, 4e6),
+        cost_estimate=cost(5e8, 2e6),
         name="last_half",
-    )(blocks, part, mine, other, rim, rim0, bc_own, bc_recv, x_weight, x_weight, bc_weight, dt_rows)
+    )(side, part, rim, rim0, bc_own, bc_recv, bc_weight, dt_rows)
 
 
 def by_chips(
@@ -1248,12 +1240,12 @@
     bc_chip, bc_send = join(meta, bc_mine, by_core(bc_other), heads)
     bc_recv = by_x(bc_send)
     part = first_half(
-        jnp.stack([x * 2 + k, x * 2 + 1 - k]), g_mine, g_core, rim0, x_weight, 640
-    )
-    grad_tokens = last_half(
-        jnp.stack([(1 - x) * 2 + k, (1 - x) * 2 + 1 - k, x]), part, g_x, g_cross, rim1, rim0, bc_chip,
-        bc_recv, x_weight, bc_weight, dt_rows, 640,
-    )
+        jnp.stack([x * 2 + k, x * 2 + 1 - k]), None, g_mine, g_core, rim0, x_weight, 640
+    )
+    part = first_half(
+        jnp.stack([(1 - x) * 2 + k, (1 - x) * 2 + 1 - k]), part, g_x, g_cross, rim1, x_weight, 640
+    )
+    grad_tokens = last_half(x[None], part, rim1, rim0, bc_chip, bc_recv, bc_weight, dt_rows, width)
     return (mixed, grad_tokens)
 
 

time: 142 us -> 139 us (0.979)
  waiting for transfers between devices: 28.8 us -> 25.3 us
  local copies, waits for them, and re-layouts: 11.1 us -> 9.57 us
  starting transfers between devices: 33.8 us -> 35.3 us
    ppermute x6, waiting for transfers between devices: 22.7 us -> 14.9 us  [by_chips(): by_x = lambda a: lax.ppermute(a, 'fsdp', pair)]
    all_to_all x4, waiting for transfers between devices: 5.75 us -> 10.3 us  [by_chips(): lax.all_to_all(a, 'ctx', 0, 0, axis_index_groups=groups)]
    unnamed x57, local copies, waits for them, and re-layouts: 9.58 us -> 8.08 us
    pallas_call x2 -> x3, Pallas kernels: 6.77 us -> 7.36 us  [the longest x2 5.28 us: first_half(): pl.pallas_call(half_kernel, grid_spec=pltpu.PrefetchScalarGridSpec(num_sc...]
  transfers between devices with their start and end apart: 26 -> 26, of which waited for: 11 -> 8; matrix products, arithmetic and copies ran while one was open for 3% -> 3% of each run, Pallas kernels for 26% -> 40%
where the time goes in v2:
time: 139 us; the launch traced here: 138 us
  Pallas kernels  63.9 us (46%)
  starting transfers between devices  35.3 us (25%)
  waiting for transfers between devices  25.3 us (18%)
  local copies, waits for them, and re-layouts  9.57 us (7%)
  other arithmetic  3 us (2%)
    all_to_all x4, starting transfers between devices, by_chips(): lax.all_to_all(a, 'ctx', 0, 0, axis_index_groups=groups)  17.6 us
    ppermute x6, waiting for transfers between devices, by_chips(): by_x = lambda a: lax.ppermute(a, 'fsdp', pair)  14.9 us
    all_to_all x4, waiting for transfers between devices, by_chips(): lax.all_to_all(a, 'ctx', 0, 0, axis_index_groups=groups)  10.3 us
    unnamed x57, local copies, waits for them, and re-layouts  8.08 us
    pallas_call x1, Pallas kernels, grads_of(): pl.pallas_call(functools.partial(grads_kernel, doc_starts.shape[0], heads...  8.07 us
    ppermute x6, starting transfers between devices, by_chips(): by_x = lambda a: lax.ppermute(a, 'fsdp', pair)  7.17 us
    pallas_call x1, Pallas kernels, outputs_of(): pl.pallas_call(functools.partial(out_kernel, heads), grid_spec=pltpu.Pref...  7.13 us
    pallas_call x1, Pallas kernels, within(): pl.pallas_call(functools.partial(within_kernel, doc_starts.shape[0], head...  6.83 us
  transfers between devices with their start and end apart: 26, of which 8 were waited for; matrix products, arithmetic and copies ran while one was open for 3% of the time, Pallas kernels for 40%

profile of v2, /device:TPU:0, one launch (start us, length us, event | category | flops | bytes accessed | tf_op | source)
XLA Modules:
  0.0 138.1 jit_solution(14492177535553434367)
XLA Ops:
  2.8 3.7 %lead_proj.1 = (bf16[256,640]{1,0:T(8,128)(2,1)}, bf16[256,384]{1,0:T(8,128)(2,1)}, bf16[256,256]{1,0:T(8,128)(2,1)}) custom-call(s32[1]{0:T(128)} %bitcast.6.meta_ref, bf16[256,1280]{1,0:T(8,128)(2,1)} %tok_hbm.3, bf16[1280,2560]{1,0:T(8,128)(2,1)} %refs_5_.1, bf16[1280,256]{1,0:T(8,128)(2,1)} %bcw_ref.1, bf16[40,1280]{1,0:T(8,128)(2,1)} %bitcast.15), custom_call_target="tpu_custom_call" | custom-call | flops 419430400 | bytes 3000000 | tf_op jit(solution)/shard_map/lead_proj/pallas_call | solution.py:284
  6.5 4.5 %collective-permute-start.7 = (bf16[256,384]{1,0:T(8,128)(2,1)}, bf16[256,384]{1,0:T(8,128)(2,1)S(1)}, u32[]{:S(2)}, u32[]{:S(2)}) collective-permute-start(bf16[256,384]{1,0:T(8,128)(2,1)} %get-tuple-element.55.own_ref), channel_id=1, source_target_pairs={{0,2},{2,0},{4,6},{6,4},{8,10},{10,8},{12,14},{14,12},{16,18},{18,... | collective-permute-start | bytes 589832 | tf_op jit(solution)/shard_map/ppermute | solution.py:1164
  11.0 1.5 %collective-permute-start.6 = (bf16[256,384]{1,0:T(8,128)(2,1)}, bf16[256,384]{1,0:T(8,128)(2,1)S(1)}, u32[]{:S(2)}, u32[]{:S(2)}) collective-permute-start(bf16[256,384]{1,0:T(8,128)(2,1)} %get-tuple-element.55.own_ref), channel_id=1, source_target_pairs={{0,1},{1,0},{2,3},{3,2},{4,5},{5,4},{6,7},{7,6},{8,9},{9,8},{10,11... | collective-permute-start | bytes 589832 | tf_op jit(solution)/shard_map/ppermute | solution.py:1165
  14.9 4.0 %collective-permute-done.6.xr_ref = bf16[256,384]{1,0:T(8,128)(2,1)S(1)} collective-permute-done((bf16[256,384]{1,0:T(8,128)(2,1)}, bf16[256,384]{1,0:T(8,128)(2,1)S(1)}, u32[]{:S(2)}, u32[]{:S(2)}) %collective-permute-start.6) | collective-permute-done | bytes 196640 | tf_op jit(solution)/shard_map/ppermute | solution.py:1165
  19.7 5.8 %rest_proj.1 = (bf16[256,640]{1,0:T(8,128)(2,1)}, bf16[256,640]{1,0:T(8,128)(2,1)}, bf16[256,640]{1,0:T(8,128)(2,1)}, bf16[16,896]{1,0:T(8,128)(2,1)}, bf16[16,896]{1,0:T(8,128)(2,1)}) custom-call(s32[3]{0:T(128)} %pad_add_fusion.1.meta_ref, bf16[256,1280]{1,0:T(8,128)(2,1)} %tok_hbm.3, bf16[1280,2560]{1,0:T(8,128)(2,1)} %refs_5_.1, ...), custom_call_target="tpu_custom_call" | custom-call | flops 1258291200 | bytes 6000000 | tf_op jit(solution)/shard_map/rest_proj/pallas_call | solution.py:342
  25.5 1.6 %collective-permute-start.5 = (bf16[16,896]{1,0:T(8,128)(2,1)}, bf16[16,896]{1,0:T(8,128)(2,1)S(1)}, u32[]{:S(2)}, u32[]{:S(2)}) collective-permute-start(bf16[16,896]{1,0:T(8,128)(2,1)} %get-tuple-element.54), channel_id=1, source_target_pairs={{0,1},{1,0},{2,3},{3,2},{4,5},{5,4},{6,7},{7,6},{8,9},{9,8},{10,11... | collective-permute-start | bytes 86024 | tf_op jit(solution)/shard_map/ppermute | solution.py:1165
  27.6 2.0 %collective-permute-done.5.rim_recv_ref = bf16[16,896]{1,0:T(8,128)(2,1)S(1)} collective-permute-done((bf16[16,896]{1,0:T(8,128)(2,1)}, bf16[16,896]{1,0:T(8,128)(2,1)S(1)}, u32[]{:S(2)}, u32[]{:S(2)}) %collective-permute-start.5) | collective-permute-done | bytes 28704 | tf_op jit(solution)/shard_map/ppermute | solution.py:1165
  29.6 1.5 %collective-permute-start.2 = (bf16[256,640]{1,0:T(8,128)(2,1)}, bf16[256,640]{1,0:T(8,128)(2,1)S(1)}, u32[]{:S(2)}, u32[]{:S(2)}) collective-permute-start(bf16[256,640]{1,0:T(8,128)(2,1)} %get-tuple-element.50), channel_id=1, source_target_pairs={{0,1},{1,0},{2,3},{3,2},{4,5},{5,4},{6,7},{7,6},{8,9},{9,8},{10,11... | collective-permute-start | bytes 983048 | tf_op jit(solution)/shard_map/ppermute | solution.py:1165
  31.9 4.9 %shared_maps.1 = (bf16[512,256]{1,0:T(8,128)(2,1)}, f32[512,256]{1,0:T(8,128)}, f32[512,128]{1,0:T(8,128)}, f32[512,128]{1,0:T(8,128)}, f32[512,128]{1,0:T(8,128...) custom-call(s32[3]{0:T(128)} %pad_add_fusion.meta_ref, ...), custom_call_target="tpu_custom_call" | custom-call | flops 4000000000 | bytes 4000000 | tf_op jit(solution)/shard_map/shared_maps/pallas_call | solution.py:448
  36.8 1.9 %collective-permute-done.2.xr_ref = bf16[256,640]{1,0:T(8,128)(2,1)S(1)} collective-permute-done((bf16[256,640]{1,0:T(8,128)(2,1)}, bf16[256,640]{1,0:T(8,128)(2,1)S(1)}, u32[]{:S(2)}, u32[]{:S(2)}) %collective-permute-start.2) | collective-permute-done | bytes 327712 | tf_op jit(solution)/shard_map/ppermute | solution.py:1165
  39.6 6.3 %inner_maps.1 = (f32[512,640]{1,0:T(8,128)}, bf16[512,640]{1,0:T(8,128)(2,1)}, f32[2,128,640]{2,1,0:T(8,128)}, bf16[8,16,768]{2,1,0:T(8,128)(2,1)}) custom-call(s32[3]{0:T(128)} %pad_add_fusion.meta_ref, s32[4]{0:T(128)} %docs_ref.9, bf16[256,640]{1,0:T(8,128)(2,1)} %get-tuple-element.49.own_ref, bf16[256,640]{1,0:T(8,128)(2,1)} %copy-done.18, ...), custom_call_target="tpu_custom_call" | custom-call | flops 4000000000 | bytes 4000000 | tf_op jit(solution)/shard_map/inner_maps/pallas_call | solution.py:561
  45.8 4.9 %all-to-all-start = ((bf16[8,16,768]{2,1,0:T(8,128)(2,1)}), bf16[8,16,768]{2,1,0:T(8,128)(2,1)S(1)}, u32[]{:S(2)}, u32[]{:S(2)}) async-start(bf16[8,16,768]{2,1,0:T(8,128)(2,1)} %get-tuple-element.65), calls=%async_computation | async-start | bytes 393216 | tf_op jit(solution)/shard_map/all_to_all | solution.py:1168
  52.2 6.3 %all-to-all-done.recv_ref.keep_ref = bf16[8,16,768]{2,1,0:T(8,128)(2,1)S(1)} async-done(((bf16[8,16,768]{2,1,0:T(8,128)(2,1)}), bf16[8,16,768]{2,1,0:T(8,128)(2,1)S(1)}, u32[]{:S(2)}, u32[]{:S(2)}) %all-to-all-start) | async-done | bytes 196640 | tf_op jit(solution)/shard_map/all_to_all | solution.py:1168
  58.5 1.1 chain.2
  59.6 3.4 %all-to-all-start.1 = ((bf16[8,16,640]{2,1,0:T(8,128)(2,1)}), bf16[8,16,640]{2,1,0:T(8,128)(2,1)S(1)}, u32[]{:S(2)}, u32[]{:S(2)}) async-start(bf16[8,16,640]{2,1,0:T(8,128)(2,1)} %chain.2), calls=%async_computation.1 | async-start | bytes 327680 | tf_op jit(solution)/shard_map/all_to_all | solution.py:1168
  63.7 6.8 %within.1 = (f32[512,640]{1,0:T(8,128)}, f32[2,256,256]{2,1,0:T(8,128)}) custom-call(s32[3]{0:T(128)} %pad_add_fusion.meta_ref, s32[4]{0:T(128)} %docs_ref.9, bf16[512,640]{1,0:T(8,128)(2,1)} %get-tuple-element.60.xd_ref, f32[512,128]{1,0:T(8,128)} %get-tuple-element.61.ramp_ref, f32[2,16,256]{2,1,0:T(8,128)} %get-tuple-element.62.rampt_ref, ...), custom_call_target="tpu_custom_call" | custom-call | flops 6000000000 | bytes 4000000 | tf_op jit(solution)/shard_map/within/pallas_call | solution.py:646
  71.3 7.1 %outputs_of.1 = (bf16[256,640]{1,0:T(8,128)(2,1)}, bf16[256,640]{1,0:T(8,128)(2,1)}, bf16[512,1280]{1,0:T(8,128)(2,1)}, bf16[512,640]{1,0:T(8,128)(2,1)}, f32[51...) custom-call(s32[3]{0:T(128)} %pad_add_fusion.meta_ref, ...), custom_call_target="tpu_custom_call" | custom-call | flops 4000000000 | bytes 4000000 | tf_op jit(solution)/shard_map/outputs_of/pallas_call | solution.py:770
  78.4 5.9 %all-to-all-start.2 = ((bf16[8,16,640]{2,1,0:T(8,128)(2,1)}), bf16[8,16,640]{2,1,0:T(8,128)(2,1)S(1)}, u32[]{:S(2)}, u32[]{:S(2)}) async-start(bf16[8,16,640]{2,1,0:T(8,128)(2,1)} %get-tuple-element.70), calls=%async_computation.2 | async-start | bytes 327680 | tf_op jit(solution)/shard_map/all_to_all | solution.py:1168
  84.5 4.2 %slopes_of.1 = (bf16[512,640]{1,0:T(8,128)(2,1)}, bf16[512,640]{1,0:T(8,128)(2,1)}, bf16[512,640]{1,0:T(8,128)(2,1)}, bf16[512,640]{1,0:T(8,128)(2,1)}, bf16[512,640]{1,0:T(8,128)(2,1)}) custom-call(f32[512,640]{1,0:T(8,128)} %get-tuple-element.76.pre_ref, bf16[512,128]{1,0:T(8,128)(2,1)} %get-tuple-element.57.dpk_ref, ...), custom_call_target="tpu_custom_call" | custom-call | flops 2000000000 | bytes 4000000 | tf_op jit(solution)/shard_map/slopes_of/pallas_call | solution.py:876
  88.6 3.3 %all-to-all-done.2.recv_ref = bf16[8,16,640]{2,1,0:T(8,128)(2,1)S(1)} async-done(((bf16[8,16,640]{2,1,0:T(8,128)(2,1)}), bf16[8,16,640]{2,1,0:T(8,128)(2,1)S(1)}, u32[]{:S(2)}, u32[]{:S(2)}) %all-to-all-start.2) | async-done | bytes 163872 | tf_op jit(solution)/shard_map/all_to_all | solution.py:1168
  91.9 1.1 chain.3
  93.0 3.4 %all-to-all-start.3 = ((bf16[8,16,640]{2,1,0:T(8,128)(2,1)}), bf16[8,16,640]{2,1,0:T(8,128)(2,1)S(1)}, u32[]{:S(2)}, u32[]{:S(2)}) async-start(bf16[8,16,640]{2,1,0:T(8,128)(2,1)} %chain.3), calls=%async_computation.3 | async-start | bytes 327680 | tf_op jit(solution)/shard_map/all_to_all | solution.py:1168
  96.4 6.8 %within_back.1 = (bf16[512,640]{1,0:T(8,128)(2,1)}, f32[512,128]{1,0:T(8,128)}, f32[512,256]{1,0:T(8,128)}) custom-call(s32[3]{0:T(128)} %pad_add_fusion.meta_ref, s32[4]{0:T(128)} %docs_ref.9, bf16[512,1280]{1,0:T(8,128)(2,1)} %get-tuple-element.73.dy_ref, bf16[512,640]{1,0:T(8,128)(2,1)} %get-tuple-element.74.edy_ref, ...), custom_call_target="tpu_custom_call" | custom-call | flops 10000000000 | bytes 6000000 | tf_op jit(solution)/shard_map/within_back/pallas_call | solution.py:836
  104.6 8.1 %grads_of.1 = (bf16[256,640]{1,0:T(8,128)(2,1)}, bf16[256,640]{1,0:T(8,128)(2,1)}, f32[256,384]{1,0:T(8,128)}, f32[256,384]{1,0:T(8,128)}, bf16[16,896]{1,0:T(8,128)(2,1)}) custom-call(s32[3]{0:T(128)} %pad_add_fusion.meta_ref, s32[4]{0:T(128)} %docs_ref.9, bf16[128,640]{1,0:T(8,128)(2,1)} %bitcast.18, f32[128,640]{1,0:T(8,128)} %get-tuple-element.71.late_ref, ...), custom_call_target="tpu_custom_call" | custom-call | flops 4000000000 | bytes 8000000 | tf_op jit(solution)/shard_map/grads_of/pallas_call | solution.py:995
  114.0 1.2 collective-permute-start.18
  119.3 1.6 %collective-permute-start.21 = (bf16[256,384]{1,0:T(8,128)(2,1)S(1)}, bf16[256,384]{1,0:T(8,128)(2,1)S(1)}, u32[]{:S(2)}, u32[]{:S(2)}) collective-permute-start(bf16[256,384]{1,0:T(8,128)(2,1)S(1)} %get-tuple-element.95), channel_id=1, source_target_pairs={{0,1},{1,0},{2,3},{3,2},{4,5},{5,4},{6,7},{7,6},{8,9},{9,8},{10,11... | collective-permute-start | bytes 589832 | tf_op jit(solution)/shard_map/ppermute | solution.py:1165
  120.8 2.9 %copy-done = bf16[1280,2560]{1,0:T(8,128)(2,1)S(1)} copy-done((bf16[1280,2560]{1,0:T(8,128)(2,1)S(1)}, bf16[1280,2560]{1,0:T(8,128)(2,1)}, u32[]{:S(2)}) %copy-start) | copy-done | bytes 6553624
  123.7 2.6 %half_sum.2.refs_0_ = f32[256,1280]{1,0:T(8,128)S(1)} custom-call(s32[2]{0:T(128)S(1)} %pad_add_fusion.3.meta_ref, bf16[256,640]{1,0:T(8,128)(2,1)S(1)} %copy-done.4, bf16[256,640]{1,0:T(8,128)(2,1)S(1)} %collective-permute-done.14.refs_1_, bf16[32,896]{1,0:T(8,128)(2,1)S(1)} %collective-permute-done.16.refs_2_.rim0_ref, bf16[1280,2560]{1,0:T(8,128)(2,1)S(1)} %copy-done, ...), custom_call_target="tpu_custom_call" | custom-call | flops 2000000000 | bytes 4000000 | tf_op jit(solution)/shard_map/half_sum/pallas_call | solution.py:1071
  126.3 5.8 %collective-permute-done.17.refs_1_ = bf16[256,640]{1,0:T(8,128)(2,1)S(1)} collective-permute-done((bf16[256,640]{1,0:T(8,128)(2,1)}, bf16[256,640]{1,0:T(8,128)(2,1)S(1)}, u32[]{:S(2)}, u32[]{:S(2)}) %collective-permute-start.17) | collective-permute-done | bytes 327712 | tf_op jit(solution)/shard_map/ppermute | solution.py:1165
  132.1 2.7 %half_sum.3.part_ref = f32[256,1280]{1,0:T(8,128)S(1)} custom-call(s32[2]{0:T(128)S(1)} %pad_add_fusion.2.meta_ref, f32[256,1280]{1,0:T(8,128)S(1)} %half_sum.2.refs_0_, bf16[256,640]{1,0:T(8,128)(2,1)S(1)} %collective-permute-done.17.refs_1_, bf16[256,640]{1,0:T(8,128)(2,1)S(1)} %collective-permute-done.18.refs_2_, ...), custom_call_target="tpu_custom_call" | custom-call | flops 2000000000 | bytes 4000000 | tf_op jit(solution)/shard_map/half_sum/pallas_call | solution.py:1071
  134.8 1.2 collective-permute-done.21.bc_recv_ref
  136.1 2.1 %last_half.1 = bf16[256,1280]{1,0:T(8,128)(2,1)} custom-call(s32[1]{0:T(128)} %bitcast.1.side_ref, f32[256,1280]{1,0:T(8,128)S(1)} %half_sum.3.part_ref, bf16[32,896]{1,0:T(8,128)(2,1)S(1)} %collective-permute-done.19.refs_3_.rim_ref, bf16[32,896]{1,0:T(8,128)(2,1)S(1)} %collective-permute-done.16.refs_2_.rim0_ref, ...), custom_call_target="tpu_custom_call" | custom-call | flops 500000000 | bytes 2000000 | tf_op jit(solution)/shard_map/last_half/pallas_call | solution.py:1125
  (103 shorter events, 17.2 us)
Async XLA Ops:
  1.4 12.9 %collective-permute-start.1 = (bf16[16,1280]{1,0:T(8,128)(2,1)S(1)}, bf16[16,1280]{1,0:T(8,128)(2,1)S(1)}, u32[]{:S(2)}, u32[]{:S(2)}) collective-permute-start(bf16[16,1280]{1,0:T(8,128)(2,1)S(1)} %slice.3), channel_id=1, source_target_pairs={{2,6},{6,10},{10,14},{14,18},{18,22},{22,26},{26,30},{3,7},{7,11},... | collective-permute-start | bytes 122888 | tf_op jit(solution)/shard_map/ppermute | solution.py:1175
  2.1 16.9 %collective-permute-start = (bf16[16,1280]{1,0:T(8,128)(2,1)S(1)}, bf16[16,1280]{1,0:T(8,128)(2,1)S(1)}, u32[]{:S(2)}, u32[]{:S(2)}) collective-permute-start(bf16[16,1280]{1,0:T(8,128)(2,1)S(1)} %slice.3), channel_id=1, source_target_pairs={{2,4},{6,8},{10,12},{14,16},{18,20},{22,24},{26,28},{3,5},{7,9},{1... | collective-permute-start | bytes 122888 | tf_op jit(solution)/shard_map/ppermute | solution.py:1174
  2.8 10.3 %copy-start.13 = (f32[20]{0:T(128)S(1)}, f32[20]{0:T(128)}, u32[]{:S(2)}) copy-start(f32[20]{0:T(128)} %param.18) | copy-start | bytes 244
  6.5 24.6 %collective-permute-start.7 = (bf16[256,384]{1,0:T(8,128)(2,1)}, bf16[256,384]{1,0:T(8,128)(2,1)S(1)}, u32[]{:S(2)}, u32[]{:S(2)}) collective-permute-start(bf16[256,384]{1,0:T(8,128)(2,1)} %get-tuple-element.55.own_ref), channel_id=1, source_target_pairs={{0,2},{2,0},{4,6},{6,4},{8,10},{10,8},{12,14},{14,12},{16,18},{18,... | collective-permute-start | bytes 589832 | tf_op jit(solution)/shard_map/ppermute | solution.py:1164
  11.0 8.0 %collective-permute-start.6 = (bf16[256,384]{1,0:T(8,128)(2,1)}, bf16[256,384]{1,0:T(8,128)(2,1)S(1)}, u32[]{:S(2)}, u32[]{:S(2)}) collective-permute-start(bf16[256,384]{1,0:T(8,128)(2,1)} %get-tuple-element.55.own_ref), channel_id=1, source_target_pairs={{0,1},{1,0},{2,3},{3,2},{4,5},{5,4},{6,7},{7,6},{8,9},{9,8},{10,11... | collective-permute-start | bytes 589832 | tf_op jit(solution)/shard_map/ppermute | solution.py:1165
  12.5 38.3 %collective-permute-start.9 = (bf16[256,256]{1,0:T(8,128)(2,1)}, bf16[256,256]{1,0:T(8,128)(2,1)S(1)}, u32[]{:S(2)}, u32[]{:S(2)}) collective-permute-start(bf16[256,256]{1,0:T(8,128)(2,1)} %get-tuple-element.63.own_low_ref), channel_id=1, source_target_pairs={{0,1},{1,0},{2,3},{3,2},{4,5},{5,4},{6,7},{7,6},{8,9},{9,8},{10,11... | collective-permute-start | bytes 393224 | tf_op jit(solution)/shard_map/ppermute | solution.py:1165
  14.3 22.5 %collective-permute-start.4 = (bf16[256,640]{1,0:T(8,128)(2,1)}, bf16[256,640]{1,0:T(8,128)(2,1)S(1)}, u32[]{:S(2)}, u32[]{:S(2)}) collective-permute-start(bf16[256,640]{1,0:T(8,128)(2,1)} %get-tuple-element.52), channel_id=1, source_target_pairs={{0,3},{1,2},{2,1},{3,0},{4,7},{5,6},{6,5},{7,4},{8,11},{9,10},{10,... | collective-permute-start | bytes 983048 | tf_op jit(solution)/shard_map/ppermute | solution.py:1166
  19.0 12.1 %collective-permute-start.8 = (bf16[256,384]{1,0:T(8,128)(2,1)S(1)}, bf16[256,384]{1,0:T(8,128)(2,1)S(1)}, u32[]{:S(2)}, u32[]{:S(2)}) collective-permute-start(bf16[256,384]{1,0:T(8,128)(2,1)S(1)} %collective-permute-done.6.xr_ref), channel_id=1, source_target_pairs={{0,2},{2,0},{4,6},{6,4},{8,10},{10,8},{12,14},{14,12},{16,18},{18,... | collective-permute-start | bytes 589832 | tf_op jit(solution)/shard_map/ppermute | solution.py:1164
  25.5 4.1 %collective-permute-start.5 = (bf16[16,896]{1,0:T(8,128)(2,1)}, bf16[16,896]{1,0:T(8,128)(2,1)S(1)}, u32[]{:S(2)}, u32[]{:S(2)}) collective-permute-start(bf16[16,896]{1,0:T(8,128)(2,1)} %get-tuple-element.54), channel_id=1, source_target_pairs={{0,1},{1,0},{2,3},{3,2},{4,5},{5,4},{6,7},{7,6},{8,9},{9,8},{10,11... | collective-permute-start | bytes 86024 | tf_op jit(solution)/shard_map/ppermute | solution.py:1165
  29.6 9.1 %collective-permute-start.2 = (bf16[256,640]{1,0:T(8,128)(2,1)}, bf16[256,640]{1,0:T(8,128)(2,1)S(1)}, u32[]{:S(2)}, u32[]{:S(2)}) collective-permute-start(bf16[256,640]{1,0:T(8,128)(2,1)} %get-tuple-element.50), channel_id=1, source_target_pairs={{0,1},{1,0},{2,3},{3,2},{4,5},{5,4},{6,7},{7,6},{8,9},{9,8},{10,11... | collective-permute-start | bytes 983048 | tf_op jit(solution)/shard_map/ppermute | solution.py:1165
  31.1 7.6 %collective-permute-start.3 = (bf16[256,640]{1,0:T(8,128)(2,1)}, bf16[256,640]{1,0:T(8,128)(2,1)S(1)}, u32[]{:S(2)}, u32[]{:S(2)}) collective-permute-start(bf16[256,640]{1,0:T(8,128)(2,1)} %get-tuple-element.51), channel_id=1, source_target_pairs={{0,2},{2,0},{4,6},{6,4},{8,10},{10,8},{12,14},{14,12},{16,18},{18,... | collective-permute-start | bytes 983048 | tf_op jit(solution)/shard_map/ppermute | solution.py:1164
  39.6 11.1 %copy-start.23 = (bf16[256,256]{1,0:T(8,128)(2,1)S(1)}, bf16[256,256]{1,0:T(8,128)(2,1)}, u32[]{:S(2)}) copy-start(bf16[256,256]{1,0:T(8,128)(2,1)} %get-tuple-element.63.own_low_ref) | copy-start | bytes 393220
  39.6 11.7 %copy-start.9 = (bf16[256,1280]{1,0:T(8,128)(2,1)S(1)}, bf16[256,1280]{1,0:T(8,128)(2,1)}, u32[]{:S(2)}) copy-start(bf16[256,1280]{1,0:T(8,128)(2,1)} %go_ref.1) | copy-start | bytes 1966084
  39.6 11.9 %copy-start.12 = (f32[1280]{0:T(1024)S(1)}, f32[1280]{0:T(1024)}, u32[]{:S(2)}) copy-start(f32[1280]{0:T(1024)} %param.19) | copy-start | bytes 15364
  45.8 12.7 %all-to-all-start = ((bf16[8,16,768]{2,1,0:T(8,128)(2,1)}), bf16[8,16,768]{2,1,0:T(8,128)(2,1)S(1)}, u32[]{:S(2)}, u32[]{:S(2)}) async-start(bf16[8,16,768]{2,1,0:T(8,128)(2,1)} %get-tuple-element.65), calls=%async_computation | async-start | bytes 393216 | tf_op jit(solution)/shard_map/all_to_all | solution.py:1168
  50.7 12.2 %collective-permute-start.10 = (bf16[256,256]{1,0:T(8,128)(2,1)S(1)}, bf16[256,256]{1,0:T(8,128)(2,1)S(1)}, u32[]{:S(2)}, u32[]{:S(2)}) collective-permute-start(bf16[256,256]{1,0:T(8,128)(2,1)S(1)} %copy-done.23), channel_id=1, source_target_pairs={{0,2},{2,0},{4,6},{6,4},{8,10},{10,8},{12,14},{14,12},{16,18},{18,... | collective-permute-start | bytes 393224 | tf_op jit(solution)/shard_map/ppermute | solution.py:1164
  50.8 12.2 %copy-start.24 = (bf16[256,256]{1,0:T(8,128)(2,1)}, bf16[256,256]{1,0:T(8,128)(2,1)S(1)}, u32[]{:S(2)}) copy-start(bf16[256,256]{1,0:T(8,128)(2,1)S(1)} %collective-permute-done.9.xr_low_ref) | copy-start | bytes 393220
  50.8 12.1 %collective-permute-start.11 = (bf16[256,256]{1,0:T(8,128)(2,1)S(1)}, bf16[256,256]{1,0:T(8,128)(2,1)S(1)}, u32[]{:S(2)}, u32[]{:S(2)}) collective-permute-start(bf16[256,256]{1,0:T(8,128)(2,1)S(1)} %collective-permute-done.9.xr_low_ref), channel_id=1, source_target_pairs={{0,2},{2,0},{4,6},{6,4},{8,10},{10,8},{12,14},{14,12},{16,18},{18,... | collective-permute-start | bytes 393224 | tf_op jit(solution)/shard_map/ppermute | solution.py:1164
  51.3 19.2 %collective-permute-start.12 = (bf16[256,640]{1,0:T(8,128)(2,1)S(1)}, bf16[256,640]{1,0:T(8,128)(2,1)S(1)}, u32[]{:S(2)}, u32[]{:S(2)}) collective-permute-start(bf16[256,640]{1,0:T(8,128)(2,1)S(1)} %constant_dynamic-slice_fusion), channel_id=1, source_target_pairs={{0,2},{2,0},{4,6},{6,4},{8,10},{10,8},{12,14},{14,12},{16,18},{18,... | collective-permute-start | bytes 983048 | tf_op jit(solution)/shard_map/ppermute | solution.py:1164
  59.6 11.0 %all-to-all-start.1 = ((bf16[8,16,640]{2,1,0:T(8,128)(2,1)}), bf16[8,16,640]{2,1,0:T(8,128)(2,1)S(1)}, u32[]{:S(2)}, u32[]{:S(2)}) async-start(bf16[8,16,640]{2,1,0:T(8,128)(2,1)} %chain.2), calls=%async_computation.1 | async-start | bytes 327680 | tf_op jit(solution)/shard_map/all_to_all | solution.py:1168
  78.4 13.5 %all-to-all-start.2 = ((bf16[8,16,640]{2,1,0:T(8,128)(2,1)}), bf16[8,16,640]{2,1,0:T(8,128)(2,1)S(1)}, u32[]{:S(2)}, u32[]{:S(2)}) async-start(bf16[8,16,640]{2,1,0:T(8,128)(2,1)} %get-tuple-element.70), calls=%async_computation.2 | async-start | bytes 327680 | tf_op jit(solution)/shard_map/all_to_all | solution.py:1168
  88.6 27.5 %collective-permute-start.13 = (bf16[256,640]{1,0:T(8,128)(2,1)S(1)}, bf16[256,640]{1,0:T(8,128)(2,1)S(1)}, u32[]{:S(2)}, u32[]{:S(2)}) collective-permute-start(bf16[256,640]{1,0:T(8,128)(2,1)S(1)} %copy-done.15), channel_id=1, source_target_pairs={{0,2},{2,0},{4,6},{6,4},{8,10},{10,8},{12,14},{14,12},{16,18},{18,... | collective-permute-start | bytes 983048 | tf_op jit(solution)/shard_map/ppermute | solution.py:1164
  93.0 10.9 %all-to-all-start.3 = ((bf16[8,16,640]{2,1,0:T(8,128)(2,1)}), bf16[8,16,640]{2,1,0:T(8,128)(2,1)S(1)}, u32[]{:S(2)}, u32[]{:S(2)}) async-start(bf16[8,16,640]{2,1,0:T(8,128)(2,1)} %chain.3), calls=%async_computation.3 | async-start | bytes 327680 | tf_op jit(solution)/shard_map/all_to_all | solution.py:1168
  104.6 12.2 %copy-start.6 = (bf16[256,640]{1,0:T(8,128)(2,1)S(1)}, bf16[256,640]{1,0:T(8,128)(2,1)}, u32[]{:S(2)}) copy-start(bf16[256,640]{1,0:T(8,128)(2,1)} %get-tuple-element.68) | copy-start | bytes 983044
  112.7 2.9 %collective-permute-start.15 = (bf16[16,896]{1,0:T(8,128)(2,1)}, bf16[16,896]{1,0:T(8,128)(2,1)S(1)}, u32[]{:S(2)}, u32[]{:S(2)}) collective-permute-start(bf16[16,896]{1,0:T(8,128)(2,1)} %get-tuple-element.91), channel_id=1, source_target_pairs={{0,2},{2,0},{4,6},{6,4},{8,10},{10,8},{12,14},{14,12},{16,18},{18,... | collective-permute-start | bytes 86024 | tf_op jit(solution)/shard_map/ppermute | solution.py:1164
  112.7 5.1 %collective-permute-start.20 = (f32[256,384]{1,0:T(8,128)}, f32[256,384]{1,0:T(8,128)S(1)}, u32[]{:S(2)}, u32[]{:S(2)}) collective-permute-start(f32[256,384]{1,0:T(8,128)} %get-tuple-element.93), channel_id=1, source_target_pairs={{0,2},{2,0},{4,6},{6,4},{8,10},{10,8},{12,14},{14,12},{16,18},{18,... | collective-permute-start | bytes 1179656 | tf_op jit(solution)/shard_map/ppermute | solution.py:1164
  114.0 18.1 %collective-permute-start.18 = (bf16[256,640]{1,0:T(8,128)(2,1)}, bf16[256,640]{1,0:T(8,128)(2,1)S(1)}, u32[]{:S(2)}, u32[]{:S(2)}) collective-permute-start(bf16[256,640]{1,0:T(8,128)(2,1)} %get-tuple-element.90), channel_id=1, source_target_pairs={{0,3},{1,2},{2,1},{3,0},{4,7},{5,6},{6,5},{7,4},{8,11},{9,10},{10,... | collective-permute-start | bytes 983048 | tf_op jit(solution)/shard_map/ppermute | solution.py:1166
  115.2 5.7 %collective-permute-start.14 = (bf16[256,640]{1,0:T(8,128)(2,1)}, bf16[256,640]{1,0:T(8,128)(2,1)S(1)}, u32[]{:S(2)}, u32[]{:S(2)}) collective-permute-start(bf16[256,640]{1,0:T(8,128)(2,1)} %get-tuple-element.90), channel_id=1, source_target_pairs={{0,2},{2,0},{4,6},{6,4},{8,10},{10,8},{12,14},{14,12},{16,18},{18,... | collective-permute-start | bytes 983048 | tf_op jit(solution)/shard_map/ppermute | solution.py:1164
  115.6 16.5 %collective-permute-start.17 = (bf16[256,640]{1,0:T(8,128)(2,1)}, bf16[256,640]{1,0:T(8,128)(2,1)S(1)}, u32[]{:S(2)}, u32[]{:S(2)}) collective-permute-start(bf16[256,640]{1,0:T(8,128)(2,1)} %get-tuple-element.89.refs_0_), channel_id=1, source_target_pairs={{0,1},{1,0},{2,3},{3,2},{4,5},{5,4},{6,7},{7,6},{8,9},{9,8},{10,11... | collective-permute-start | bytes 983048 | tf_op jit(solution)/shard_map/ppermute | solution.py:1165
  116.1 3.1 %collective-permute-start.16 = (bf16[32,896]{1,0:T(8,128)(2,1)S(1)}, bf16[32,896]{1,0:T(8,128)(2,1)S(1)}, u32[]{:S(2)}, u32[]{:S(2)}) collective-permute-start(bf16[32,896]{1,0:T(8,128)(2,1)S(1)} %constant_dynamic-update-slice_fusion), channel_id=1, source_target_pairs={{6,2},{10,6},{14,10},{18,14},{22,18},{26,22},{30,26},{7,3},{11,7},... | collective-permute-start | bytes 172040 | tf_op jit(solution)/shard_map/ppermute | solution.py:1236
  117.8 8.5 %collective-permute-start.19 = (bf16[32,896]{1,0:T(8,128)(2,1)S(1)}, bf16[32,896]{1,0:T(8,128)(2,1)S(1)}, u32[]{:S(2)}, u32[]{:S(2)}) collective-permute-start(bf16[32,896]{1,0:T(8,128)(2,1)S(1)} %constant_dynamic-update-slice_fusion), channel_id=1, source_target_pairs={{6,3},{7,2},{10,7},{11,6},{14,11},{15,10},{18,15},{19,14},{22,19},... | collective-permute-start | bytes 172040 | tf_op jit(solution)/shard_map/ppermute | solution.py:1237
  119.3 16.8 %collective-permute-start.21 = (bf16[256,384]{1,0:T(8,128)(2,1)S(1)}, bf16[256,384]{1,0:T(8,128)(2,1)S(1)}, u32[]{:S(2)}, u32[]{:S(2)}) collective-permute-start(bf16[256,384]{1,0:T(8,128)(2,1)S(1)} %get-tuple-element.95), channel_id=1, source_target_pairs={{0,1},{1,0},{2,3},{3,2},{4,5},{5,4},{6,7},{7,6},{8,9},{9,8},{10,11... | collective-permute-start | bytes 589832 | tf_op jit(solution)/shard_map/ppermute | solution.py:1165
  (22 other events, 78.6 us)

commit v3 on v2

--- a/solution.py
+++ b/solution.py
@@ -1231,6 +1231,7 @@
     g_x = by_x(g_mine)
     g_cross = by_both(g_other)
     g_core = by_core(g_other)
+    rim, g_core = lax.optimization_barrier((rim, g_core))
     rims = jnp.concatenate([rim, by_core(rim)], axis=0)
     back_perm = [(2 * i + 1, 2 * i - 1) for i in range(1, chips)]
     rim0 = lax.ppermute(rims, "ctx", back_perm)

time: 139 us -> 139 us (level)
  starting transfers between devices: 35.3 us -> 33.8 us
    ppermute x6, waiting for transfers between devices: 14.9 us -> 19.8 us  [by_chips(): by_x = lambda a: lax.ppermute(a, 'fsdp', pair)]
    all_to_all x4, waiting for transfers between devices: 10.3 us -> 5.75 us  [by_chips(): lax.all_to_all(a, 'ctx', 0, 0, axis_index_groups=groups)]
    ppermute x2, starting transfers between devices: 1.79 us -> 0.18 us  [by_chips(): by_both = lambda a: lax.ppermute(a, ('ctx', 'fsdp'), cross)]
  transfers between devices with their start and end apart: 26 -> 26, of which waited for: 8 -> 11; matrix products, arithmetic and copies ran while one was open for 3% -> 3% of each run, Pallas kernels for 40% -> 28%
where the time goes in v3:
time: 139 us; the launch traced here: 138 us
  Pallas kernels  63.7 us (46%)
  starting transfers between devices  33.8 us (24%)
  waiting for transfers between devices  26.3 us (19%)
  local copies, waits for them, and re-layouts  10.1 us (7%)
  other arithmetic  3.05 us (2%)
    ppermute x6, waiting for transfers between devices, by_chips(): by_x = lambda a: lax.ppermute(a, 'fsdp', pair)  19.8 us
    all_to_all x4, starting transfers between devices, by_chips(): lax.all_to_all(a, 'ctx', 0, 0, axis_index_groups=groups)  18.6 us
    unnamed x57, local copies, waits for them, and re-layouts  8.6 us
    pallas_call x1, Pallas kernels, grads_of(): pl.pallas_call(functools.partial(grads_kernel, doc_starts.shape[0], heads...  7.96 us
    pallas_call x1, Pallas kernels, outputs_of(): pl.pallas_call(functools.partial(out_kernel, heads), grid_spec=pltpu.Pref...  7.12 us
    pallas_call x1, Pallas kernels, within(): pl.pallas_call(functools.partial(within_kernel, doc_starts.shape[0], head...  6.83 us
    pallas_call x1, Pallas kernels, within_back(): pl.pallas_call(functools.partial(within_back_kernel, doc_starts.shape[0],...  6.8 us
    ppermute x6, starting transfers between devices, by_chips(): by_x = lambda a: lax.ppermute(a, 'fsdp', pair)  6.27 us
  transfers between devices with their start and end apart: 26, of which 11 were waited for; matrix products, arithmetic and copies ran while one was open for 3% of the time, Pallas kernels for 28%

profile of v3, /device:TPU:0, one launch (start us, length us, event | category | flops | bytes accessed | tf_op | source)
XLA Modules:
  0.0 138.0 jit_solution(996325661016594358)
XLA Ops:
  2.8 3.7 %lead_proj.1 = (bf16[256,640]{1,0:T(8,128)(2,1)}, bf16[256,384]{1,0:T(8,128)(2,1)}, bf16[256,256]{1,0:T(8,128)(2,1)}) custom-call(s32[1]{0:T(128)} %bitcast.6.meta_ref, bf16[256,1280]{1,0:T(8,128)(2,1)} %tok_hbm.3, bf16[1280,2560]{1,0:T(8,128)(2,1)} %refs_5_.1, bf16[1280,256]{1,0:T(8,128)(2,1)} %bcw_ref.1, bf16[40,1280]{1,0:T(8,128)(2,1)} %bitcast.15), custom_call_target="tpu_custom_call" | custom-call | flops 419430400 | bytes 3000000 | tf_op jit(solution)/shard_map/lead_proj/pallas_call | solution.py:284
  6.5 4.5 %collective-permute-start.7 = (bf16[256,384]{1,0:T(8,128)(2,1)}, bf16[256,384]{1,0:T(8,128)(2,1)S(1)}, u32[]{:S(2)}, u32[]{:S(2)}) collective-permute-start(bf16[256,384]{1,0:T(8,128)(2,1)} %get-tuple-element.57.own_ref), channel_id=1, source_target_pairs={{0,2},{2,0},{4,6},{6,4},{8,10},{10,8},{12,14},{14,12},{16,18},{18,... | collective-permute-start | bytes 589832 | tf_op jit(solution)/shard_map/ppermute | solution.py:1164
  11.0 1.5 %collective-permute-start.6 = (bf16[256,384]{1,0:T(8,128)(2,1)}, bf16[256,384]{1,0:T(8,128)(2,1)S(1)}, u32[]{:S(2)}, u32[]{:S(2)}) collective-permute-start(bf16[256,384]{1,0:T(8,128)(2,1)} %get-tuple-element.57.own_ref), channel_id=1, source_target_pairs={{0,1},{1,0},{2,3},{3,2},{4,5},{5,4},{6,7},{7,6},{8,9},{9,8},{10,11... | collective-permute-start | bytes 589832 | tf_op jit(solution)/shard_map/ppermute | solution.py:1165
  13.8 5.2 %collective-permute-done.6.xr_ref = bf16[256,384]{1,0:T(8,128)(2,1)S(1)} collective-permute-done((bf16[256,384]{1,0:T(8,128)(2,1)}, bf16[256,384]{1,0:T(8,128)(2,1)S(1)}, u32[]{:S(2)}, u32[]{:S(2)}) %collective-permute-start.6) | collective-permute-done | bytes 196640 | tf_op jit(solution)/shard_map/ppermute | solution.py:1165
  20.2 5.8 %rest_proj.1 = (bf16[256,640]{1,0:T(8,128)(2,1)}, bf16[256,640]{1,0:T(8,128)(2,1)}, bf16[256,640]{1,0:T(8,128)(2,1)}, bf16[16,896]{1,0:T(8,128)(2,1)}, bf16[16,896]{1,0:T(8,128)(2,1)}) custom-call(s32[3]{0:T(128)} %pad_add_fusion.1.meta_ref, bf16[256,1280]{1,0:T(8,128)(2,1)} %tok_hbm.3, bf16[1280,2560]{1,0:T(8,128)(2,1)} %refs_5_.1, ...), custom_call_target="tpu_custom_call" | custom-call | flops 1258291200 | bytes 6000000 | tf_op jit(solution)/shard_map/rest_proj/pallas_call | solution.py:342
  26.0 1.6 %collective-permute-start.5 = (bf16[16,896]{1,0:T(8,128)(2,1)}, bf16[16,896]{1,0:T(8,128)(2,1)S(1)}, u32[]{:S(2)}, u32[]{:S(2)}) collective-permute-start(bf16[16,896]{1,0:T(8,128)(2,1)} %get-tuple-element.56), channel_id=1, source_target_pairs={{0,1},{1,0},{2,3},{3,2},{4,5},{5,4},{6,7},{7,6},{8,9},{9,8},{10,11... | collective-permute-start | bytes 86024 | tf_op jit(solution)/shard_map/ppermute | solution.py:1165
  28.8 1.4 %collective-permute-done.5.rim_recv_ref = bf16[16,896]{1,0:T(8,128)(2,1)S(1)} collective-permute-done((bf16[16,896]{1,0:T(8,128)(2,1)}, bf16[16,896]{1,0:T(8,128)(2,1)S(1)}, u32[]{:S(2)}, u32[]{:S(2)}) %collective-permute-start.5) | collective-permute-done | bytes 28704 | tf_op jit(solution)/shard_map/ppermute | solution.py:1165
  31.0 4.9 %shared_maps.1 = (bf16[512,256]{1,0:T(8,128)(2,1)}, f32[512,256]{1,0:T(8,128)}, f32[512,128]{1,0:T(8,128)}, f32[512,128]{1,0:T(8,128)}, f32[512,128]{1,0:T(8,128...) custom-call(s32[3]{0:T(128)} %pad_add_fusion.meta_ref, ...), custom_call_target="tpu_custom_call" | custom-call | flops 4000000000 | bytes 4000000 | tf_op jit(solution)/shard_map/shared_maps/pallas_call | solution.py:448
  35.9 2.3 %collective-permute-done.2.xr_ref = bf16[256,640]{1,0:T(8,128)(2,1)S(1)} collective-permute-done((bf16[256,640]{1,0:T(8,128)(2,1)}, bf16[256,640]{1,0:T(8,128)(2,1)S(1)}, u32[]{:S(2)}, u32[]{:S(2)}) %collective-permute-start.2) | collective-permute-done | bytes 327712 | tf_op jit(solution)/shard_map/ppermute | solution.py:1165
  39.1 6.2 %inner_maps.1 = (f32[512,640]{1,0:T(8,128)}, bf16[512,640]{1,0:T(8,128)(2,1)}, f32[2,128,640]{2,1,0:T(8,128)}, bf16[8,16,768]{2,1,0:T(8,128)(2,1)}) custom-call(s32[3]{0:T(128)} %pad_add_fusion.meta_ref, s32[4]{0:T(128)} %docs_ref.9, bf16[256,640]{1,0:T(8,128)(2,1)} %get-tuple-element.51.own_ref, bf16[256,640]{1,0:T(8,128)(2,1)} %copy-done.18, ...), custom_call_target="tpu_custom_call" | custom-call | flops 4000000000 | bytes 4000000 | tf_op jit(solution)/shard_map/inner_maps/pallas_call | solution.py:561
  45.4 4.9 %all-to-all-start = ((bf16[8,16,768]{2,1,0:T(8,128)(2,1)}), bf16[8,16,768]{2,1,0:T(8,128)(2,1)S(1)}, u32[]{:S(2)}, u32[]{:S(2)}) async-start(bf16[8,16,768]{2,1,0:T(8,128)(2,1)} %get-tuple-element.67), calls=%async_computation | async-start | bytes 393216 | tf_op jit(solution)/shard_map/all_to_all | solution.py:1168
  50.9 4.4 %collective-permute-done.9.xr_low_ref = bf16[256,256]{1,0:T(8,128)(2,1)S(1)} collective-permute-done((bf16[256,256]{1,0:T(8,128)(2,1)S(1)}, bf16[256,256]{1,0:T(8,128)(2,1)S(1)}, u32[]{:S(2)}, u32[]{:S(2)}) %collective-permute-start.9) | collective-permute-done | bytes 131104 | tf_op jit(solution)/shard_map/ppermute | solution.py:1165
  56.5 1.5 %all-to-all-done.recv_ref.keep_ref = bf16[8,16,768]{2,1,0:T(8,128)(2,1)S(1)} async-done(((bf16[8,16,768]{2,1,0:T(8,128)(2,1)}), bf16[8,16,768]{2,1,0:T(8,128)(2,1)S(1)}, u32[]{:S(2)}, u32[]{:S(2)}) %all-to-all-start) | async-done | bytes 196640 | tf_op jit(solution)/shard_map/all_to_all | solution.py:1168
  58.0 1.1 chain.2
  59.1 4.4 %all-to-all-start.1 = ((bf16[8,16,640]{2,1,0:T(8,128)(2,1)}), bf16[8,16,640]{2,1,0:T(8,128)(2,1)S(1)}, u32[]{:S(2)}, u32[]{:S(2)}) async-start(bf16[8,16,640]{2,1,0:T(8,128)(2,1)} %chain.2), calls=%async_computation.1 | async-start | bytes 327680 | tf_op jit(solution)/shard_map/all_to_all | solution.py:1168
  64.2 6.8 %within.1 = (f32[512,640]{1,0:T(8,128)}, f32[2,256,256]{2,1,0:T(8,128)}) custom-call(s32[3]{0:T(128)} %pad_add_fusion.meta_ref, s32[4]{0:T(128)} %docs_ref.9, bf16[512,640]{1,0:T(8,128)(2,1)} %get-tuple-element.62.xd_ref, f32[512,128]{1,0:T(8,128)} %get-tuple-element.63.ramp_ref, f32[2,16,256]{2,1,0:T(8,128)} %get-tuple-element.64.rampt_ref, ...), custom_call_target="tpu_custom_call" | custom-call | flops 6000000000 | bytes 4000000 | tf_op jit(solution)/shard_map/within/pallas_call | solution.py:646
  71.9 7.1 %outputs_of.1 = (bf16[256,640]{1,0:T(8,128)(2,1)}, bf16[256,640]{1,0:T(8,128)(2,1)}, bf16[512,1280]{1,0:T(8,128)(2,1)}, bf16[512,640]{1,0:T(8,128)(2,1)}, f32[51...) custom-call(s32[3]{0:T(128)} %pad_add_fusion.meta_ref, ...), custom_call_target="tpu_custom_call" | custom-call | flops 4000000000 | bytes 4000000 | tf_op jit(solution)/shard_map/outputs_of/pallas_call | solution.py:770
  79.0 6.0 %all-to-all-start.2 = ((bf16[8,16,640]{2,1,0:T(8,128)(2,1)}), bf16[8,16,640]{2,1,0:T(8,128)(2,1)S(1)}, u32[]{:S(2)}, u32[]{:S(2)}) async-start(bf16[8,16,640]{2,1,0:T(8,128)(2,1)} %get-tuple-element.72), calls=%async_computation.2 | async-start | bytes 327680 | tf_op jit(solution)/shard_map/all_to_all | solution.py:1168
  85.0 4.1 %slopes_of.1 = (bf16[512,640]{1,0:T(8,128)(2,1)}, bf16[512,640]{1,0:T(8,128)(2,1)}, bf16[512,640]{1,0:T(8,128)(2,1)}, bf16[512,640]{1,0:T(8,128)(2,1)}, bf16[512,640]{1,0:T(8,128)(2,1)}) custom-call(f32[512,640]{1,0:T(8,128)} %get-tuple-element.78.pre_ref, bf16[512,128]{1,0:T(8,128)(2,1)} %get-tuple-element.59.dpk_ref, ...), custom_call_target="tpu_custom_call" | custom-call | flops 2000000000 | bytes 4000000 | tf_op jit(solution)/shard_map/slopes_of/pallas_call | solution.py:876
  89.1 3.4 %all-to-all-done.2.recv_ref = bf16[8,16,640]{2,1,0:T(8,128)(2,1)S(1)} async-done(((bf16[8,16,640]{2,1,0:T(8,128)(2,1)}), bf16[8,16,640]{2,1,0:T(8,128)(2,1)S(1)}, u32[]{:S(2)}, u32[]{:S(2)}) %all-to-all-start.2) | async-done | bytes 163872 | tf_op jit(solution)/shard_map/all_to_all | solution.py:1168
  92.5 1.1 chain.3
  93.6 3.4 %all-to-all-start.3 = ((bf16[8,16,640]{2,1,0:T(8,128)(2,1)}), bf16[8,16,640]{2,1,0:T(8,128)(2,1)S(1)}, u32[]{:S(2)}, u32[]{:S(2)}) async-start(bf16[8,16,640]{2,1,0:T(8,128)(2,1)} %chain.3), calls=%async_computation.3 | async-start | bytes 327680 | tf_op jit(solution)/shard_map/all_to_all | solution.py:1168
  97.0 6.8 %within_back.1 = (bf16[512,640]{1,0:T(8,128)(2,1)}, f32[512,128]{1,0:T(8,128)}, f32[512,256]{1,0:T(8,128)}) custom-call(s32[3]{0:T(128)} %pad_add_fusion.meta_ref, s32[4]{0:T(128)} %docs_ref.9, bf16[512,1280]{1,0:T(8,128)(2,1)} %get-tuple-element.75.dy_ref, bf16[512,640]{1,0:T(8,128)(2,1)} %get-tuple-element.76.edy_ref, ...), custom_call_target="tpu_custom_call" | custom-call | flops 10000000000 | bytes 6000000 | tf_op jit(solution)/shard_map/within_back/pallas_call | solution.py:836
  105.2 8.0 %grads_of.1 = (bf16[256,640]{1,0:T(8,128)(2,1)}, bf16[256,640]{1,0:T(8,128)(2,1)}, f32[256,384]{1,0:T(8,128)}, f32[256,384]{1,0:T(8,128)}, bf16[16,896]{1,0:T(8,128)(2,1)}) custom-call(s32[3]{0:T(128)} %pad_add_fusion.meta_ref, s32[4]{0:T(128)} %docs_ref.9, bf16[128,640]{1,0:T(8,128)(2,1)} %bitcast.18, f32[128,640]{1,0:T(8,128)} %get-tuple-element.73.late_ref, ...), custom_call_target="tpu_custom_call" | custom-call | flops 4000000000 | bytes 8000000 | tf_op jit(solution)/shard_map/grads_of/pallas_call | solution.py:995
  114.1 1.5 %collective-permute-start.17 = (bf16[256,640]{1,0:T(8,128)(2,1)}, bf16[256,640]{1,0:T(8,128)(2,1)S(1)}, u32[]{:S(2)}, u32[]{:S(2)}) collective-permute-start(bf16[256,640]{1,0:T(8,128)(2,1)} %get-tuple-element.91.refs_0_), channel_id=1, source_target_pairs={{0,1},{1,0},{2,3},{3,2},{4,5},{5,4},{6,7},{7,6},{8,9},{9,8},{10,11... | collective-permute-start | bytes 983048 | tf_op jit(solution)/shard_map/ppermute | solution.py:1165
  118.2 1.0 maximum_select_fusion
  121.3 2.9 %copy-done = bf16[1280,2560]{1,0:T(8,128)(2,1)S(1)} copy-done((bf16[1280,2560]{1,0:T(8,128)(2,1)S(1)}, bf16[1280,2560]{1,0:T(8,128)(2,1)}, u32[]{:S(2)}) %copy-start) | copy-done | bytes 6553624
  124.1 2.6 %half_sum.2.refs_0_ = f32[256,1280]{1,0:T(8,128)S(1)} custom-call(s32[2]{0:T(128)S(1)} %pad_add_fusion.3.meta_ref, bf16[256,640]{1,0:T(8,128)(2,1)S(1)} %copy-done.4, bf16[256,640]{1,0:T(8,128)(2,1)S(1)} %collective-permute-done.14.refs_1_, bf16[32,896]{1,0:T(8,128)(2,1)S(1)} %collective-permute-done.16.refs_2_.rim0_ref, bf16[1280,2560]{1,0:T(8,128)(2,1)S(1)} %copy-done, ...), custom_call_target="tpu_custom_call" | custom-call | flops 2000000000 | bytes 4000000 | tf_op jit(solution)/shard_map/half_sum/pallas_call | solution.py:1071
  126.7 5.2 %collective-permute-done.17.refs_1_ = bf16[256,640]{1,0:T(8,128)(2,1)S(1)} collective-permute-done((bf16[256,640]{1,0:T(8,128)(2,1)}, bf16[256,640]{1,0:T(8,128)(2,1)S(1)}, u32[]{:S(2)}, u32[]{:S(2)}) %collective-permute-start.17) | collective-permute-done | bytes 327712 | tf_op jit(solution)/shard_map/ppermute | solution.py:1165
  132.0 2.7 %half_sum.3.part_ref = f32[256,1280]{1,0:T(8,128)S(1)} custom-call(s32[2]{0:T(128)S(1)} %pad_add_fusion.2.meta_ref, f32[256,1280]{1,0:T(8,128)S(1)} %half_sum.2.refs_0_, bf16[256,640]{1,0:T(8,128)(2,1)S(1)} %collective-permute-done.17.refs_1_, bf16[256,640]{1,0:T(8,128)(2,1)S(1)} %collective-permute-done.18.refs_2_, ...), custom_call_target="tpu_custom_call" | custom-call | flops 2000000000 | bytes 4000000 | tf_op jit(solution)/shard_map/half_sum/pallas_call | solution.py:1071
  134.7 1.3 collective-permute-done.21.bc_recv_ref
  136.0 2.1 %last_half.1 = bf16[256,1280]{1,0:T(8,128)(2,1)} custom-call(s32[1]{0:T(128)} %bitcast.1.side_ref, f32[256,1280]{1,0:T(8,128)S(1)} %half_sum.3.part_ref, bf16[32,896]{1,0:T(8,128)(2,1)S(1)} %collective-permute-done.19.refs_3_.rim_ref, bf16[32,896]{1,0:T(8,128)(2,1)S(1)} %collective-permute-done.16.refs_2_.rim0_ref, ...), custom_call_target="tpu_custom_call" | custom-call | flops 500000000 | bytes 2000000 | tf_op jit(solution)/shard_map/last_half/pallas_call | solution.py:1125
  (103 shorter events, 17.7 us)
Async XLA Ops:
  1.4 17.6 %collective-permute-start.1 = (bf16[16,1280]{1,0:T(8,128)(2,1)S(1)}, bf16[16,1280]{1,0:T(8,128)(2,1)S(1)}, u32[]{:S(2)}, u32[]{:S(2)}) collective-permute-start(bf16[16,1280]{1,0:T(8,128)(2,1)S(1)} %slice.3), channel_id=1, source_target_pairs={{2,6},{6,10},{10,14},{14,18},{18,22},{22,26},{26,30},{3,7},{7,11},... | collective-permute-start | bytes 122888 | tf_op jit(solution)/shard_map/ppermute | solution.py:1175
  2.1 16.9 %collective-permute-start = (bf16[16,1280]{1,0:T(8,128)(2,1)S(1)}, bf16[16,1280]{1,0:T(8,128)(2,1)S(1)}, u32[]{:S(2)}, u32[]{:S(2)}) collective-permute-start(bf16[16,1280]{1,0:T(8,128)(2,1)S(1)} %slice.3), channel_id=1, source_target_pairs={{2,4},{6,8},{10,12},{14,16},{18,20},{22,24},{26,28},{3,5},{7,9},{1... | collective-permute-start | bytes 122888 | tf_op jit(solution)/shard_map/ppermute | solution.py:1174
  2.8 9.7 %copy-start.13 = (f32[20]{0:T(128)S(1)}, f32[20]{0:T(128)}, u32[]{:S(2)}) copy-start(f32[20]{0:T(128)} %param.18) | copy-start | bytes 244
  2.8 9.7 %copy-start.14 = (f32[20]{0:T(128)S(1)}, f32[20]{0:T(128)}, u32[]{:S(2)}) copy-start(f32[20]{0:T(128)} %param.17) | copy-start | bytes 244
  6.5 23.7 %collective-permute-start.7 = (bf16[256,384]{1,0:T(8,128)(2,1)}, bf16[256,384]{1,0:T(8,128)(2,1)S(1)}, u32[]{:S(2)}, u32[]{:S(2)}) collective-permute-start(bf16[256,384]{1,0:T(8,128)(2,1)} %get-tuple-element.57.own_ref), channel_id=1, source_target_pairs={{0,2},{2,0},{4,6},{6,4},{8,10},{10,8},{12,14},{14,12},{16,18},{18,... | collective-permute-start | bytes 589832 | tf_op jit(solution)/shard_map/ppermute | solution.py:1164
  11.0 8.0 %collective-permute-start.6 = (bf16[256,384]{1,0:T(8,128)(2,1)}, bf16[256,384]{1,0:T(8,128)(2,1)S(1)}, u32[]{:S(2)}, u32[]{:S(2)}) collective-permute-start(bf16[256,384]{1,0:T(8,128)(2,1)} %get-tuple-element.57.own_ref), channel_id=1, source_target_pairs={{0,1},{1,0},{2,3},{3,2},{4,5},{5,4},{6,7},{7,6},{8,9},{9,8},{10,11... | collective-permute-start | bytes 589832 | tf_op jit(solution)/shard_map/ppermute | solution.py:1165
  12.5 23.4 %collective-permute-start.4 = (bf16[256,640]{1,0:T(8,128)(2,1)}, bf16[256,640]{1,0:T(8,128)(2,1)S(1)}, u32[]{:S(2)}, u32[]{:S(2)}) collective-permute-start(bf16[256,640]{1,0:T(8,128)(2,1)} %get-tuple-element.54), channel_id=1, source_target_pairs={{0,3},{1,2},{2,1},{3,0},{4,7},{5,6},{6,5},{7,4},{8,11},{9,10},{10,... | collective-permute-start | bytes 983048 | tf_op jit(solution)/shard_map/ppermute | solution.py:1166
  19.0 11.2 %collective-permute-start.8 = (bf16[256,384]{1,0:T(8,128)(2,1)S(1)}, bf16[256,384]{1,0:T(8,128)(2,1)S(1)}, u32[]{:S(2)}, u32[]{:S(2)}) collective-permute-start(bf16[256,384]{1,0:T(8,128)(2,1)S(1)} %collective-permute-done.6.xr_ref), channel_id=1, source_target_pairs={{0,2},{2,0},{4,6},{6,4},{8,10},{10,8},{12,14},{14,12},{16,18},{18,... | collective-permute-start | bytes 589832 | tf_op jit(solution)/shard_map/ppermute | solution.py:1164
  26.0 4.1 %collective-permute-start.5 = (bf16[16,896]{1,0:T(8,128)(2,1)}, bf16[16,896]{1,0:T(8,128)(2,1)S(1)}, u32[]{:S(2)}, u32[]{:S(2)}) collective-permute-start(bf16[16,896]{1,0:T(8,128)(2,1)} %get-tuple-element.56), channel_id=1, source_target_pairs={{0,1},{1,0},{2,3},{3,2},{4,5},{5,4},{6,7},{7,6},{8,9},{9,8},{10,11... | collective-permute-start | bytes 86024 | tf_op jit(solution)/shard_map/ppermute | solution.py:1165
  28.3 10.0 %collective-permute-start.2 = (bf16[256,640]{1,0:T(8,128)(2,1)}, bf16[256,640]{1,0:T(8,128)(2,1)S(1)}, u32[]{:S(2)}, u32[]{:S(2)}) collective-permute-start(bf16[256,640]{1,0:T(8,128)(2,1)} %get-tuple-element.52), channel_id=1, source_target_pairs={{0,1},{1,0},{2,3},{3,2},{4,5},{5,4},{6,7},{7,6},{8,9},{9,8},{10,11... | collective-permute-start | bytes 983048 | tf_op jit(solution)/shard_map/ppermute | solution.py:1165
  30.2 8.1 %collective-permute-start.3 = (bf16[256,640]{1,0:T(8,128)(2,1)}, bf16[256,640]{1,0:T(8,128)(2,1)S(1)}, u32[]{:S(2)}, u32[]{:S(2)}) collective-permute-start(bf16[256,640]{1,0:T(8,128)(2,1)} %get-tuple-element.53), channel_id=1, source_target_pairs={{0,2},{2,0},{4,6},{6,4},{8,10},{10,8},{12,14},{14,12},{16,18},{18,... | collective-permute-start | bytes 983048 | tf_op jit(solution)/shard_map/ppermute | solution.py:1164
  39.1 11.1 %copy-start.23 = (bf16[256,256]{1,0:T(8,128)(2,1)S(1)}, bf16[256,256]{1,0:T(8,128)(2,1)}, u32[]{:S(2)}) copy-start(bf16[256,256]{1,0:T(8,128)(2,1)} %get-tuple-element.65.own_low_ref) | copy-start | bytes 393220
  39.1 16.2 %copy-start.9 = (bf16[256,1280]{1,0:T(8,128)(2,1)S(1)}, bf16[256,1280]{1,0:T(8,128)(2,1)}, u32[]{:S(2)}) copy-start(bf16[256,1280]{1,0:T(8,128)(2,1)} %go_ref.1) | copy-start | bytes 1966084
  39.1 16.8 %copy-start.12 = (f32[1280]{0:T(1024)S(1)}, f32[1280]{0:T(1024)}, u32[]{:S(2)}) copy-start(f32[1280]{0:T(1024)} %param.19) | copy-start | bytes 15364
  45.4 12.7 %all-to-all-start = ((bf16[8,16,768]{2,1,0:T(8,128)(2,1)}), bf16[8,16,768]{2,1,0:T(8,128)(2,1)S(1)}, u32[]{:S(2)}, u32[]{:S(2)}) async-start(bf16[8,16,768]{2,1,0:T(8,128)(2,1)} %get-tuple-element.67), calls=%async_computation | async-start | bytes 393216 | tf_op jit(solution)/shard_map/all_to_all | solution.py:1168
  50.3 5.0 %collective-permute-start.9 = (bf16[256,256]{1,0:T(8,128)(2,1)S(1)}, bf16[256,256]{1,0:T(8,128)(2,1)S(1)}, u32[]{:S(2)}, u32[]{:S(2)}) collective-permute-start(bf16[256,256]{1,0:T(8,128)(2,1)S(1)} %copy-done.23), channel_id=1, source_target_pairs={{0,1},{1,0},{2,3},{3,2},{4,5},{5,4},{6,7},{7,6},{8,9},{9,8},{10,11... | collective-permute-start | bytes 393224 | tf_op jit(solution)/shard_map/ppermute | solution.py:1165
  50.9 12.6 %collective-permute-start.10 = (bf16[256,256]{1,0:T(8,128)(2,1)S(1)}, bf16[256,256]{1,0:T(8,128)(2,1)S(1)}, u32[]{:S(2)}, u32[]{:S(2)}) collective-permute-start(bf16[256,256]{1,0:T(8,128)(2,1)S(1)} %copy-done.23), channel_id=1, source_target_pairs={{0,2},{2,0},{4,6},{6,4},{8,10},{10,8},{12,14},{14,12},{16,18},{18,... | collective-permute-start | bytes 393224 | tf_op jit(solution)/shard_map/ppermute | solution.py:1164
  55.3 8.2 %collective-permute-start.11 = (bf16[256,256]{1,0:T(8,128)(2,1)S(1)}, bf16[256,256]{1,0:T(8,128)(2,1)S(1)}, u32[]{:S(2)}, u32[]{:S(2)}) collective-permute-start(bf16[256,256]{1,0:T(8,128)(2,1)S(1)} %collective-permute-done.9.xr_low_ref), channel_id=1, source_target_pairs={{0,2},{2,0},{4,6},{6,4},{8,10},{10,8},{12,14},{14,12},{16,18},{18,... | collective-permute-start | bytes 393224 | tf_op jit(solution)/shard_map/ppermute | solution.py:1164
  55.4 15.7 %collective-permute-start.12 = (bf16[256,640]{1,0:T(8,128)(2,1)S(1)}, bf16[256,640]{1,0:T(8,128)(2,1)S(1)}, u32[]{:S(2)}, u32[]{:S(2)}) collective-permute-start(bf16[256,640]{1,0:T(8,128)(2,1)S(1)} %constant_dynamic-slice_fusion), channel_id=1, source_target_pairs={{0,2},{2,0},{4,6},{6,4},{8,10},{10,8},{12,14},{14,12},{16,18},{18,... | collective-permute-start | bytes 983048 | tf_op jit(solution)/shard_map/ppermute | solution.py:1164
  59.1 12.0 %all-to-all-start.1 = ((bf16[8,16,640]{2,1,0:T(8,128)(2,1)}), bf16[8,16,640]{2,1,0:T(8,128)(2,1)S(1)}, u32[]{:S(2)}, u32[]{:S(2)}) async-start(bf16[8,16,640]{2,1,0:T(8,128)(2,1)} %chain.2), calls=%async_computation.1 | async-start | bytes 327680 | tf_op jit(solution)/shard_map/all_to_all | solution.py:1168
  79.0 13.6 %all-to-all-start.2 = ((bf16[8,16,640]{2,1,0:T(8,128)(2,1)}), bf16[8,16,640]{2,1,0:T(8,128)(2,1)S(1)}, u32[]{:S(2)}, u32[]{:S(2)}) async-start(bf16[8,16,640]{2,1,0:T(8,128)(2,1)} %get-tuple-element.72), calls=%async_computation.2 | async-start | bytes 327680 | tf_op jit(solution)/shard_map/all_to_all | solution.py:1168
  93.6 10.9 %all-to-all-start.3 = ((bf16[8,16,640]{2,1,0:T(8,128)(2,1)}), bf16[8,16,640]{2,1,0:T(8,128)(2,1)S(1)}, u32[]{:S(2)}, u32[]{:S(2)}) async-start(bf16[8,16,640]{2,1,0:T(8,128)(2,1)} %chain.3), calls=%async_computation.3 | async-start | bytes 327680 | tf_op jit(solution)/shard_map/all_to_all | solution.py:1168
  105.2 13.1 %copy-start.6 = (bf16[256,640]{1,0:T(8,128)(2,1)S(1)}, bf16[256,640]{1,0:T(8,128)(2,1)}, u32[]{:S(2)}) copy-start(bf16[256,640]{1,0:T(8,128)(2,1)} %get-tuple-element.70) | copy-start | bytes 983044
  113.1 2.6 %collective-permute-start.14 = (bf16[256,640]{1,0:T(8,128)(2,1)}, bf16[256,640]{1,0:T(8,128)(2,1)S(1)}, u32[]{:S(2)}, u32[]{:S(2)}) collective-permute-start(bf16[256,640]{1,0:T(8,128)(2,1)} %get-tuple-element.93), channel_id=1, source_target_pairs={{0,2},{2,0},{4,6},{6,4},{8,10},{10,8},{12,14},{14,12},{16,18},{18,... | collective-permute-start | bytes 983048 | tf_op jit(solution)/shard_map/ppermute | solution.py:1164
  113.3 4.9 %collective-permute-start.13 = (bf16[256,640]{1,0:T(8,128)(2,1)S(1)}, bf16[256,640]{1,0:T(8,128)(2,1)S(1)}, u32[]{:S(2)}, u32[]{:S(2)}) collective-permute-start(bf16[256,640]{1,0:T(8,128)(2,1)S(1)} %copy-done.15), channel_id=1, source_target_pairs={{0,2},{2,0},{4,6},{6,4},{8,10},{10,8},{12,14},{14,12},{16,18},{18,... | collective-permute-start | bytes 983048 | tf_op jit(solution)/shard_map/ppermute | solution.py:1164
  113.9 18.1 %collective-permute-start.18 = (bf16[256,640]{1,0:T(8,128)(2,1)}, bf16[256,640]{1,0:T(8,128)(2,1)S(1)}, u32[]{:S(2)}, u32[]{:S(2)}) collective-permute-start(bf16[256,640]{1,0:T(8,128)(2,1)} %get-tuple-element.93), channel_id=1, source_target_pairs={{0,3},{1,2},{2,1},{3,0},{4,7},{5,6},{6,5},{7,4},{8,11},{9,10},{10,... | collective-permute-start | bytes 983048 | tf_op jit(solution)/shard_map/ppermute | solution.py:1166
  114.1 17.9 %collective-permute-start.17 = (bf16[256,640]{1,0:T(8,128)(2,1)}, bf16[256,640]{1,0:T(8,128)(2,1)S(1)}, u32[]{:S(2)}, u32[]{:S(2)}) collective-permute-start(bf16[256,640]{1,0:T(8,128)(2,1)} %get-tuple-element.91.refs_0_), channel_id=1, source_target_pairs={{0,1},{1,0},{2,3},{3,2},{4,5},{5,4},{6,7},{7,6},{8,9},{9,8},{10,11... | collective-permute-start | bytes 983048 | tf_op jit(solution)/shard_map/ppermute | solution.py:1165
  115.5 4.4 %collective-permute-start.20 = (f32[256,384]{1,0:T(8,128)}, f32[256,384]{1,0:T(8,128)S(1)}, u32[]{:S(2)}, u32[]{:S(2)}) collective-permute-start(f32[256,384]{1,0:T(8,128)} %get-tuple-element.97), channel_id=1, source_target_pairs={{0,2},{2,0},{4,6},{6,4},{8,10},{10,8},{12,14},{14,12},{16,18},{18,... | collective-permute-start | bytes 1179656 | tf_op jit(solution)/shard_map/ppermute | solution.py:1164
  115.7 1.8 %collective-permute-start.15 = (bf16[16,896]{1,0:T(8,128)(2,1)}, bf16[16,896]{1,0:T(8,128)(2,1)S(1)}, u32[]{:S(2)}, u32[]{:S(2)}) collective-permute-start(bf16[16,896]{1,0:T(8,128)(2,1)} %get-tuple-element.95), channel_id=1, source_target_pairs={{0,2},{2,0},{4,6},{6,4},{8,10},{10,8},{12,14},{14,12},{16,18},{18,... | collective-permute-start | bytes 86024 | tf_op jit(solution)/shard_map/ppermute | solution.py:1164
  117.5 3.7 %collective-permute-start.16 = (bf16[32,896]{1,0:T(8,128)(2,1)S(1)}, bf16[32,896]{1,0:T(8,128)(2,1)S(1)}, u32[]{:S(2)}, u32[]{:S(2)}) collective-permute-start(bf16[32,896]{1,0:T(8,128)(2,1)S(1)} %constant_dynamic-update-slice_fusion), channel_id=1, source_target_pairs={{6,2},{10,6},{14,10},{18,14},{22,18},{26,22},{30,26},{7,3},{11,7},... | collective-permute-start | bytes 172040 | tf_op jit(solution)/shard_map/ppermute | solution.py:1237
  119.2 12.7 %collective-permute-start.19 = (bf16[32,896]{1,0:T(8,128)(2,1)S(1)}, bf16[32,896]{1,0:T(8,128)(2,1)S(1)}, u32[]{:S(2)}, u32[]{:S(2)}) collective-permute-start(bf16[32,896]{1,0:T(8,128)(2,1)S(1)} %constant_dynamic-update-slice_fusion), channel_id=1, source_target_pairs={{6,3},{7,2},{10,7},{11,6},{14,11},{15,10},{18,15},{19,14},{22,19},... | collective-permute-start | bytes 172040 | tf_op jit(solution)/shard_map/ppermute | solution.py:1238
  120.7 15.3 %collective-permute-start.21 = (bf16[256,384]{1,0:T(8,128)(2,1)S(1)}, bf16[256,384]{1,0:T(8,128)(2,1)S(1)}, u32[]{:S(2)}, u32[]{:S(2)}) collective-permute-start(bf16[256,384]{1,0:T(8,128)(2,1)S(1)} %get-tuple-element.99), channel_id=1, source_target_pairs={{0,1},{1,0},{2,3},{3,2},{4,5},{5,4},{6,7},{7,6},{8,9},{9,8},{10,11... | collective-permute-start | bytes 589832 | tf_op jit(solution)/shard_map/ppermute | solution.py:1165
  (22 other events, 77.3 us)

commit v4 on v3

--- a/solution.py
+++ b/solution.py
@@ -257,7 +257,7 @@
 ):
     width = w_ref.shape[1]
     get_tok = fetch(tok_hbm, tok_ref, sems.at[0])
-    get_w = fetch(columns(w_hbm, meta_ref[0], width), w_ref, sems.at[1])
+    get_w = fetch(columns(w_hbm, (1 - meta_ref[1]) * 2 + 1 - meta_ref[0], width), w_ref, sems.at[1])
     get_bcw = fetch(bcw_hbm, bcw_ref, sems.at[2])
     get_dtw = fetch(dtw_hbm, dtw_ref, sems.at[3])
     get_tok.wait()
@@ -313,7 +313,9 @@
 ):
     width = w_ref.shape[2]
     get_tok = fetch(tok_hbm, tok_ref, sems.at[0])
-    get_w = [fetch(columns(w_hbm, meta_ref[i], width), w_ref.at[i], sems.at[1 + i]) for i in range(3)]
+    k, x = meta_ref[0], meta_ref[1]
+    blocks = ((1 - x) * 2 + k, x * 2 + 1 - k, x * 2 + k)
+    get_w = [fetch(columns(w_hbm, b, width), w_ref.at[i], sems.at[1 + i]) for i, b in enumerate(blocks)]
     get_bcw = fetch(bcw_hbm, bcw_ref, sems.at[4])
     get_ra = fetch(ra_hbm, ra_ref, sems.at[5])
     get_rb = fetch(rb_hbm, rb_ref, sems.at[6])
@@ -1062,12 +1064,13 @@
     out_ref[...] = total
 
 
-def first_half(blocks, before, mine, other, rim, x_weight, tile):
+def first_half(meta, far, before, mine, other, rim, x_weight, tile):
     rows, width = mine.shape
     depth = x_weight.shape[0]
     whole = lambda shape: pl.BlockSpec(shape, lambda i, m: (0, 0))
     part = pl.BlockSpec((rows, tile), lambda i, m: (0, i))
     parts = [] if before is None else [before]
+    side = lambda m: 1 - m[1] if far else m[1]
     return pl.pallas_call(
         half_kernel,
         grid_spec=pltpu.PrefetchScalarGridSpec(
@@ -1076,8 +1079,8 @@
             in_specs=[part] * len(parts)
             + [
                 whole(mine.shape), whole(other.shape), whole(rim.shape),
-                pl.BlockSpec((tile, width), lambda i, m: (i, m[0])),
-                pl.BlockSpec((tile, width), lambda i, m: (i, m[1])),
+                pl.BlockSpec((tile, width), lambda i, m: (i, side(m) * 2 + m[0])),
+                pl.BlockSpec((tile, width), lambda i, m: (i, side(m) * 2 + 1 - m[0])),
             ],
             out_specs=part,
         ),
@@ -1085,7 +1088,7 @@
         compiler_params=params(16),
         cost_estimate=cost(2e9, 4e6),
         name="half_sum",
-    )(blocks, *parts, mine, other, rim, x_weight, x_weight)
+    )(meta, *parts, mine, other, rim, x_weight, x_weight)
 
 
 def last_kernel(
@@ -1107,7 +1110,7 @@
             bc_ref[at : at + value.shape[0], states2:] = low
         shape = (LANES, all_heads)
         row, col = iota(shape, 0), iota(shape, 1)
-        x = side_ref[0]
+        x = side_ref[1]
         here = jnp.where((row < heads) & (col == row + x * heads), 1.0, 0.0).astype(BF)
         there = jnp.where((row < heads) & (col == row + (1 - x) * heads), 1.0, 0.0).astype(BF)
         dt = mm(bc_own_ref[:, states2:].astype(BF), here) + mm(bc_recv_ref[:, states2:], there)
@@ -1167,21 +1170,18 @@
     groups = [[2 * i for i in range(chips)], [2 * i + 1 for i in range(chips)]]
     exchange = lambda a: lax.all_to_all(a, "ctx", 0, 0, axis_index_groups=groups)
 
-    def column_block(side, half):
-        return (side * 2 + half)[None]
-
     tail = tokens[rows - 16 :]
     ra = lax.ppermute(tail, "ctx", [(2 * i - 1, 2 * i) for i in range(1, chips)])
     rb = lax.ppermute(tail, "ctx", [(2 * i - 1, 2 * i + 1) for i in range(1, chips)])
 
     dt_rows = dt_weight.T
     to_cross, small, low = lead_proj(
-        column_block(1 - x, 1 - k), tokens, x_weight, bc_weight, dt_rows, width
+        meta, tokens, x_weight, bc_weight, dt_rows, width
     )
     from_cross = by_both(to_cross)
     small_x = by_x(small)
     to_x, to_core, mine, rim_own, rim_send = rest_proj(
-        jnp.stack([(1 - x) * 2 + k, x * 2 + 1 - k, x * 2 + k]), tokens, x_weight, bc_weight, ra, rb, width
+        meta, tokens, x_weight, bc_weight, ra, rb, width
     )
     from_x = by_x(to_x)
     from_core = by_core(to_core)
@@ -1241,12 +1241,12 @@
     bc_chip, bc_send = join(meta, bc_mine, by_core(bc_other), heads)
     bc_recv = by_x(bc_send)
     part = first_half(
-        jnp.stack([x * 2 + k, x * 2 + 1 - k]), None, g_mine, g_core, rim0, x_weight, 640
+        meta, False, None, g_mine, g_core, rim0, x_weight, 640
     )
     part = first_half(
-        jnp.stack([(1 - x) * 2 + k, (1 - x) * 2 + 1 - k]), part, g_x, g_cross, rim1, x_weight, 640
-    )
-    grad_tokens = last_half(x[None], part, rim1, rim0, bc_chip, bc_recv, bc_weight, dt_rows, width)
+        meta, True, part, g_x, g_cross, rim1, x_weight, 640
+    )
+    grad_tokens = last_half(meta, part, rim1, rim0, bc_chip, bc_recv, bc_weight, dt_rows, width)
     return (mixed, grad_tokens)
 
 

time: 139 us -> 136 us (0.978)
  waiting for transfers between devices: 26.3 us -> 20.8 us
  starting transfers between devices: 33.8 us -> 35.6 us
  Pallas kernels: 63.7 us -> 65.1 us
    ppermute x6, waiting for transfers between devices: 19.8 us -> 14.3 us  [by_chips(): by_x = lambda a: lax.ppermute(a, 'fsdp', pair)]
    ppermute x6, starting transfers between devices: 6.27 us -> 7.74 us  [by_chips(): by_x = lambda a: lax.ppermute(a, 'fsdp', pair)]
  transfers between devices with their start and end apart: 26 -> 26, of which waited for: 11 -> 10; matrix products, arithmetic and copies ran while one was open for 3% -> 3% of each run, Pallas kernels for 28% -> 26%
where the time goes in v4:
time: 136 us; the launch traced here: 135 us
  Pallas kernels  65.1 us (48%)
  starting transfers between devices  35.6 us (26%)
  waiting for transfers between devices  20.8 us (15%)
  local copies, waits for them, and re-layouts  10.1 us (7%)
  other arithmetic  2.26 us (2%)
    all_to_all x4, starting transfers between devices, by_chips(): lax.all_to_all(a, 'ctx', 0, 0, axis_index_groups=groups)  19.8 us
    ppermute x6, waiting for transfers between devices, by_chips(): by_x = lambda a: lax.ppermute(a, 'fsdp', pair)  14.3 us
    unnamed x57, local copies, waits for them, and re-layouts  8.57 us
    pallas_call x1, Pallas kernels, grads_of(): pl.pallas_call(functools.partial(grads_kernel, doc_starts.shape[0], heads...  7.96 us
    ppermute x6, starting transfers between devices, by_chips(): by_x = lambda a: lax.ppermute(a, 'fsdp', pair)  7.74 us
    pallas_call x1, Pallas kernels, outputs_of(): pl.pallas_call(functools.partial(out_kernel, heads), grid_spec=pltpu.Pref...  7.12 us
    pallas_call x1, Pallas kernels, within(): pl.pallas_call(functools.partial(within_kernel, doc_starts.shape[0], head...  6.83 us
    pallas_call x1, Pallas kernels, within_back(): pl.pallas_call(functools.partial(within_back_kernel, doc_starts.shape[0],...  6.8 us
  transfers between devices with their start and end apart: 26, of which 10 were waited for; matrix products, arithmetic and copies ran while one was open for 3% of the time, Pallas kernels for 26%

profile of v4, /device:TPU:0, one launch (start us, length us, event | category | flops | bytes accessed | tf_op | source)
XLA Modules:
  0.0 134.8 jit_solution(14203711136042120937)
XLA Ops:
  1.3 4.5 %lead_proj.1 = (bf16[256,640]{1,0:T(8,128)(2,1)}, bf16[256,384]{1,0:T(8,128)(2,1)}, bf16[256,256]{1,0:T(8,128)(2,1)}) custom-call(s32[3]{0:T(128)} %pad_add_fusion.meta_ref.side_ref, bf16[256,1280]{1,0:T(8,128)(2,1)} %tok_hbm.3, bf16[1280,2560]{1,0:T(8,128)(2,1)} %refs_5_.1, bf16[1280,256]{1,0:T(8,128)(2,1)} %bcw_ref.1, bf16[40,1280]{1,0:T(8,128)(2,1)} %bitcast.10), custom_call_target="tpu_custom_call" | custom-call | flops 419430400 | bytes 3000000 | tf_op jit(solution)/shard_map/lead_proj/pallas_call | solution.py:284
  5.9 3.0 %collective-permute-start.6 = (bf16[256,384]{1,0:T(8,128)(2,1)}, bf16[256,384]{1,0:T(8,128)(2,1)S(1)}, u32[]{:S(2)}, u32[]{:S(2)}) collective-permute-start(bf16[256,384]{1,0:T(8,128)(2,1)} %get-tuple-element.57.own_ref), channel_id=1, source_target_pairs={{0,1},{1,0},{2,3},{3,2},{4,5},{5,4},{6,7},{7,6},{8,9},{9,8},{10,11... | collective-permute-start | bytes 589832 | tf_op jit(solution)/shard_map/ppermute | solution.py:1168
  8.9 0.8 slice.3
  11.0 2.9 %collective-permute-start.7 = (bf16[256,384]{1,0:T(8,128)(2,1)}, bf16[256,384]{1,0:T(8,128)(2,1)S(1)}, u32[]{:S(2)}, u32[]{:S(2)}) collective-permute-start(bf16[256,384]{1,0:T(8,128)(2,1)} %get-tuple-element.57.own_ref), channel_id=1, source_target_pairs={{0,2},{2,0},{4,6},{6,4},{8,10},{10,8},{12,14},{14,12},{16,18},{18,... | collective-permute-start | bytes 589832 | tf_op jit(solution)/shard_map/ppermute | solution.py:1167
  15.9 5.8 %rest_proj.1 = (bf16[256,640]{1,0:T(8,128)(2,1)}, bf16[256,640]{1,0:T(8,128)(2,1)}, bf16[256,640]{1,0:T(8,128)(2,1)}, bf16[16,896]{1,0:T(8,128)(2,1)}, bf16[16,896]{1,0:T(8,128)(2,1)}) custom-call(s32[3]{0:T(128)} %pad_add_fusion.meta_ref.side_ref, bf16[256,1280]{1,0:T(8,128)(2,1)} %tok_hbm.3, bf16[1280,2560]{1,0:T(8,128)(2,1)} %refs_5_.1, ...), custom_call_target="tpu_custom_call" | custom-call | flops 1258291200 | bytes 6000000 | tf_op jit(solution)/shard_map/rest_proj/pallas_call | solution.py:344
  21.7 1.6 %collective-permute-start.5 = (bf16[16,896]{1,0:T(8,128)(2,1)}, bf16[16,896]{1,0:T(8,128)(2,1)S(1)}, u32[]{:S(2)}, u32[]{:S(2)}) collective-permute-start(bf16[16,896]{1,0:T(8,128)(2,1)} %get-tuple-element.56), channel_id=1, source_target_pairs={{0,1},{1,0},{2,3},{3,2},{4,5},{5,4},{6,7},{7,6},{8,9},{9,8},{10,11... | collective-permute-start | bytes 86024 | tf_op jit(solution)/shard_map/ppermute | solution.py:1168
  24.4 1.5 %collective-permute-done.5.rim_recv_ref = bf16[16,896]{1,0:T(8,128)(2,1)S(1)} collective-permute-done((bf16[16,896]{1,0:T(8,128)(2,1)}, bf16[16,896]{1,0:T(8,128)(2,1)S(1)}, u32[]{:S(2)}, u32[]{:S(2)}) %collective-permute-start.5) | collective-permute-done | bytes 28704 | tf_op jit(solution)/shard_map/ppermute | solution.py:1168
  26.7 4.9 %shared_maps.1 = (bf16[512,256]{1,0:T(8,128)(2,1)}, f32[512,256]{1,0:T(8,128)}, f32[512,128]{1,0:T(8,128)}, f32[512,128]{1,0:T(8,128)}, f32[512,128]{1,0:T(8,128...) custom-call(s32[3]{0:T(128)} %pad_add_fusion.meta_ref.side_ref, ...), custom_call_target="tpu_custom_call" | custom-call | flops 4000000000 | bytes 4000000 | tf_op jit(solution)/shard_map/shared_maps/pallas_call | solution.py:450
  31.6 1.9 %collective-permute-done.2.xr_ref = bf16[256,640]{1,0:T(8,128)(2,1)S(1)} collective-permute-done((bf16[256,640]{1,0:T(8,128)(2,1)}, bf16[256,640]{1,0:T(8,128)(2,1)S(1)}, u32[]{:S(2)}, u32[]{:S(2)}) %collective-permute-start.2) | collective-permute-done | bytes 327712 | tf_op jit(solution)/shard_map/ppermute | solution.py:1168
  34.3 6.3 %inner_maps.1 = (f32[512,640]{1,0:T(8,128)}, bf16[512,640]{1,0:T(8,128)(2,1)}, f32[2,128,640]{2,1,0:T(8,128)}, bf16[8,16,768]{2,1,0:T(8,128)(2,1)}) custom-call(s32[3]{0:T(128)} %pad_add_fusion.meta_ref.side_ref, s32[4]{0:T(128)} %docs_ref.9, bf16[256,640]{1,0:T(8,128)(2,1)} %get-tuple-element.51.own_ref, bf16[256,640]{1,0:T(8,128)(2,1)} %copy-done.18, ...), custom_call_target="tpu_custom_call" | custom-call | flops 4000000000 | bytes 4000000 | tf_op jit(solution)/shard_map/inner_maps/pallas_call | solution.py:563
  40.6 6.0 %all-to-all-start = ((bf16[8,16,768]{2,1,0:T(8,128)(2,1)}), bf16[8,16,768]{2,1,0:T(8,128)(2,1)S(1)}, u32[]{:S(2)}, u32[]{:S(2)}) async-start(bf16[8,16,768]{2,1,0:T(8,128)(2,1)} %get-tuple-element.67), calls=%async_computation | async-start | bytes 393216 | tf_op jit(solution)/shard_map/all_to_all | solution.py:1171
  47.1 4.5 %collective-permute-done.9.xr_low_ref = bf16[256,256]{1,0:T(8,128)(2,1)S(1)} collective-permute-done((bf16[256,256]{1,0:T(8,128)(2,1)S(1)}, bf16[256,256]{1,0:T(8,128)(2,1)S(1)}, u32[]{:S(2)}, u32[]{:S(2)}) %collective-permute-start.9) | collective-permute-done | bytes 131104 | tf_op jit(solution)/shard_map/ppermute | solution.py:1168
  52.8 1.5 %all-to-all-done.recv_ref.keep_ref = bf16[8,16,768]{2,1,0:T(8,128)(2,1)S(1)} async-done(((bf16[8,16,768]{2,1,0:T(8,128)(2,1)}), bf16[8,16,768]{2,1,0:T(8,128)(2,1)S(1)}, u32[]{:S(2)}, u32[]{:S(2)}) %all-to-all-start) | async-done | bytes 196640 | tf_op jit(solution)/shard_map/all_to_all | solution.py:1171
  54.4 1.1 chain.2
  55.4 4.4 %all-to-all-start.1 = ((bf16[8,16,640]{2,1,0:T(8,128)(2,1)}), bf16[8,16,640]{2,1,0:T(8,128)(2,1)S(1)}, u32[]{:S(2)}, u32[]{:S(2)}) async-start(bf16[8,16,640]{2,1,0:T(8,128)(2,1)} %chain.2), calls=%async_computation.1 | async-start | bytes 327680 | tf_op jit(solution)/shard_map/all_to_all | solution.py:1171
  60.5 6.8 %within.1 = (f32[512,640]{1,0:T(8,128)}, f32[2,256,256]{2,1,0:T(8,128)}) custom-call(s32[3]{0:T(128)} %pad_add_fusion.meta_ref.side_ref, s32[4]{0:T(128)} %docs_ref.9, bf16[512,640]{1,0:T(8,128)(2,1)} %get-tuple-element.62.xd_ref, f32[512,128]{1,0:T(8,128)} %get-tuple-element.63.ramp_ref, f32[2,16,256]{2,1,0:T(8,128)} %get-tuple-element.64.rampt_ref, ...), custom_call_target="tpu_custom_call" | custom-call | flops 6000000000 | bytes 4000000 | tf_op jit(solution)/shard_map/within/pallas_call | solution.py:648
  68.2 7.1 %outputs_of.1 = (bf16[256,640]{1,0:T(8,128)(2,1)}, bf16[256,640]{1,0:T(8,128)(2,1)}, bf16[512,1280]{1,0:T(8,128)(2,1)}, bf16[512,640]{1,0:T(8,128)(2,1)}, f32[51...) custom-call(s32[3]{0:T(128)} %pad_add_fusion.meta_ref.side_ref, ...), custom_call_target="tpu_custom_call" | custom-call | flops 4000000000 | bytes 4000000 | tf_op jit(solution)/shard_map/outputs_of/pallas_call | solution.py:772
  75.3 6.0 %all-to-all-start.2 = ((bf16[8,16,640]{2,1,0:T(8,128)(2,1)}), bf16[8,16,640]{2,1,0:T(8,128)(2,1)S(1)}, u32[]{:S(2)}, u32[]{:S(2)}) async-start(bf16[8,16,640]{2,1,0:T(8,128)(2,1)} %get-tuple-element.72), calls=%async_computation.2 | async-start | bytes 327680 | tf_op jit(solution)/shard_map/all_to_all | solution.py:1171
  81.3 4.1 %slopes_of.1 = (bf16[512,640]{1,0:T(8,128)(2,1)}, bf16[512,640]{1,0:T(8,128)(2,1)}, bf16[512,640]{1,0:T(8,128)(2,1)}, bf16[512,640]{1,0:T(8,128)(2,1)}, bf16[512,640]{1,0:T(8,128)(2,1)}) custom-call(f32[512,640]{1,0:T(8,128)} %get-tuple-element.78.pre_ref, bf16[512,128]{1,0:T(8,128)(2,1)} %get-tuple-element.59.dpk_ref, ...), custom_call_target="tpu_custom_call" | custom-call | flops 2000000000 | bytes 4000000 | tf_op jit(solution)/shard_map/slopes_of/pallas_call | solution.py:878
  85.4 3.4 %all-to-all-done.2.recv_ref = bf16[8,16,640]{2,1,0:T(8,128)(2,1)S(1)} async-done(((bf16[8,16,640]{2,1,0:T(8,128)(2,1)}), bf16[8,16,640]{2,1,0:T(8,128)(2,1)S(1)}, u32[]{:S(2)}, u32[]{:S(2)}) %all-to-all-start.2) | async-done | bytes 163872 | tf_op jit(solution)/shard_map/all_to_all | solution.py:1171
  88.9 1.1 chain.3
  89.9 3.4 %all-to-all-start.3 = ((bf16[8,16,640]{2,1,0:T(8,128)(2,1)}), bf16[8,16,640]{2,1,0:T(8,128)(2,1)S(1)}, u32[]{:S(2)}, u32[]{:S(2)}) async-start(bf16[8,16,640]{2,1,0:T(8,128)(2,1)} %chain.3), calls=%async_computation.3 | async-start | bytes 327680 | tf_op jit(solution)/shard_map/all_to_all | solution.py:1171
  93.3 6.8 %within_back.1 = (bf16[512,640]{1,0:T(8,128)(2,1)}, f32[512,128]{1,0:T(8,128)}, f32[512,256]{1,0:T(8,128)}) custom-call(s32[3]{0:T(128)} %pad_add_fusion.meta_ref.side_ref, s32[4]{0:T(128)} %docs_ref.9, bf16[512,1280]{1,0:T(8,128)(2,1)} %get-tuple-element.75.dy_ref, bf16[512,640]{1,0:T(8,128)(2,1)} %get-tuple-element.76.edy_ref, ...), custom_call_target="tpu_custom_call" | custom-call | flops 10000000000 | bytes 6000000 | tf_op jit(solution)/shard_map/within_back/pallas_call | solution.py:838
  101.5 8.0 %grads_of.1 = (bf16[256,640]{1,0:T(8,128)(2,1)}, bf16[256,640]{1,0:T(8,128)(2,1)}, f32[256,384]{1,0:T(8,128)}, f32[256,384]{1,0:T(8,128)}, bf16[16,896]{1,0:T(8,128)(2,1)}) custom-call(s32[3]{0:T(128)} %pad_add_fusion.meta_ref.side_ref, s32[4]{0:T(128)} %docs_ref.9, bf16[128,640]{1,0:T(8,128)(2,1)} %bitcast.13, f32[128,640]{1,0:T(8,128)} %get-tuple-element.73.late_ref, ...), custom_call_target="tpu_custom_call" | custom-call | flops 4000000000 | bytes 8000000 | tf_op jit(solution)/shard_map/grads_of/pallas_call | solution.py:997
  110.2 1.5 %collective-permute-start.17 = (bf16[256,640]{1,0:T(8,128)(2,1)}, bf16[256,640]{1,0:T(8,128)(2,1)S(1)}, u32[]{:S(2)}, u32[]{:S(2)}) collective-permute-start(bf16[256,640]{1,0:T(8,128)(2,1)} %get-tuple-element.91.refs_0_), channel_id=1, source_target_pairs={{0,1},{1,0},{2,3},{3,2},{4,5},{5,4},{6,7},{7,6},{8,9},{9,8},{10,11... | collective-permute-start | bytes 983048 | tf_op jit(solution)/shard_map/ppermute | solution.py:1168
  114.4 1.0 maximum_select_fusion
  117.4 2.9 %copy-done = bf16[1280,2560]{1,0:T(8,128)(2,1)S(1)} copy-done((bf16[1280,2560]{1,0:T(8,128)(2,1)S(1)}, bf16[1280,2560]{1,0:T(8,128)(2,1)}, u32[]{:S(2)}) %copy-start) | copy-done | bytes 6553624
  120.3 2.6 %half_sum.2.refs_0_ = f32[256,1280]{1,0:T(8,128)S(1)} custom-call(s32[3]{0:T(128)S(1)} %copy-done.5, bf16[256,640]{1,0:T(8,128)(2,1)S(1)} %copy-done.4, bf16[256,640]{1,0:T(8,128)(2,1)S(1)} %collective-permute-done.14.refs_1_, bf16[32,896]{1,0:T(8,128)(2,1)S(1)} %collective-permute-done.16.refs_2_.rim0_ref, bf16[1280,2560]{1,0:T(8,128)(2,1)S(1)} %copy-done, ...), custom_call_target="tpu_custom_call" | custom-call | flops 2000000000 | bytes 4000000 | tf_op jit(solution)/shard_map/half_sum/pallas_call | solution.py:1074
  122.9 5.3 %collective-permute-done.17.refs_1_ = bf16[256,640]{1,0:T(8,128)(2,1)S(1)} collective-permute-done((bf16[256,640]{1,0:T(8,128)(2,1)}, bf16[256,640]{1,0:T(8,128)(2,1)S(1)}, u32[]{:S(2)}, u32[]{:S(2)}) %collective-permute-start.17) | collective-permute-done | bytes 327712 | tf_op jit(solution)/shard_map/ppermute | solution.py:1168
  128.2 2.7 %half_sum.3.part_ref = f32[256,1280]{1,0:T(8,128)S(1)} custom-call(s32[3]{0:T(128)S(1)} %copy-done.5, f32[256,1280]{1,0:T(8,128)S(1)} %half_sum.2.refs_0_, bf16[256,640]{1,0:T(8,128)(2,1)S(1)} %collective-permute-done.17.refs_1_, bf16[256,640]{1,0:T(8,128)(2,1)S(1)} %collective-permute-done.18.refs_2_, ...), custom_call_target="tpu_custom_call" | custom-call | flops 2000000000 | bytes 4000000 | tf_op jit(solution)/shard_map/half_sum/pallas_call | solution.py:1074
  130.9 1.2 collective-permute-done.21.bc_recv_ref
  132.1 2.6 %last_half.1 = bf16[256,1280]{1,0:T(8,128)(2,1)} custom-call(s32[3]{0:T(128)S(1)} %copy-done.5, f32[256,1280]{1,0:T(8,128)S(1)} %half_sum.3.part_ref, bf16[32,896]{1,0:T(8,128)(2,1)S(1)} %collective-permute-done.19.refs_3_.rim_ref, bf16[32,896]{1,0:T(8,128)(2,1)S(1)} %collective-permute-done.16.refs_2_.rim0_ref, ...), custom_call_target="tpu_custom_call" | custom-call | flops 500000000 | bytes 2000000 | tf_op jit(solution)/shard_map/last_half/pallas_call | solution.py:1128
  (100 shorter events, 16.7 us)
Async XLA Ops:
  1.3 12.8 %copy-start.13 = (f32[20]{0:T(128)S(1)}, f32[20]{0:T(128)}, u32[]{:S(2)}) copy-start(f32[20]{0:T(128)} %param.18) | copy-start | bytes 244
  1.3 12.8 %copy-start.14 = (f32[20]{0:T(128)S(1)}, f32[20]{0:T(128)}, u32[]{:S(2)}) copy-start(f32[20]{0:T(128)} %param.17) | copy-start | bytes 244
  5.9 8.4 %collective-permute-start.6 = (bf16[256,384]{1,0:T(8,128)(2,1)}, bf16[256,384]{1,0:T(8,128)(2,1)S(1)}, u32[]{:S(2)}, u32[]{:S(2)}) collective-permute-start(bf16[256,384]{1,0:T(8,128)(2,1)} %get-tuple-element.57.own_ref), channel_id=1, source_target_pairs={{0,1},{1,0},{2,3},{3,2},{4,5},{5,4},{6,7},{7,6},{8,9},{9,8},{10,11... | collective-permute-start | bytes 589832 | tf_op jit(solution)/shard_map/ppermute | solution.py:1168
  9.6 5.0 %collective-permute-start.1 = (bf16[16,1280]{1,0:T(8,128)(2,1)S(1)}, bf16[16,1280]{1,0:T(8,128)(2,1)S(1)}, u32[]{:S(2)}, u32[]{:S(2)}) collective-permute-start(bf16[16,1280]{1,0:T(8,128)(2,1)S(1)} %slice.3), channel_id=1, source_target_pairs={{2,6},{6,10},{10,14},{14,18},{18,22},{22,26},{26,30},{3,7},{7,11},... | collective-permute-start | bytes 122888 | tf_op jit(solution)/shard_map/ppermute | solution.py:1175
  10.3 4.4 %collective-permute-start = (bf16[16,1280]{1,0:T(8,128)(2,1)S(1)}, bf16[16,1280]{1,0:T(8,128)(2,1)S(1)}, u32[]{:S(2)}, u32[]{:S(2)}) collective-permute-start(bf16[16,1280]{1,0:T(8,128)(2,1)S(1)} %slice.3), channel_id=1, source_target_pairs={{2,4},{6,8},{10,12},{14,16},{18,20},{22,24},{26,28},{3,5},{7,9},{1... | collective-permute-start | bytes 122888 | tf_op jit(solution)/shard_map/ppermute | solution.py:1174
  11.0 14.9 %collective-permute-start.7 = (bf16[256,384]{1,0:T(8,128)(2,1)}, bf16[256,384]{1,0:T(8,128)(2,1)S(1)}, u32[]{:S(2)}, u32[]{:S(2)}) collective-permute-start(bf16[256,384]{1,0:T(8,128)(2,1)} %get-tuple-element.57.own_ref), channel_id=1, source_target_pairs={{0,2},{2,0},{4,6},{6,4},{8,10},{10,8},{12,14},{14,12},{16,18},{18,... | collective-permute-start | bytes 589832 | tf_op jit(solution)/shard_map/ppermute | solution.py:1167
  13.9 17.7 %collective-permute-start.4 = (bf16[256,640]{1,0:T(8,128)(2,1)}, bf16[256,640]{1,0:T(8,128)(2,1)S(1)}, u32[]{:S(2)}, u32[]{:S(2)}) collective-permute-start(bf16[256,640]{1,0:T(8,128)(2,1)} %get-tuple-element.54), channel_id=1, source_target_pairs={{0,3},{1,2},{2,1},{3,0},{4,7},{5,6},{6,5},{7,4},{8,11},{9,10},{10,... | collective-permute-start | bytes 983048 | tf_op jit(solution)/shard_map/ppermute | solution.py:1169
  14.2 11.7 %collective-permute-start.8 = (bf16[256,384]{1,0:T(8,128)(2,1)S(1)}, bf16[256,384]{1,0:T(8,128)(2,1)S(1)}, u32[]{:S(2)}, u32[]{:S(2)}) collective-permute-start(bf16[256,384]{1,0:T(8,128)(2,1)S(1)} %collective-permute-done.6.xr_ref), channel_id=1, source_target_pairs={{0,2},{2,0},{4,6},{6,4},{8,10},{10,8},{12,14},{14,12},{16,18},{18,... | collective-permute-start | bytes 589832 | tf_op jit(solution)/shard_map/ppermute | solution.py:1167
  21.7 4.1 %collective-permute-start.5 = (bf16[16,896]{1,0:T(8,128)(2,1)}, bf16[16,896]{1,0:T(8,128)(2,1)S(1)}, u32[]{:S(2)}, u32[]{:S(2)}) collective-permute-start(bf16[16,896]{1,0:T(8,128)(2,1)} %get-tuple-element.56), channel_id=1, source_target_pairs={{0,1},{1,0},{2,3},{3,2},{4,5},{5,4},{6,7},{7,6},{8,9},{9,8},{10,11... | collective-permute-start | bytes 86024 | tf_op jit(solution)/shard_map/ppermute | solution.py:1168
  23.9 9.6 %collective-permute-start.2 = (bf16[256,640]{1,0:T(8,128)(2,1)}, bf16[256,640]{1,0:T(8,128)(2,1)S(1)}, u32[]{:S(2)}, u32[]{:S(2)}) collective-permute-start(bf16[256,640]{1,0:T(8,128)(2,1)} %get-tuple-element.52), channel_id=1, source_target_pairs={{0,1},{1,0},{2,3},{3,2},{4,5},{5,4},{6,7},{7,6},{8,9},{9,8},{10,11... | collective-permute-start | bytes 983048 | tf_op jit(solution)/shard_map/ppermute | solution.py:1168
  25.9 7.6 %collective-permute-start.3 = (bf16[256,640]{1,0:T(8,128)(2,1)}, bf16[256,640]{1,0:T(8,128)(2,1)S(1)}, u32[]{:S(2)}, u32[]{:S(2)}) collective-permute-start(bf16[256,640]{1,0:T(8,128)(2,1)} %get-tuple-element.53), channel_id=1, source_target_pairs={{0,2},{2,0},{4,6},{6,4},{8,10},{10,8},{12,14},{14,12},{16,18},{18,... | collective-permute-start | bytes 983048 | tf_op jit(solution)/shard_map/ppermute | solution.py:1167
  34.3 12.2 %copy-start.23 = (bf16[256,256]{1,0:T(8,128)(2,1)S(1)}, bf16[256,256]{1,0:T(8,128)(2,1)}, u32[]{:S(2)}) copy-start(bf16[256,256]{1,0:T(8,128)(2,1)} %get-tuple-element.65.own_low_ref) | copy-start | bytes 393220
  34.3 17.3 %copy-start.9 = (bf16[256,1280]{1,0:T(8,128)(2,1)S(1)}, bf16[256,1280]{1,0:T(8,128)(2,1)}, u32[]{:S(2)}) copy-start(bf16[256,1280]{1,0:T(8,128)(2,1)} %go_ref.1) | copy-start | bytes 1966084
  34.3 17.9 %copy-start.12 = (f32[1280]{0:T(1024)S(1)}, f32[1280]{0:T(1024)}, u32[]{:S(2)}) copy-start(f32[1280]{0:T(1024)} %param.19) | copy-start | bytes 15364
  40.6 13.8 %all-to-all-start = ((bf16[8,16,768]{2,1,0:T(8,128)(2,1)}), bf16[8,16,768]{2,1,0:T(8,128)(2,1)S(1)}, u32[]{:S(2)}, u32[]{:S(2)}) async-start(bf16[8,16,768]{2,1,0:T(8,128)(2,1)} %get-tuple-element.67), calls=%async_computation | async-start | bytes 393216 | tf_op jit(solution)/shard_map/all_to_all | solution.py:1171
  46.6 5.0 %collective-permute-start.9 = (bf16[256,256]{1,0:T(8,128)(2,1)S(1)}, bf16[256,256]{1,0:T(8,128)(2,1)S(1)}, u32[]{:S(2)}, u32[]{:S(2)}) collective-permute-start(bf16[256,256]{1,0:T(8,128)(2,1)S(1)} %copy-done.23), channel_id=1, source_target_pairs={{0,1},{1,0},{2,3},{3,2},{4,5},{5,4},{6,7},{7,6},{8,9},{9,8},{10,11... | collective-permute-start | bytes 393224 | tf_op jit(solution)/shard_map/ppermute | solution.py:1168
  47.1 12.7 %collective-permute-start.10 = (bf16[256,256]{1,0:T(8,128)(2,1)S(1)}, bf16[256,256]{1,0:T(8,128)(2,1)S(1)}, u32[]{:S(2)}, u32[]{:S(2)}) collective-permute-start(bf16[256,256]{1,0:T(8,128)(2,1)S(1)} %copy-done.23), channel_id=1, source_target_pairs={{0,2},{2,0},{4,6},{6,4},{8,10},{10,8},{12,14},{14,12},{16,18},{18,... | collective-permute-start | bytes 393224 | tf_op jit(solution)/shard_map/ppermute | solution.py:1167
  51.6 8.2 %collective-permute-start.11 = (bf16[256,256]{1,0:T(8,128)(2,1)S(1)}, bf16[256,256]{1,0:T(8,128)(2,1)S(1)}, u32[]{:S(2)}, u32[]{:S(2)}) collective-permute-start(bf16[256,256]{1,0:T(8,128)(2,1)S(1)} %collective-permute-done.9.xr_low_ref), channel_id=1, source_target_pairs={{0,2},{2,0},{4,6},{6,4},{8,10},{10,8},{12,14},{14,12},{16,18},{18,... | collective-permute-start | bytes 393224 | tf_op jit(solution)/shard_map/ppermute | solution.py:1167
  51.7 15.7 %collective-permute-start.12 = (bf16[256,640]{1,0:T(8,128)(2,1)S(1)}, bf16[256,640]{1,0:T(8,128)(2,1)S(1)}, u32[]{:S(2)}, u32[]{:S(2)}) collective-permute-start(bf16[256,640]{1,0:T(8,128)(2,1)S(1)} %constant_dynamic-slice_fusion), channel_id=1, source_target_pairs={{0,2},{2,0},{4,6},{6,4},{8,10},{10,8},{12,14},{14,12},{16,18},{18,... | collective-permute-start | bytes 983048 | tf_op jit(solution)/shard_map/ppermute | solution.py:1167
  55.4 12.0 %all-to-all-start.1 = ((bf16[8,16,640]{2,1,0:T(8,128)(2,1)}), bf16[8,16,640]{2,1,0:T(8,128)(2,1)S(1)}, u32[]{:S(2)}, u32[]{:S(2)}) async-start(bf16[8,16,640]{2,1,0:T(8,128)(2,1)} %chain.2), calls=%async_computation.1 | async-start | bytes 327680 | tf_op jit(solution)/shard_map/all_to_all | solution.py:1171
  75.3 13.6 %all-to-all-start.2 = ((bf16[8,16,640]{2,1,0:T(8,128)(2,1)}), bf16[8,16,640]{2,1,0:T(8,128)(2,1)S(1)}, u32[]{:S(2)}, u32[]{:S(2)}) async-start(bf16[8,16,640]{2,1,0:T(8,128)(2,1)} %get-tuple-element.72), calls=%async_computation.2 | async-start | bytes 327680 | tf_op jit(solution)/shard_map/all_to_all | solution.py:1171
  89.9 10.9 %all-to-all-start.3 = ((bf16[8,16,640]{2,1,0:T(8,128)(2,1)}), bf16[8,16,640]{2,1,0:T(8,128)(2,1)S(1)}, u32[]{:S(2)}, u32[]{:S(2)}) async-start(bf16[8,16,640]{2,1,0:T(8,128)(2,1)} %chain.3), calls=%async_computation.3 | async-start | bytes 327680 | tf_op jit(solution)/shard_map/all_to_all | solution.py:1171
  101.5 12.9 %copy-start.6 = (bf16[256,640]{1,0:T(8,128)(2,1)S(1)}, bf16[256,640]{1,0:T(8,128)(2,1)}, u32[]{:S(2)}) copy-start(bf16[256,640]{1,0:T(8,128)(2,1)} %get-tuple-element.70) | copy-start | bytes 983044
  109.5 2.5 %collective-permute-start.14 = (bf16[256,640]{1,0:T(8,128)(2,1)}, bf16[256,640]{1,0:T(8,128)(2,1)S(1)}, u32[]{:S(2)}, u32[]{:S(2)}) collective-permute-start(bf16[256,640]{1,0:T(8,128)(2,1)} %get-tuple-element.93), channel_id=1, source_target_pairs={{0,2},{2,0},{4,6},{6,4},{8,10},{10,8},{12,14},{14,12},{16,18},{18,... | collective-permute-start | bytes 983048 | tf_op jit(solution)/shard_map/ppermute | solution.py:1167
  109.6 4.9 %collective-permute-start.13 = (bf16[256,640]{1,0:T(8,128)(2,1)S(1)}, bf16[256,640]{1,0:T(8,128)(2,1)S(1)}, u32[]{:S(2)}, u32[]{:S(2)}) collective-permute-start(bf16[256,640]{1,0:T(8,128)(2,1)S(1)} %copy-done.15), channel_id=1, source_target_pairs={{0,2},{2,0},{4,6},{6,4},{8,10},{10,8},{12,14},{14,12},{16,18},{18,... | collective-permute-start | bytes 983048 | tf_op jit(solution)/shard_map/ppermute | solution.py:1167
  110.0 18.1 %collective-permute-start.18 = (bf16[256,640]{1,0:T(8,128)(2,1)}, bf16[256,640]{1,0:T(8,128)(2,1)S(1)}, u32[]{:S(2)}, u32[]{:S(2)}) collective-permute-start(bf16[256,640]{1,0:T(8,128)(2,1)} %get-tuple-element.93), channel_id=1, source_target_pairs={{0,3},{1,2},{2,1},{3,0},{4,7},{5,6},{6,5},{7,4},{8,11},{9,10},{10,... | collective-permute-start | bytes 983048 | tf_op jit(solution)/shard_map/ppermute | solution.py:1169
  110.2 17.9 %collective-permute-start.17 = (bf16[256,640]{1,0:T(8,128)(2,1)}, bf16[256,640]{1,0:T(8,128)(2,1)S(1)}, u32[]{:S(2)}, u32[]{:S(2)}) collective-permute-start(bf16[256,640]{1,0:T(8,128)(2,1)} %get-tuple-element.91.refs_0_), channel_id=1, source_target_pairs={{0,1},{1,0},{2,3},{3,2},{4,5},{5,4},{6,7},{7,6},{8,9},{9,8},{10,11... | collective-permute-start | bytes 983048 | tf_op jit(solution)/shard_map/ppermute | solution.py:1168
  111.8 4.3 %collective-permute-start.20 = (f32[256,384]{1,0:T(8,128)}, f32[256,384]{1,0:T(8,128)S(1)}, u32[]{:S(2)}, u32[]{:S(2)}) collective-permute-start(f32[256,384]{1,0:T(8,128)} %get-tuple-element.97), channel_id=1, source_target_pairs={{0,2},{2,0},{4,6},{6,4},{8,10},{10,8},{12,14},{14,12},{16,18},{18,... | collective-permute-start | bytes 1179656 | tf_op jit(solution)/shard_map/ppermute | solution.py:1167
  111.9 1.8 %collective-permute-start.15 = (bf16[16,896]{1,0:T(8,128)(2,1)}, bf16[16,896]{1,0:T(8,128)(2,1)S(1)}, u32[]{:S(2)}, u32[]{:S(2)}) collective-permute-start(bf16[16,896]{1,0:T(8,128)(2,1)} %get-tuple-element.95), channel_id=1, source_target_pairs={{0,2},{2,0},{4,6},{6,4},{8,10},{10,8},{12,14},{14,12},{16,18},{18,... | collective-permute-start | bytes 86024 | tf_op jit(solution)/shard_map/ppermute | solution.py:1167
  113.7 3.7 %collective-permute-start.16 = (bf16[32,896]{1,0:T(8,128)(2,1)S(1)}, bf16[32,896]{1,0:T(8,128)(2,1)S(1)}, u32[]{:S(2)}, u32[]{:S(2)}) collective-permute-start(bf16[32,896]{1,0:T(8,128)(2,1)S(1)} %constant_dynamic-update-slice_fusion), channel_id=1, source_target_pairs={{6,2},{10,6},{14,10},{18,14},{22,18},{26,22},{30,26},{7,3},{11,7},... | collective-permute-start | bytes 172040 | tf_op jit(solution)/shard_map/ppermute | solution.py:1237
  115.4 12.8 %collective-permute-start.19 = (bf16[32,896]{1,0:T(8,128)(2,1)S(1)}, bf16[32,896]{1,0:T(8,128)(2,1)S(1)}, u32[]{:S(2)}, u32[]{:S(2)}) collective-permute-start(bf16[32,896]{1,0:T(8,128)(2,1)S(1)} %constant_dynamic-update-slice_fusion), channel_id=1, source_target_pairs={{6,3},{7,2},{10,7},{11,6},{14,11},{15,10},{18,15},{19,14},{22,19},... | collective-permute-start | bytes 172040 | tf_op jit(solution)/shard_map/ppermute | solution.py:1238
  116.8 15.3 %collective-permute-start.21 = (bf16[256,384]{1,0:T(8,128)(2,1)S(1)}, bf16[256,384]{1,0:T(8,128)(2,1)S(1)}, u32[]{:S(2)}, u32[]{:S(2)}) collective-permute-start(bf16[256,384]{1,0:T(8,128)(2,1)S(1)} %get-tuple-element.99), channel_id=1, source_target_pairs={{0,1},{1,0},{2,3},{3,2},{4,5},{5,4},{6,7},{7,6},{8,9},{9,8},{10,11... | collective-permute-start | bytes 589832 | tf_op jit(solution)/shard_map/ppermute | solution.py:1168
  (22 other events, 76.6 us)
